TPU v7x, 32 devices: a whole 2x2x4 slice. The times are simulated.
32 devices in a mesh: dp: 8 (over y, x, core), tensor: 4 (over z).
Axes of the slice: x: 2, y: 2, z: 4, core: 2. Of those that a mesh axis runs over, the one named last changes fastest.
Arguments:
- activations: bfloat16 [8, 256, 1536], P('dp', 'tensor'), may hold values from -6 to 6
- encoder: bfloat16 [8, 512, 1536], P('dp', 'tensor'), may hold values from -6 to 6
- species: int32 [8], P('dp'), may hold values from 0 to 1
- cotangent: bfloat16 [8, 512, 1536], P('dp', 'tensor'), may hold values from -6 to 6
- norm_gain: bfloat16 [2, 1536], P(None, ('dp', 'tensor')), may hold values from 0.25 to 1.75
- norm_shift: bfloat16 [2, 1536], P(None, ('dp', 'tensor')), may hold values from -1.5 to 1.5
- species_table: bfloat16 [2, 1536], P(None, ('dp', 'tensor')), may hold values from -3 to 3
- query_weight: bfloat16 [1536, 512], P('dp', 'tensor'), may hold values from -0.15625 to 0.15625
- key_weight: bfloat16 [1536, 512], P('dp', 'tensor'), may hold values from -0.15625 to 0.15625
- value_weight: bfloat16 [1536, 1536], P('dp', 'tensor'), may hold values from -0.15625 to 0.15625
- output_weight: bfloat16 [1536, 1536], P('tensor', 'dp'), may hold values from -1.25 to 1.25
- expand_weight: bfloat16 [1536, 3072], P('dp', 'tensor'), may hold values from -0.15625 to 0.15625
- contract_weight: bfloat16 [3072, 1536], P('tensor', 'dp'), may hold values from -0.109375 to 0.109375
- position_weight: bfloat16 [64, 32, 8], P('dp', None, 'tensor'), may hold values from -1 to 1
- content_bias: bfloat16 [64, 8], P('dp', 'tensor'), may hold values from -3 to 3
- position_bias: bfloat16 [64, 8], P('dp', 'tensor'), may hold values from -3 to 3
- upsample_weight: bfloat16 [1536, 1536], P(None, ('dp', 'tensor')), may hold values from -0.15625 to 0.15625
- lateral_weight: bfloat16 [1536, 1536], P(None, ('dp', 'tensor')), may hold values from -0.15625 to 0.15625
- depthwise_weight: bfloat16 [3, 1536], P(None, ('dp', 'tensor')), may hold values from -3.5 to 3.5
- section_bias: bfloat16 [1536], P(('dp', 'tensor')), may hold values from -3 to 3
- pointwise_weight: bfloat16 [1536, 1536], P(('dp', 'tensor')), may hold values from -0.15625 to 0.15625
Outputs:
- section_output: bfloat16 [8, 512, 1536], P('dp', 'tensor')
- activations_grad: float32 [8, 256, 1536], P('dp', 'tensor')
- encoder_grad: float32 [8, 512, 1536], P('dp', 'tensor')
- norm_gain_grad: float32 [2, 1536], P(None, ('dp', 'tensor'))
- norm_shift_grad: float32 [2, 1536], P(None, ('dp', 'tensor'))
- species_table_grad: float32 [2, 1536], P(None, ('dp', 'tensor'))
- query_weight_grad: float32 [1536, 512], P('dp', 'tensor')
- key_weight_grad: float32 [1536, 512], P('dp', 'tensor')
- value_weight_grad: float32 [1536, 1536], P('dp', 'tensor')
- output_weight_grad: float32 [1536, 1536], P('tensor', 'dp')
- expand_weight_grad: float32 [1536, 3072], P('dp', 'tensor')
- contract_weight_grad: float32 [3072, 1536], P('tensor', 'dp')
- position_weight_grad: float32 [64, 32, 8], P('dp', None, 'tensor')
- content_bias_grad: float32 [64, 8], P('dp', 'tensor')
- position_bias_grad: float32 [64, 8], P('dp', 'tensor')
- upsample_weight_grad: float32 [1536, 1536], P(None, ('dp', 'tensor'))
- lateral_weight_grad: float32 [1536, 1536], P(None, ('dp', 'tensor'))
- depthwise_weight_grad: float32 [3, 1536], P(None, ('dp', 'tensor'))
- section_bias_grad: float32 [1536], P(('dp', 'tensor'))
- pointwise_weight_grad: float32 [1536, 1536], P(('dp', 'tensor'))
Inputs may be any that keep to these rules, and one draw needn't show every extreme that they name: Both species occur among the windows.
All inputs are finite; a program needn't handle non-finite values.
Results may differ from a plain program's by a relative error of at most 0.019.
Values may be sent and summed in bfloat16 or wider, within the bound.
No kernel may reach another device: no remote copies, remote signals or barrier semaphores. Data moves between devices by JAX's collectives and lax.ppermute only.
A program may use at most 192 MiB of HBM per device.

v0:
```python
import math

import jax
import jax.numpy as jnp
from jax import lax
from jax.sharding import PartitionSpec as P

KEYD = 64
VALD = 192
BASIS = 32
SPECIES = 2
QBLOCK = 256


def padded_2(cells, sides, width):
    for axis, dim in sides:
        count = lax.axis_size(axis)
        ends = count - 1
        head = lax.slice_in_dim(cells, 0, width, axis=dim)
        tail = lax.slice_in_dim(cells, cells.shape[dim] - width, cells.shape[dim], axis=dim)
        cells = jnp.concatenate(
            [
                lax.ppermute(tail, axis, [(i, (i + 1) % count) for i in range(ends)]),
                cells,
                lax.ppermute(head, axis, [((i + 1) % count, i) for i in range(ends)]),
            ],
            axis=dim,
        )
    return cells


def layer_norm(values, gain_vec, shift_vec):
    centred = values - jnp.mean(values, axis=-1, keepdims=True)
    variance = jnp.mean(centred * centred, axis=-1, keepdims=True)
    return centred * lax.rsqrt(variance + 1e-05) * gain_vec + shift_vec


def basis_table(length, features):
    distance = jnp.arange(2 * length - 1).astype(jnp.float32) - (length - 1)
    halves = features // 2
    fraction = jnp.arange(halves).astype(jnp.float32) / (halves - 1)
    lifetimes = 3.0 * jnp.power(length / 3.0, fraction)
    decays = jnp.exp(-0.6931471805599453 * jnp.abs(distance)[:, None] / lifetimes[None, :])
    return jnp.concatenate([decays, jnp.sign(distance)[:, None] * decays], axis=1)


def skew_band(banded, length):
    head_count, row_count, band_width = banded.shape
    flipped = banded[:, :, ::-1]
    flat = flipped.reshape(head_count, row_count * band_width)
    flat = flat[:, row_count - 1 : row_count - 1 + row_count * (band_width - 1)]
    return flat.reshape(head_count, row_count, band_width - 1)[:, :, :length]


def unskew_band(grid, band_width):
    head_count, row_count, length = grid.shape
    padded = jnp.pad(grid, ((0, 0), (0, 0), (0, band_width - 1 - length)))
    flat = jnp.pad(
        padded.reshape(head_count, row_count * (band_width - 1)), ((0, 0), (row_count - 1, 1))
    )
    return flat.reshape(head_count, row_count, band_width)[:, :, ::-1]


def dot_plain(left_side, right_side):
    return jnp.dot(left_side, right_side, preferred_element_type=jnp.float32)


def dot_transposed(left_side, right_side):
    return lax.dot_general(
        left_side, right_side, (((1,), (1,)), ((), ())), preferred_element_type=jnp.float32
    )


def dot_leading(left_side, right_side):
    return lax.dot_general(
        left_side, right_side, (((0,), (0,)), ((), ())), preferred_element_type=jnp.float32
    )


def exact_gelu(values):
    return jax.nn.gelu(values, approximate=False)


def spread_rows(row_block):
    return lax.all_gather(row_block, "tensor", axis=0, tiled=True)


def collect_rows(partial_rows):
    return lax.psum_scatter(
        partial_rows.astype(jnp.bfloat16), "tensor", scatter_dimension=0, tiled=True
    ).astype(jnp.float32)


def head_scores(content_heads, position_heads, key_heads, rel_heads):
    length = key_heads.shape[0]
    content = jnp.einsum(
        "bhk,jhk->hbj", content_heads, key_heads, preferred_element_type=jnp.float32
    )
    banded = jnp.einsum(
        "bhk,whk->hbw", position_heads, rel_heads, preferred_element_type=jnp.float32
    )
    scores = (content + skew_band(banded, length)) * (1.0 / math.sqrt(KEYD))
    return (scores, content_heads, position_heads, rel_heads)


def section_forward(
    section_rows, encoder_rows, cotangent_rows, w_upsample, w_lateral, bias_section, w_point
):
    coarse_rows = dot_plain(section_rows, w_upsample)
    section_pre = (
        jnp.repeat(coarse_rows, 2, axis=0)
        + dot_plain(encoder_rows, w_lateral)
        + bias_section.astype(jnp.float32)
    )
    grad_deep = dot_transposed(cotangent_rows, w_point).astype(jnp.bfloat16)
    return (section_pre.astype(jnp.bfloat16), grad_deep)


def section_backward(
    section_rows,
    encoder_rows,
    cotangent_rows,
    mix_padded,
    grad_padded,
    w_upsample,
    w_lateral,
    w_depth,
    w_point,
):
    depth_taps = w_depth.astype(jnp.float32)
    mix_wide = mix_padded.astype(jnp.float32)
    grad_wide = grad_padded.astype(jnp.float32)
    deep_rows = (
        depth_taps[0] * mix_wide[:-2]
        + depth_taps[1] * mix_wide[1:-1]
        + depth_taps[2] * mix_wide[2:]
    ).astype(jnp.bfloat16)
    output_part = dot_plain(deep_rows, w_point)
    grad_point = dot_leading(deep_rows, cotangent_rows)
    grad_centre = grad_wide[1:-1]
    grad_taps_cols = jnp.stack(
        [
            jnp.sum(mix_wide[:-2] * grad_centre, axis=0),
            jnp.sum(mix_wide[1:-1] * grad_centre, axis=0),
            jnp.sum(mix_wide[2:] * grad_centre, axis=0),
        ],
        axis=1,
    )
    grad_mix = (
        depth_taps[0] * grad_wide[2:]
        + depth_taps[1] * grad_wide[1:-1]
        + depth_taps[2] * grad_wide[:-2]
    ).astype(jnp.bfloat16)
    grad_bias = jnp.sum(grad_mix.astype(jnp.float32), axis=0)
    encoder_part = dot_transposed(grad_mix, w_lateral)
    grad_lateral_cols = dot_leading(grad_mix, encoder_rows)
    coarse_count = grad_mix.shape[0] // 2
    grad_coarse = jnp.sum(grad_mix.astype(jnp.float32).reshape(coarse_count, 2, -1), axis=1).astype(
        jnp.bfloat16
    )
    grad_upsample_cols = dot_leading(grad_coarse, section_rows)
    section_part = dot_transposed(grad_coarse, w_upsample)
    return (
        output_part,
        encoder_part,
        section_part,
        (grad_upsample_cols, grad_lateral_cols, grad_taps_cols, grad_bias, grad_point),
    )


def body(
    activations,
    encoder,
    species,
    cotangent,
    norm_gain,
    norm_shift,
    species_table,
    query_weight,
    key_weight,
    value_weight,
    output_weight,
    expand_weight,
    contract_weight,
    position_weight,
    content_bias,
    position_bias,
    upsample_weight,
    lateral_weight,
    depthwise_weight,
    section_bias,
    pointwise_weight,
):
    (
        w_query,
        w_key,
        w_value,
        w_output,
        w_expand,
        w_contract,
        w_position,
        bias_content,
        bias_position,
    ) = (
        lax.all_gather(query_weight, "dp", axis=0, tiled=True),
        lax.all_gather(key_weight, "dp", axis=0, tiled=True),
        lax.all_gather(value_weight, "dp", axis=0, tiled=True),
        lax.all_gather(output_weight, "dp", axis=1, tiled=True),
        lax.all_gather(expand_weight, "dp", axis=0, tiled=True),
        lax.all_gather(contract_weight, "dp", axis=1, tiled=True),
        lax.all_gather(position_weight, "dp", axis=0, tiled=True),
        lax.all_gather(content_bias, "dp", axis=0, tiled=True),
        lax.all_gather(position_bias, "dp", axis=0, tiled=True),
    )
    gain_rows, shift_rows, table_rows, w_upsample, w_lateral, w_depth, bias_section, w_point = (
        lax.all_gather(norm_gain, ("dp", "tensor"), axis=1, tiled=True),
        lax.all_gather(norm_shift, ("dp", "tensor"), axis=1, tiled=True),
        lax.all_gather(species_table, ("dp", "tensor"), axis=1, tiled=True),
        lax.all_gather(upsample_weight, ("dp", "tensor"), axis=1, tiled=True),
        lax.all_gather(lateral_weight, ("dp", "tensor"), axis=1, tiled=True),
        lax.all_gather(depthwise_weight, ("dp", "tensor"), axis=1, tiled=True),
        lax.all_gather(section_bias, ("dp", "tensor"), axis=0, tiled=True),
        lax.all_gather(pointwise_weight, ("dp", "tensor"), axis=0, tiled=True),
    )
    gain_vals = gain_rows.astype(jnp.float32)
    shift_vals = shift_rows.astype(jnp.float32)
    species_mask = (jnp.arange(SPECIES, dtype=jnp.int32) == species[0]).astype(jnp.float32)
    species_row = jnp.sum(species_mask[:, None] * table_rows.astype(jnp.float32), axis=0)
    resid_in = activations[0].astype(jnp.float32) + species_row[None, :]
    normed_one = layer_norm(resid_in, gain_vals[0], shift_vals[0]).astype(jnp.bfloat16)
    normed_all = spread_rows(normed_one)
    length = normed_all.shape[0]
    local_heads = w_query.shape[1] // KEYD
    query_full = dot_plain(normed_all, w_query)
    key_low = dot_plain(normed_all, w_key).astype(jnp.bfloat16)
    value_low = dot_plain(normed_all, w_value).astype(jnp.bfloat16)
    content_flat = bias_content.astype(jnp.float32).T.reshape(-1)
    position_flat = bias_position.astype(jnp.float32).T.reshape(-1)
    query_content = (query_full + content_flat).astype(jnp.bfloat16)
    query_position = (query_full + position_flat).astype(jnp.bfloat16)
    basis_low = basis_table(length, BASIS).astype(jnp.bfloat16)
    rel_weight = jnp.transpose(w_position, (1, 2, 0)).reshape(BASIS, -1)
    rel_low = dot_plain(basis_low, rel_weight).astype(jnp.bfloat16)
    content_heads = query_content.reshape(length, local_heads, KEYD)
    position_heads = query_position.reshape(length, local_heads, KEYD)
    key_heads = key_low.reshape(length, local_heads, KEYD)
    value_heads = value_low.reshape(length, local_heads, VALD)
    rel_heads = rel_low.reshape(2 * length - 1, local_heads, KEYD)
    block_count = length // QBLOCK
    offsets = jnp.arange(block_count, dtype=jnp.int32) * QBLOCK
    score_scale = 1.0 / math.sqrt(KEYD)

    def forward_block(offset):
        scores = head_scores(content_heads, position_heads, key_heads, rel_heads)[0]
        row_max = jnp.max(scores, axis=-1, keepdims=True)
        exponent = jnp.exp(scores - row_max)
        totals = jnp.sum(exponent, axis=-1, keepdims=True)
        attn_probs = (exponent / totals).astype(jnp.bfloat16)
        mixed_block = jnp.einsum(
            "hbj,jhv->bhv", attn_probs, value_heads, preferred_element_type=jnp.float32
        )
        return (
            mixed_block.reshape(QBLOCK, -1).astype(jnp.bfloat16),
            (row_max + jnp.log(totals))[:, :, 0],
        )

    mixed_blocks, log_totals = lax.map(forward_block, offsets)
    mixed_rows = mixed_blocks.reshape(length, -1)
    resid_one = resid_in + collect_rows(dot_plain(mixed_rows, w_output))
    normed_two = layer_norm(resid_one, gain_vals[1], shift_vals[1]).astype(jnp.bfloat16)
    normed_two_all = spread_rows(normed_two)
    hidden_pre = dot_plain(normed_two_all, w_expand)
    hidden_low = exact_gelu(hidden_pre).astype(jnp.bfloat16)
    resid_two = resid_one + collect_rows(dot_plain(hidden_low, w_contract))
    section_in = resid_two.astype(jnp.bfloat16)
    mix_rows, grad_deep = section_forward(
        section_in, encoder[0], cotangent[0], w_upsample, w_lateral, bias_section, w_point
    )
    padded = padded_2(jnp.stack([mix_rows, grad_deep]), (("tensor", 1),), 1)
    output_part, encoder_grad, grad_resid_two, section_grads = section_backward(
        section_in,
        encoder[0],
        cotangent[0],
        padded[0],
        padded[1],
        w_upsample,
        w_lateral,
        w_depth,
        w_point,
    )
    section_out = output_part.astype(jnp.bfloat16)
    grad_ffn = spread_rows(grad_resid_two.astype(jnp.bfloat16))
    grad_contract_cols = dot_leading(grad_ffn, hidden_low)
    grad_hidden = dot_transposed(grad_ffn, w_contract)
    grad_hidden_pre = jax.vjp(exact_gelu, hidden_pre)[1](grad_hidden)[0].astype(jnp.bfloat16)
    grad_expand = dot_leading(normed_two_all, grad_hidden_pre)
    grad_normed_two = collect_rows(dot_transposed(grad_hidden_pre, w_expand))
    norm_pull = jax.vjp(layer_norm, resid_one, gain_vals[1], shift_vals[1])[1]
    grad_from_second, grad_gain_two, grad_shift_two = norm_pull(grad_normed_two)
    grad_resid_one = grad_resid_two + grad_from_second
    grad_attn = spread_rows(grad_resid_one.astype(jnp.bfloat16))
    grad_output_cols = dot_leading(grad_attn, mixed_rows)
    grad_mixed = dot_transposed(grad_attn, w_output).astype(jnp.bfloat16)
    grad_blocks = grad_mixed.reshape(block_count, QBLOCK, local_heads, VALD)

    def backward_block(sums_in, inputs):
        key_sum, value_sum, rel_sum = sums_in
        offset, grad_block, log_block = inputs
        scores, content_block, position_block, band_keys = head_scores(
            content_heads, position_heads, key_heads, rel_heads
        )
        attn_probs = jnp.exp(scores - log_block[:, :, None])
        grad_probs = jnp.einsum(
            "bhv,jhv->hbj", grad_block, value_heads, preferred_element_type=jnp.float32
        )
        centre = jnp.sum(attn_probs * grad_probs, axis=-1, keepdims=True)
        grad_scores = (attn_probs * (grad_probs - centre)).astype(jnp.bfloat16)
        value_sum = value_sum + jnp.einsum(
            "hbj,bhv->jhv",
            attn_probs.astype(jnp.bfloat16),
            grad_block,
            preferred_element_type=jnp.float32,
        )
        key_sum = (
            key_sum
            + jnp.einsum(
                "hbj,bhk->jhk", grad_scores, content_block, preferred_element_type=jnp.float32
            )
            * score_scale
        )
        grad_content = (
            jnp.einsum("hbj,jhk->bhk", grad_scores, key_heads, preferred_element_type=jnp.float32)
            * score_scale
        )
        grad_band = unskew_band(grad_scores, band_keys.shape[0])
        grad_position = (
            jnp.einsum("hbw,whk->bhk", grad_band, band_keys, preferred_element_type=jnp.float32)
            * score_scale
        )
        band_sum = (
            jnp.einsum(
                "hbw,bhk->whk", grad_band, position_block, preferred_element_type=jnp.float32
            )
            * score_scale
        )
        current = rel_sum
        rel_sum = current + band_sum
        return ((key_sum, value_sum, rel_sum), (grad_content, grad_position))

    initial = (
        jnp.zeros((length, local_heads, KEYD), jnp.float32),
        jnp.zeros((length, local_heads, VALD), jnp.float32),
        jnp.zeros((2 * length - 1, local_heads, KEYD), jnp.float32),
    )
    (key_sum, value_sum, rel_sum), (grad_content, grad_position) = lax.scan(
        backward_block, initial, (offsets, grad_blocks, log_totals)
    )
    grad_content = grad_content.reshape(length, -1)
    grad_position = grad_position.reshape(length, -1)
    grad_query = (grad_content + grad_position).astype(jnp.bfloat16)
    grad_content_bias = jnp.sum(grad_content, axis=0).reshape(local_heads, KEYD).T
    grad_position_bias = jnp.sum(grad_position, axis=0).reshape(local_heads, KEYD).T
    grad_keys = key_sum.reshape(length, -1).astype(jnp.bfloat16)
    grad_values = value_sum.reshape(length, -1).astype(jnp.bfloat16)
    grad_rel = rel_sum.reshape(2 * length - 1, -1).astype(jnp.bfloat16)
    grad_position_weight = jnp.transpose(
        dot_leading(basis_low, grad_rel).reshape(BASIS, local_heads, KEYD), (2, 0, 1)
    )
    grad_query_weight = dot_leading(normed_all, grad_query)
    grad_key_weight = dot_leading(normed_all, grad_keys)
    grad_value_weight = dot_leading(normed_all, grad_values)
    grad_normed_one = collect_rows(
        dot_transposed(grad_query, w_query)
        + dot_transposed(grad_keys, w_key)
        + dot_transposed(grad_values, w_value)
    )
    first_pull = jax.vjp(layer_norm, resid_in, gain_vals[0], shift_vals[0])[1]
    grad_from_first, grad_gain_one, grad_shift_one = first_pull(grad_normed_one)
    grad_resid_in = grad_resid_one + grad_from_first
    grad_table_sum = jnp.sum(grad_resid_in, axis=0)
    norm_cols = jnp.concatenate(
        [
            jnp.stack([grad_gain_one, grad_gain_two], axis=1),
            jnp.stack([grad_shift_one, grad_shift_two], axis=1),
            grad_table_sum[:, None] * species_mask[None, :],
        ],
        axis=1,
    )
    grad_upsample_cols, grad_lateral_cols, grad_taps_cols, grad_bias, grad_point = section_grads
    section_cols = jnp.concatenate([grad_taps_cols, grad_bias[:, None]], axis=1)
    (
        query_out,
        key_out,
        value_out,
        output_cols,
        expand_out,
        contract_cols,
        position_out,
        content_out,
        position_bias_out,
    ) = (
        lax.psum_scatter(grad_query_weight, "dp", scatter_dimension=0, tiled=True),
        lax.psum_scatter(grad_key_weight, "dp", scatter_dimension=0, tiled=True),
        lax.psum_scatter(grad_value_weight, "dp", scatter_dimension=0, tiled=True),
        lax.psum_scatter(grad_output_cols, "dp", scatter_dimension=0, tiled=True),
        lax.psum_scatter(grad_expand, "dp", scatter_dimension=0, tiled=True),
        lax.psum_scatter(grad_contract_cols, "dp", scatter_dimension=0, tiled=True),
        lax.psum_scatter(grad_position_weight, "dp", scatter_dimension=0, tiled=True),
        lax.psum_scatter(grad_content_bias, "dp", scatter_dimension=0, tiled=True),
        lax.psum_scatter(grad_position_bias, "dp", scatter_dimension=0, tiled=True),
    )
    small_out, upsample_cols, lateral_cols, point_out = (
        lax.psum_scatter(
            jnp.concatenate([norm_cols, section_cols], axis=1),
            ("dp", "tensor"),
            scatter_dimension=0,
            tiled=True,
        ),
        lax.psum_scatter(grad_upsample_cols, ("dp", "tensor"), scatter_dimension=0, tiled=True),
        lax.psum_scatter(grad_lateral_cols, ("dp", "tensor"), scatter_dimension=0, tiled=True),
        lax.psum_scatter(grad_point, ("dp", "tensor"), scatter_dimension=0, tiled=True),
    )
    norm_out = small_out[:, : 4 + SPECIES]
    section_small = small_out[:, 4 + SPECIES :]
    gain_out = norm_out[:, 0:2].T
    shift_out = norm_out[:, 2:4].T
    table_out = norm_out[:, 4 : 4 + SPECIES].T
    depth_out = section_small[:, 0:3].T
    section_bias_out = section_small[:, 3]
    return (
        section_out[None],
        grad_resid_in[None],
        encoder_grad[None],
        gain_out,
        shift_out,
        table_out,
        query_out,
        key_out,
        value_out,
        output_cols.T,
        expand_out,
        contract_cols.T,
        position_out,
        content_out,
        position_bias_out,
        upsample_cols.T,
        lateral_cols.T,
        depth_out,
        section_bias_out,
        point_out,
    )


def solution(mesh):
    return jax.shard_map(
        body,
        mesh=mesh,
        in_specs=(
            P("dp", "tensor", None),
            P("dp", "tensor", None),
            P("dp"),
            P("dp", "tensor", None),
            P(None, ("dp", "tensor")),
            P(None, ("dp", "tensor")),
            P(None, ("dp", "tensor")),
            P("dp", "tensor"),
            P("dp", "tensor"),
            P("dp", "tensor"),
            P("tensor", "dp"),
            P("dp", "tensor"),
            P("tensor", "dp"),
            P("dp", None, "tensor"),
            P("dp", "tensor"),
            P("dp", "tensor"),
            P(None, ("dp", "tensor")),
            P(None, ("dp", "tensor")),
            P(None, ("dp", "tensor")),
            P(("dp", "tensor")),
            P(("dp", "tensor"), None),
        ),
        out_specs=(
            P("dp", "tensor", None),
            P("dp", "tensor", None),
            P("dp", "tensor", None),
            P(None, ("dp", "tensor")),
            P(None, ("dp", "tensor")),
            P(None, ("dp", "tensor")),
            P("dp", "tensor"),
            P("dp", "tensor"),
            P("dp", "tensor"),
            P("tensor", "dp"),
            P("dp", "tensor"),
            P("tensor", "dp"),
            P("dp", None, "tensor"),
            P("dp", "tensor"),
            P("dp", "tensor"),
            P(None, ("dp", "tensor")),
            P(None, ("dp", "tensor")),
            P(None, ("dp", "tensor")),
            P(("dp", "tensor")),
            P(("dp", "tensor"), None),
        ),
        check_vma=False,
    )
```

profile of v0, /device:TPU:0, one launch (start us, length us, event | category | flops | bytes accessed | tf_op | source)
XLA Modules:
  0.0 1541.5 jit_solution(17201521276802982911)
XLA Ops:
  10.3 69.5 %all-gather.1 = bf16[32,48,2]{1,2,0:T(2,128)(2,1)S(1)} all-gather(bf16[1,48,2]{1,2,0:T(2,128)(2,1)} %bitcast.281), channel_id=1, replica_groups=mesh['dp'=8,'tensor'=4] {'dp','tensor'}, dimensions={0}, use_global_device_ids=true | all-gather | bytes 6336 | tf_op jit(solution)/shard_map/all_gather | solution.py:218
  82.2 63.2 %all-gather.2 = bf16[32,48,2]{1,2,0:T(2,128)(2,1)S(1)} all-gather(bf16[1,48,2]{1,2,0:T(2,128)(2,1)} %bitcast.282), channel_id=1, replica_groups=mesh['dp'=8,'tensor'=4] {'dp','tensor'}, dimensions={0}, use_global_device_ids=true | all-gather | bytes 6336 | tf_op jit(solution)/shard_map/all_gather | solution.py:216
  145.6 65.3 %all-gather.3 = bf16[32,48,2]{1,2,0:T(2,128)(2,1)S(1)} all-gather(bf16[1,48,2]{1,2,0:T(2,128)(2,1)} %bitcast.283), channel_id=1, replica_groups=mesh['dp'=8,'tensor'=4] {'dp','tensor'}, dimensions={0}, use_global_device_ids=true | all-gather | bytes 6336 | tf_op jit(solution)/shard_map/all_gather | solution.py:217
  288.2 21.0 %reduce-scatter.19.cloned.1.call-done = bf16[64,1536]{1,0:T(8,128)(2,1)} async-done(((bf16[256,1536]{1,0:T(8,128)(2,1)}), bf16[64,1536]{1,0:T(8,128)(2,1)}) %reduce-scatter.19.cloned.1.call-update) | async-done | bytes 196624 | tf_op jit(solution)/shard_map/reduce_scatter | solution.py:89
  312.6 18.2 %all_gather.75 = bf16[256,1536]{1,0:T(8,128)(2,1)S(1)} all-gather(bf16[64,1536]{1,0:T(8,128)(2,1)S(1)} %add_convert_fusion.3), channel_id=1, replica_groups=mesh['dp'=8,'tensor'=4] {'tensor'}, dimensions={0}, use_global_device_ids=true | all-gather | bytes 983040 | tf_op jit(solution)/shard_map/all_gather | solution.py:85
  344.2 25.8 %all-gather.20.cloned.1.call-done = bf16[768,1536]{0,1:T(8,128)(2,1)} async-done(((bf16[768,192]{0,1:T(8,128)(2,1)}), bf16[768,1536]{0,1:T(8,128)(2,1)}) %all-gather.20.cloned.1.call-update) | async-done | bytes 2359312 | tf_op jit(solution)/shard_map/all_gather | solution.py:210
  375.6 40.9 %all-reduce.2 = bf16[1536]{0:T(1024)(128)(2,1)S(1)} all-reduce(bf16[1536]{0:T(1024)(128)(2,1)S(1)} %dynamic-update-slice), channel_id=1, replica_groups=mesh['dp'=8,'tensor'=4] {'dp','tensor'}, use_global_device_ids=true, to_apply=%add.2 | all-reduce | flops 1536 | bytes 6144
  416.5 65.2 %all-gather = bf16[32,48,3]{1,2,0:T(4,128)(2,1)S(1)} all-gather(bf16[1,48,3]{1,2,0:T(4,128)(2,1)S(1)} %bitcast.275), channel_id=1, replica_groups=mesh['dp'=8,'tensor'=4] {'dp','tensor'}, dimensions={0}, use_global_device_ids=true | all-gather | bytes 9504 | tf_op jit(solution)/shard_map/all_gather | solution.py:221
  490.6 19.3 %all-gather.26.cloned.1.call-done = bf16[1536,1536]{1,0:T(8,128)(2,1)} async-done(((bf16[48,1536]{1,0:T(8,128)(2,1)}), bf16[1536,1536]{1,0:T(8,128)(2,1)}) %all-gather.26.cloned.1.call-update) | async-done | bytes 4718608 | tf_op jit(solution)/shard_map/all_gather | solution.py:223
  514.8 59.9 %all-gather.24.cloned.1.call-done = bf16[1536,1536]{0,1:T(8,128)(2,1)} async-done(((bf16[1536,48]{0,1:T(8,128)(2,1)}), bf16[1536,1536]{0,1:T(8,128)(2,1)}) %all-gather.24.cloned.1.call-update) | async-done | bytes 4718608 | tf_op jit(solution)/shard_map/all_gather | solution.py:220
  620.1 22.4 %reduce-scatter.23.cloned.1.call-done = bf16[64,1536]{1,0:T(8,128)(2,1)} async-done(((bf16[256,1536]{1,0:T(8,128)(2,1)}), bf16[64,1536]{1,0:T(8,128)(2,1)}) %reduce-scatter.23.cloned.1.call-update) | async-done | bytes 196624 | tf_op jit(solution)/shard_map/reduce_scatter | solution.py:89
  647.4 18.0 %all_gather.83 = bf16[256,1536]{1,0:T(8,128)(2,1)S(1)} all-gather(bf16[64,1536]{1,0:T(8,128)(2,1)S(1)} %fusion.60), channel_id=1, replica_groups=mesh['dp'=8,'tensor'=4] {'tensor'}, dimensions={0}, use_global_device_ids=true | all-gather | bytes 983040 | tf_op jit(solution)/shard_map/all_gather | solution.py:85
  699.9 22.6 %reduce-scatter.25.cloned.1.call-done = bf16[64,1536]{1,0:T(8,128)(2,1)} async-done(((bf16[256,1536]{1,0:T(8,128)(2,1)}), bf16[64,1536]{1,0:T(8,128)(2,1)}) %reduce-scatter.25.cloned.1.call-update) | async-done | bytes 196624 | tf_op jit(solution)/shard_map/reduce_scatter | solution.py:89
  773.4 24.2 %all-reduce.6 = (f32[64,32,2]{1,2,0:T(2,128)S(1)}, f32[64,2]{0,1:T(2,128)S(1)}, f32[64,2]{0,1:T(2,128)S(1)}) all-reduce(f32[64,32,2]{1,2,0:T(2,128)S(1)} %copy.99, f32[64,2]{0,1:T(2,128)S(1)} %bitcast.273, f32[64,2]{0,1:T(2,128)S(1)} %bitcast.272), channel_id=13, replica_groups=mesh['dp'=8,'tensor'=4] {'dp'}, use_global_device_ids=true, to_apply=%region_33.34.clone | all-reduce | flops 4352 | bytes 34816
  799.5 23.9 %reduce-scatter.45.cloned.1.call-done = f32[48,10]{1,0:T(8,128)} async-done(((f32[1536,10]{1,0:T(8,128)}), f32[48,10]{1,0:T(8,128)}) %reduce-scatter.45.cloned.1.call-update) | async-done | bytes 1936
  829.1 32.1 %reduce-scatter.27.cloned.1.call-done = f32[192,128]{1,0:T(8,128)} async-done(((f32[1536,128]{1,0:T(8,128)}), f32[192,128]{1,0:T(8,128)}) %reduce-scatter.27.cloned.1.call-update) | async-done | bytes 98320 | tf_op jit(solution)/shard_map/reduce_scatter | solution.py:402
  861.2 38.7 %reduce-scatter.29.cloned.1.call-done = f32[192,128]{1,0:T(8,128)} async-done(((f32[1536,128]{1,0:T(8,128)}), f32[192,128]{1,0:T(8,128)}) %reduce-scatter.29.cloned.1.call-update) | async-done | bytes 98320 | tf_op jit(solution)/shard_map/reduce_scatter | solution.py:403
  899.9 46.2 %reduce-scatter.33.cloned.1.call-done = f32[192,384]{1,0:T(8,128)} async-done(((f32[1536,384]{1,0:T(8,128)}), f32[192,384]{1,0:T(8,128)}) %reduce-scatter.33.cloned.1.call-update) | async-done | bytes 294928 | tf_op jit(solution)/shard_map/reduce_scatter | solution.py:405
  946.1 46.5 %reduce-scatter.31.cloned.1.call-done = f32[192,384]{1,0:T(8,128)} async-done(((f32[1536,384]{1,0:T(8,128)}), f32[192,384]{1,0:T(8,128)}) %reduce-scatter.31.cloned.1.call-update) | async-done | bytes 294928 | tf_op jit(solution)/shard_map/reduce_scatter | solution.py:404
  992.6 57.7 %reduce-scatter.37.cloned.1.call-done = f32[192,768]{1,0:T(8,128)} async-done(((f32[1536,768]{1,0:T(8,128)}), f32[192,768]{1,0:T(8,128)}) %reduce-scatter.37.cloned.1.call-update) | async-done | bytes 589840 | tf_op jit(solution)/shard_map/reduce_scatter | solution.py:407
  1050.3 58.2 %reduce-scatter.35.cloned.1.call-done = f32[192,768]{1,0:T(8,128)} async-done(((f32[1536,768]{1,0:T(8,128)}), f32[192,768]{1,0:T(8,128)}) %reduce-scatter.35.cloned.1.call-update) | async-done | bytes 589840 | tf_op jit(solution)/shard_map/reduce_scatter | solution.py:406
  1108.5 142.0 %reduce-scatter.39.cloned.1.call-done = f32[48,1536]{1,0:T(8,128)} async-done(((f32[1536,1536]{1,0:T(8,128)}), f32[48,1536]{1,0:T(8,128)}) %reduce-scatter.39.cloned.1.call-update) | async-done | bytes 294928 | tf_op jit(solution)/shard_map/reduce_scatter | solution.py:419
  1250.5 142.1 %reduce-scatter.41.cloned.1.call-done = f32[48,1536]{1,0:T(8,128)} async-done(((f32[1536,1536]{1,0:T(8,128)}), f32[48,1536]{1,0:T(8,128)}) %reduce-scatter.41.cloned.1.call-update) | async-done | bytes 294928 | tf_op jit(solution)/shard_map/reduce_scatter | solution.py:420
  1392.6 140.9 %reduce-scatter.43.cloned.1.call-done = f32[48,1536]{1,0:T(8,128)} async-done(((f32[1536,1536]{1,0:T(8,128)}), f32[48,1536]{1,0:T(8,128)}) %reduce-scatter.43.cloned.1.call-update) | async-done | bytes 294928 | tf_op jit(solution)/shard_map/reduce_scatter | solution.py:421
  (349 shorter events, 258.8 us)
Async XLA Ops:
  8.0 566.7 %copy-start = (bf16[1,128,1536]{2,1,0:T(8,128)(2,1)S(1)}, bf16[1,128,1536]{2,1,0:T(8,128)(2,1)}, u32[]{:S(2)}) copy-start(bf16[1,128,1536]{2,1,0:T(8,128)(2,1)} %param.22) | copy-start | bytes 1179652
  8.0 273.8 %all-gather.14.cloned.1.call-start = ((), (), s32[]{:S(2)}) async-start(), calls=%async_computation.14 | async-start | bytes 1327104 | tf_op jit(solution)/shard_map/all_gather | solution.py:207
  8.8 275.4 %all-gather.16.cloned.1.call-start = ((), (), s32[]{:S(2)}) async-start(), calls=%async_computation.15 | async-start | bytes 1327104 | tf_op jit(solution)/shard_map/all_gather | solution.py:208
  9.5 299.7 %reduce-scatter.19.cloned.1.call-start = ((), (), s32[]{:S(2)}) async-start(), calls=%async_computation.16 | async-start | bytes 983040 | tf_op jit(solution)/shard_map/reduce_scatter | solution.py:89
  287.0 52.2 %all-gather.18.cloned.1.call-start = ((), (), s32[]{:S(2)}) async-start(), calls=%async_computation.17 | async-start | bytes 2654208 | tf_op jit(solution)/shard_map/all_gather | solution.py:209
  287.6 82.4 %all-gather.20.cloned.1.call-start = ((), (), s32[]{:S(2)}) async-start(), calls=%async_computation.18 | async-start | bytes 2654208 | tf_op jit(solution)/shard_map/all_gather | solution.py:210
  288.2 193.7 %reduce-scatter.21.cloned.1.call-start = ((), (), s32[]{:S(2)}) async-start(), calls=%async_computation.19 | async-start | bytes 983040 | tf_op jit(solution)/shard_map/reduce_scatter | solution.py:89
  373.5 109.4 %all-gather.22.cloned.1.call-start = ((), (), s32[]{:S(2)}) async-start(), calls=%async_computation.20 | async-start | bytes 4866048 | tf_op jit(solution)/shard_map/all_gather | solution.py:219
  374.1 135.9 %all-gather.26.cloned.1.call-start = ((), (), s32[]{:S(2)}) async-start(), calls=%async_computation.22 | async-start | bytes 4866048 | tf_op jit(solution)/shard_map/all_gather | solution.py:223
  374.7 200.1 %all-gather.24.cloned.1.call-start = ((), (), s32[]{:S(2)}) async-start(), calls=%async_computation.21 | async-start | bytes 4866048 | tf_op jit(solution)/shard_map/all_gather | solution.py:220
  375.2 267.2 %reduce-scatter.23.cloned.1.call-start = ((), (), s32[]{:S(2)}) async-start(), calls=%async_computation.23 | async-start | bytes 983040 | tf_op jit(solution)/shard_map/reduce_scatter | solution.py:89
  579.1 4.6 collective-permute-start
  582.3 5.6 collective-permute-start.1
  620.0 102.5 %reduce-scatter.25.cloned.1.call-start = ((), (), s32[]{:S(2)}) async-start(), calls=%async_computation.24 | async-start | bytes 983040 | tf_op jit(solution)/shard_map/reduce_scatter | solution.py:89
  699.7 123.7 %reduce-scatter.45.cloned.1.call-start = ((), (), s32[]{:S(2)}) async-start(), calls=%async_computation.34 | async-start | bytes 811008
  728.5 132.7 %reduce-scatter.27.cloned.1.call-start = ((), (), s32[]{:S(2)}) async-start(), calls=%async_computation.25 | async-start | bytes 884736 | tf_op jit(solution)/shard_map/reduce_scatter | solution.py:402
  730.8 169.1 %reduce-scatter.29.cloned.1.call-start = ((), (), s32[]{:S(2)}) async-start(), calls=%async_computation.26 | async-start | bytes 884736 | tf_op jit(solution)/shard_map/reduce_scatter | solution.py:403
  732.3 213.8 %reduce-scatter.33.cloned.1.call-start = ((), (), s32[]{:S(2)}) async-start(), calls=%async_computation.28 | async-start | bytes 2654208 | tf_op jit(solution)/shard_map/reduce_scatter | solution.py:405
  735.3 257.3 %reduce-scatter.31.cloned.1.call-start = ((), (), s32[]{:S(2)}) async-start(), calls=%async_computation.27 | async-start | bytes 2654208 | tf_op jit(solution)/shard_map/reduce_scatter | solution.py:404
  737.4 312.9 %reduce-scatter.37.cloned.1.call-start = ((), (), s32[]{:S(2)}) async-start(), calls=%async_computation.30 | async-start | bytes 5308416 | tf_op jit(solution)/shard_map/reduce_scatter | solution.py:407
  741.4 367.1 %reduce-scatter.35.cloned.1.call-start = ((), (), s32[]{:S(2)}) async-start(), calls=%async_computation.29 | async-start | bytes 5308416 | tf_op jit(solution)/shard_map/reduce_scatter | solution.py:406
  745.4 505.1 %reduce-scatter.39.cloned.1.call-start = ((), (), s32[]{:S(2)}) async-start(), calls=%async_computation.31 | async-start | bytes 9732096 | tf_op jit(solution)/shard_map/reduce_scatter | solution.py:419
  751.6 641.0 %reduce-scatter.41.cloned.1.call-start = ((), (), s32[]{:S(2)}) async-start(), calls=%async_computation.32 | async-start | bytes 9732096 | tf_op jit(solution)/shard_map/reduce_scatter | solution.py:420
  756.7 776.8 %reduce-scatter.43.cloned.1.call-start = ((), (), s32[]{:S(2)}) async-start(), calls=%async_computation.33 | async-start | bytes 9732096 | tf_op jit(solution)/shard_map/reduce_scatter | solution.py:421
  (77 other events, 2369.1 us)
Sparse Core Ops, SparseCore 0:
  10.8 26.7 all-gather.13
  39.4 24.0 all-gather.15
  287.1 22.0 reduce-scatter.18
  310.9 28.2 all-gather.17
  340.9 29.0 all-gather.19
  373.6 25.6 reduce-scatter.20
  620.1 22.3 reduce-scatter.22
  699.8 22.5 reduce-scatter.24
Sparse Core Ops, SparseCore 1:
  376.8 68.4 all-gather.21
  447.9 62.0 all-gather.25
  512.6 62.1 all-gather.23
  728.6 94.8 reduce-scatter.44
  827.2 34.0 reduce-scatter.26
  865.0 34.9 reduce-scatter.28
  903.7 42.3 reduce-scatter.32
  950.3 42.3 reduce-scatter.30
  996.5 53.7 reduce-scatter.36
  1054.7 53.7 reduce-scatter.34
  1114.8 135.6 reduce-scatter.38
  1258.0 134.5 reduce-scatter.40
  1398.9 134.5 reduce-scatter.42
where the time goes:
time: 1550 us; the launch traced here: 1540 us
  waiting for transfers between devices  916 us (59%)
  blocking collectives  443 us (29%)
  matrix products  86.2 us (6%)
  local copies, waits for them, and re-layouts  48.7 us (3%)
  other arithmetic  22.8 us (1%)
  between operations  19 us (1%)
    reduce_scatter x1, waiting for transfers between devices, body(): lax.psum_scatter(grad_lateral_cols, ('dp', 'tensor'), scatter_dimension=0...  142 us
    reduce_scatter x1, waiting for transfers between devices, body(): lax.psum_scatter(grad_upsample_cols, ('dp', 'tensor'), scatter_dimension=...  142 us
    reduce_scatter x1, waiting for transfers between devices, body(): lax.psum_scatter(grad_point, ('dp', 'tensor'), scatter_dimension=0, tiled...  141 us
    all_gather x4, blocking collectives, spread_rows(): return lax.all_gather(row_block, 'tensor', axis=0, tiled=True)  71.6 us
    all_gather x1, blocking collectives, body(): lax.all_gather(species_table, ('dp', 'tensor'), axis=1, tiled=True)  69.5 us
    reduce_scatter x4, waiting for transfers between devices, collect_rows(): lax.psum_scatter(partial_rows.astype(jnp.bfloat16), 'tensor', scatter_dim...  65.9 us
    all_gather x1, blocking collectives, body(): lax.all_gather(norm_shift, ('dp', 'tensor'), axis=1, tiled=True)  65.3 us
    all_gather x1, blocking collectives, body(): lax.all_gather(depthwise_weight, ('dp', 'tensor'), axis=1, tiled=True)  65.2 us
  transfers between devices with their start and end apart: 23, of which 18 were waited for; matrix products, arithmetic and copies ran while one was open for 5% of the time, Pallas kernels for 0%

commit v1 on v0

v1 whole, which is shorter than its diff:
```python
import math

import jax
import jax.numpy as jnp
from jax import lax
from jax.sharding import PartitionSpec as P

KEYD = 64
VALD = 192
BASIS = 32
SPECIES = 2
SCALE = 1.0 / math.sqrt(KEYD)
LOW = jnp.bfloat16


def dot_plain(left_side, right_side):
    return jnp.dot(left_side, right_side, preferred_element_type=jnp.float32)


def dot_transposed(left_side, right_side):
    return lax.dot_general(
        left_side, right_side, (((1,), (1,)), ((), ())), preferred_element_type=jnp.float32
    )


def dot_leading(left_side, right_side):
    return lax.dot_general(
        left_side, right_side, (((0,), (0,)), ((), ())), preferred_element_type=jnp.float32
    )


def exact_gelu(values):
    return jax.nn.gelu(values, approximate=False)


def normalize(values):
    centred = values - jnp.mean(values, axis=-1, keepdims=True)
    variance = jnp.mean(centred * centred, axis=-1, keepdims=True)
    scale = lax.rsqrt(variance + 1e-05)
    return centred * scale, scale


def normalize_back(unit, scale, grad_unit):
    return scale * (
        grad_unit
        - jnp.mean(grad_unit, axis=-1, keepdims=True)
        - unit * jnp.mean(grad_unit * unit, axis=-1, keepdims=True)
    )


def basis_table(length, features):
    distance = jnp.arange(2 * length - 1).astype(jnp.float32) - (length - 1)
    halves = features // 2
    fraction = jnp.arange(halves).astype(jnp.float32) / (halves - 1)
    lifetimes = 3.0 * jnp.power(length / 3.0, fraction)
    decays = jnp.exp(-0.6931471805599453 * jnp.abs(distance)[:, None] / lifetimes[None, :])
    return jnp.concatenate([decays, jnp.sign(distance)[:, None] * decays], axis=1)


def skew_band(banded, length):
    head_count, row_count, band_width = banded.shape
    flipped = banded[:, :, ::-1]
    flat = flipped.reshape(head_count, row_count * band_width)
    flat = flat[:, row_count - 1 : row_count - 1 + row_count * (band_width - 1)]
    return flat.reshape(head_count, row_count, band_width - 1)[:, :, :length]


def unskew_band(grid, band_width):
    head_count, row_count, length = grid.shape
    padded = jnp.pad(grid, ((0, 0), (0, 0), (0, band_width - 1 - length)))
    flat = jnp.pad(
        padded.reshape(head_count, row_count * (band_width - 1)), ((0, 0), (row_count - 1, 1))
    )
    return flat.reshape(head_count, row_count, band_width)[:, :, ::-1]


def from_ahead(rows, step):
    count = lax.axis_size("tensor")
    return lax.ppermute(rows, "tensor", [((i + step) % count, i) for i in range(count)])


def spread_rows(rows):
    count = lax.axis_size("tensor")
    return jnp.concatenate([rows] + [from_ahead(rows, k) for k in range(1, count)], axis=0)


def collect_rows(partial_rows):
    count = lax.axis_size("tensor")
    low = partial_rows.astype(LOW).reshape(count, -1, partial_rows.shape[1])
    total = partial_rows.reshape(low.shape)[0]
    for k in range(1, count):
        total = total + from_ahead(low[k], count - k).astype(jnp.float32)
    return total


def to_true(rows):
    return jnp.roll(rows, lax.axis_index("tensor") * (rows.shape[0] // lax.axis_size("tensor")), 0)


def to_own(rows):
    return jnp.roll(rows, -lax.axis_index("tensor") * (rows.shape[0] // lax.axis_size("tensor")), 0)


def gather_dp(shard, axis=0):
    return lax.all_gather(shard, "dp", axis=axis, tiled=True)


def scatter_dp(whole):
    return lax.psum_scatter(whole, "dp", scatter_dimension=0, tiled=True)


def scatter_tensor(whole):
    return lax.psum_scatter(whole, "tensor", scatter_dimension=0, tiled=True)


def halo(cells):
    count = lax.axis_size("tensor")
    ends = count - 1
    before = lax.ppermute(cells[:, -1:], "tensor", [(i, i + 1) for i in range(ends)])
    after = lax.ppermute(cells[:, :1], "tensor", [(i + 1, i) for i in range(ends)])
    return jnp.concatenate([before, cells, after], axis=1)


def body(
    activations,
    encoder,
    species,
    cotangent,
    norm_gain,
    norm_shift,
    species_table,
    query_weight,
    key_weight,
    value_weight,
    output_weight,
    expand_weight,
    contract_weight,
    position_weight,
    content_bias,
    position_bias,
    upsample_weight,
    lateral_weight,
    depthwise_weight,
    section_bias,
    pointwise_weight,
):
    windows = lax.axis_size("dp")
    count = lax.axis_size("tensor")
    own = activations.shape[1]
    length = own * count
    width = activations.shape[2]
    local_heads = query_weight.shape[1] // KEYD
    keys = local_heads * KEYD
    values = local_heads * VALD

    raw_all = spread_rows(activations[0])
    attn_shard = jnp.concatenate([query_weight, key_weight, value_weight, output_weight.T], axis=1)
    w_attn = gather_dp(attn_shard)
    w_query = w_attn[:, :keys]
    w_key = w_attn[:, keys : 2 * keys]
    w_value = w_attn[:, 2 * keys : 2 * keys + values]
    w_output_t = w_attn[:, 2 * keys + values :]

    small = jnp.concatenate(
        [norm_gain, norm_shift, species_table, depthwise_weight, section_bias[None]], axis=0
    )
    small_group = jnp.swapaxes(lax.all_gather(small, "tensor", axis=0), 0, 1).reshape(10, -1)
    norm_group = small_group[:6]
    heads_group = jnp.concatenate(
        [position_weight.reshape(-1), content_bias.reshape(-1), position_bias.reshape(-1)]
    )
    packed = gather_dp(jnp.concatenate([norm_group.reshape(-1), heads_group])[None])
    channels = norm_group.shape[1]
    norm_all = jnp.swapaxes(packed[:, : 6 * channels].reshape(windows, 6, channels), 0, 1)
    norm_all = norm_all.reshape(6, width).astype(jnp.float32)
    heads_all = packed[:, 6 * channels :]
    n_position = position_weight.size
    n_bias = content_bias.size
    w_position = heads_all[:, :n_position].reshape(KEYD, BASIS, local_heads)
    bias_content = heads_all[:, n_position : n_position + n_bias].reshape(KEYD, local_heads)
    bias_position = heads_all[:, n_position + n_bias :].reshape(KEYD, local_heads)
    gain_vals, shift_vals, table_rows = norm_all[:2], norm_all[2:4], norm_all[4:]
    depth_taps = small_group[6:9].astype(jnp.float32)
    bias_section = small_group[9].astype(jnp.float32)

    w_point = lax.all_gather(pointwise_weight, "tensor", axis=0, tiled=True)
    w_up = lax.all_gather(upsample_weight.T, "tensor", axis=0, tiled=True)
    w_lat = lax.all_gather(lateral_weight.T, "tensor", axis=0, tiled=True)
    cot_all = gather_dp(cotangent[0])
    ffn_shard = jnp.concatenate([expand_weight, contract_weight.T], axis=1)
    w_ffn = gather_dp(ffn_shard)
    hidden_count = expand_weight.shape[1]
    w_expand = w_ffn[:, :hidden_count]
    w_contract_t = w_ffn[:, hidden_count:]
    enc_all = gather_dp(encoder[0])

    fine = 2 * own
    grad_deep = dot_transposed(cot_all, w_point).astype(LOW)
    grad_wide = halo(grad_deep.reshape(windows, fine, channels)).astype(jnp.float32)
    grad_mix = (
        depth_taps[0] * grad_wide[:, 2:]
        + depth_taps[1] * grad_wide[:, 1:-1]
        + depth_taps[2] * grad_wide[:, :-2]
    ).astype(LOW)
    grad_coarse = jnp.sum(
        grad_mix.astype(jnp.float32).reshape(windows * own, 2, channels), axis=1
    ).astype(LOW)
    grad_resid_two = scatter_dp(dot_plain(grad_coarse, w_up).astype(LOW))
    grad_ffn_all = spread_rows(grad_resid_two)
    grad_resid_two = grad_resid_two.astype(jnp.float32)

    species_mask = (jnp.arange(SPECIES, dtype=jnp.int32) == species[0]).astype(jnp.float32)
    species_row = jnp.sum(species_mask[:, None] * table_rows, axis=0)
    resid_in_all = raw_all.astype(jnp.float32) + species_row[None, :]
    unit_one_all, scale_one_all = normalize(resid_in_all)
    normed_all = (unit_one_all * gain_vals[0] + shift_vals[0]).astype(LOW)
    resid_in = resid_in_all[:own]
    content_flat = bias_content.astype(jnp.float32).T.reshape(-1)
    position_flat = bias_position.astype(jnp.float32).T.reshape(-1)
    query_full = dot_plain(normed_all, w_query)
    query_content = to_true((query_full + content_flat).astype(LOW))
    query_position = to_true((query_full + position_flat).astype(LOW))
    key_low = to_true(dot_plain(normed_all, w_key).astype(LOW))
    value_low = to_true(dot_plain(normed_all, w_value).astype(LOW))
    basis_low = basis_table(length, BASIS).astype(LOW)
    rel_weight = jnp.transpose(w_position, (1, 2, 0)).reshape(BASIS, -1)
    rel_low = dot_plain(basis_low, rel_weight).astype(LOW)
    content_heads = query_content.reshape(length, local_heads, KEYD)
    position_heads = query_position.reshape(length, local_heads, KEYD)
    key_heads = key_low.reshape(length, local_heads, KEYD)
    value_heads = value_low.reshape(length, local_heads, VALD)
    rel_heads = rel_low.reshape(2 * length - 1, local_heads, KEYD)
    content = jnp.einsum(
        "bhk,jhk->hbj", content_heads, key_heads, preferred_element_type=jnp.float32
    )
    banded = jnp.einsum(
        "bhk,whk->hbw", position_heads, rel_heads, preferred_element_type=jnp.float32
    )
    scores = (content + skew_band(banded, length)) * SCALE
    attn_soft = jax.nn.softmax(scores, axis=-1)
    attn_low = attn_soft.astype(LOW)
    mixed = jnp.einsum("hbj,jhv->bhv", attn_low, value_heads, preferred_element_type=jnp.float32)
    mixed_rows = to_own(mixed.reshape(length, -1).astype(LOW))
    resid_one = resid_in + collect_rows(dot_transposed(mixed_rows, w_output_t))

    unit_two, scale_two = normalize(resid_one)
    normed_two = (unit_two * gain_vals[1] + shift_vals[1]).astype(LOW)
    normed_two_all = spread_rows(normed_two)
    hidden_pre = dot_plain(normed_two_all, w_expand)
    hidden_low = exact_gelu(hidden_pre).astype(LOW)
    grad_hidden = dot_plain(grad_ffn_all, w_contract_t)
    grad_hidden_pre = jax.vjp(exact_gelu, hidden_pre)[1](grad_hidden)[0].astype(LOW)
    grad_normed_two = collect_rows(dot_transposed(grad_hidden_pre, w_expand))
    grad_from_second = normalize_back(unit_two, scale_two, grad_normed_two * gain_vals[1])
    grad_resid_one = grad_resid_two + grad_from_second
    grad_gain_two = jnp.sum(grad_normed_two * unit_two, axis=0)
    grad_shift_two = jnp.sum(grad_normed_two, axis=0)
    grad_attn_own = spread_rows(grad_resid_one.astype(LOW))

    resid_two = resid_one + collect_rows(dot_transposed(hidden_low, w_contract_t))
    section_all = gather_dp(resid_two.astype(LOW))
    coarse = dot_transposed(section_all, w_up).reshape(windows, own, channels)
    section_mix = (
        jnp.repeat(coarse, 2, axis=1)
        + dot_transposed(enc_all, w_lat).reshape(windows, fine, channels)
        + bias_section
    ).astype(LOW)
    mix_wide = halo(section_mix).astype(jnp.float32)
    deep_rows = (
        depth_taps[0] * mix_wide[:, :-2]
        + depth_taps[1] * mix_wide[:, 1:-1]
        + depth_taps[2] * mix_wide[:, 2:]
    ).astype(LOW)
    deep_rows = deep_rows.reshape(windows * fine, channels)
    section_out = scatter_dp(dot_plain(deep_rows, w_point).astype(LOW))
    grad_mix_rows = grad_mix.reshape(windows * fine, channels)
    encoder_grad = scatter_dp(dot_plain(grad_mix_rows, w_lat).astype(LOW)).astype(jnp.float32)
    grad_centre = grad_wide[:, 1:-1]
    grad_section_small = jnp.stack(
        [jnp.sum(mix_wide[:, s : s + fine] * grad_centre, axis=(0, 1)) for s in range(3)]
        + [jnp.sum(grad_mix.astype(jnp.float32), axis=(0, 1))],
        axis=1,
    )
    upsample_cols = scatter_tensor(dot_leading(grad_coarse, section_all).astype(LOW))
    lateral_cols = scatter_tensor(dot_leading(grad_mix_rows, enc_all).astype(LOW))
    point_out = scatter_tensor(dot_leading(deep_rows, cot_all).astype(LOW))

    grad_contract_cols = dot_leading(grad_ffn_all, hidden_low)
    grad_expand = dot_leading(normed_two_all, grad_hidden_pre)
    ffn_out = scatter_dp(
        jnp.concatenate([grad_expand.astype(LOW), grad_contract_cols.astype(LOW)], axis=1)
    ).astype(jnp.float32)

    grad_output_cols = dot_leading(grad_attn_own, mixed_rows)
    grad_mixed = to_true(dot_plain(grad_attn_own, w_output_t).astype(LOW))
    grad_block = grad_mixed.reshape(length, local_heads, VALD)
    grad_probs = jnp.einsum(
        "bhv,jhv->hbj", grad_block, value_heads, preferred_element_type=jnp.float32
    )
    centre = jnp.sum(attn_soft * grad_probs, axis=-1, keepdims=True)
    grad_scores = (attn_soft * (grad_probs - centre)).astype(LOW)
    value_sum = jnp.einsum("hbj,bhv->jhv", attn_low, grad_block, preferred_element_type=jnp.float32)
    key_sum = (
        jnp.einsum("hbj,bhk->jhk", grad_scores, content_heads, preferred_element_type=jnp.float32)
        * SCALE
    )
    grad_content = (
        jnp.einsum("hbj,jhk->bhk", grad_scores, key_heads, preferred_element_type=jnp.float32)
        * SCALE
    ).reshape(length, -1)
    grad_band = unskew_band(grad_scores, rel_heads.shape[0])
    grad_position = (
        jnp.einsum("hbw,whk->bhk", grad_band, rel_heads, preferred_element_type=jnp.float32)
        * SCALE
    ).reshape(length, -1)
    rel_sum = (
        jnp.einsum("hbw,bhk->whk", grad_band, position_heads, preferred_element_type=jnp.float32)
        * SCALE
    )
    grad_query = to_own((grad_content + grad_position).astype(LOW))
    grad_content_bias = jnp.sum(grad_content, axis=0).reshape(local_heads, KEYD).T
    grad_position_bias = jnp.sum(grad_position, axis=0).reshape(local_heads, KEYD).T
    grad_keys = to_own(key_sum.reshape(length, -1).astype(LOW))
    grad_values = to_own(value_sum.reshape(length, -1).astype(LOW))
    grad_rel = rel_sum.reshape(2 * length - 1, -1).astype(LOW)
    grad_position_weight = jnp.transpose(
        dot_leading(basis_low, grad_rel).reshape(BASIS, local_heads, KEYD), (2, 0, 1)
    )
    grad_qkv = jnp.concatenate([grad_query, grad_keys, grad_values], axis=1)
    grad_normed_part = dot_transposed(grad_qkv, w_attn[:, : 2 * keys + values])
    grad_normed_one = collect_rows(grad_normed_part)
    attn_out = scatter_dp(
        jnp.concatenate(
            [dot_leading(normed_all, grad_qkv).astype(LOW), grad_output_cols.astype(LOW)], axis=1
        )
    ).astype(jnp.float32)
    grad_resid_in = grad_resid_one + normalize_back(
        unit_one_all[:own], scale_one_all[:own], grad_normed_one * gain_vals[0]
    )

    table_part = jnp.sum(grad_resid_one, axis=0) + jnp.sum(
        normalize_back(unit_one_all, scale_one_all, grad_normed_part * gain_vals[0]), axis=0
    )
    norm_cols = jnp.concatenate(
        [
            jnp.sum(grad_normed_part * unit_one_all, axis=0)[None],
            grad_gain_two[None],
            jnp.sum(grad_normed_part, axis=0)[None],
            grad_shift_two[None],
            table_part[None] * species_mask[:, None],
        ],
        axis=0,
    )
    norm_cols = jnp.swapaxes(norm_cols.reshape(6, windows, channels), 0, 1)
    heads_cols = jnp.concatenate(
        [
            grad_position_weight.reshape(windows, -1),
            grad_content_bias.reshape(windows, -1),
            grad_position_bias.reshape(windows, -1),
        ],
        axis=1,
    )
    small_out = scatter_dp(jnp.concatenate([norm_cols.reshape(windows, -1), heads_cols], axis=1))[0]
    n_norm = 6 * channels
    group_cols = jnp.concatenate([small_out[:n_norm].reshape(6, channels), grad_section_small.T])
    group_cols = jnp.swapaxes(group_cols.reshape(10, count, -1), 0, 1)
    norm_out = scatter_tensor(group_cols)[0]
    heads_out = small_out[n_norm:]
    return (
        section_out[None],
        grad_resid_in[None],
        encoder_grad[None],
        norm_out[0:2],
        norm_out[2:4],
        norm_out[4:6],
        attn_out[:, :keys],
        attn_out[:, keys : 2 * keys],
        attn_out[:, 2 * keys : 2 * keys + values],
        attn_out[:, 2 * keys + values :].T,
        ffn_out[:, :hidden_count],
        ffn_out[:, hidden_count:].T,
        heads_out[:n_position].reshape(position_weight.shape),
        heads_out[n_position : n_position + n_bias].reshape(content_bias.shape),
        heads_out[n_position + n_bias :].reshape(position_bias.shape),
        upsample_cols.astype(jnp.float32).T,
        lateral_cols.astype(jnp.float32).T,
        norm_out[6:9],
        norm_out[9],
        point_out.astype(jnp.float32),
    )


def solution(mesh):
    rows = P("dp", "tensor", None)
    narrow = P(None, ("dp", "tensor"))
    split = P("dp", "tensor")
    turned = P("tensor", "dp")
    vector = P(("dp", "tensor"))
    tall = P(("dp", "tensor"), None)
    position = P("dp", None, "tensor")
    weights = (split, split, split, turned, split, turned, position, split, split)
    return jax.shard_map(
        body,
        mesh=mesh,
        in_specs=(rows, rows, P("dp"), rows, narrow, narrow, narrow)
        + weights
        + (narrow, narrow, narrow, vector, tall),
        out_specs=(rows, rows, rows, narrow, narrow, narrow)
        + weights
        + (narrow, narrow, narrow, vector, tall),
        check_vma=False,
    )
```

time: 1550 us -> 588 us (0.38)
  waiting for transfers between devices: 916 us -> 223 us
  blocking collectives: 443 us -> 138 us
  starting transfers between devices: 5.66 us -> 55.7 us
  matrix products: 86.2 us -> 57 us
    reduce_scatter x13 -> x6, waiting for transfers between devices: 770 us -> 73.1 us  [the longest x3 73.1 us: scatter_dp(): return lax.psum_scatter(whole, 'dp', scatter_dimension=0, tiled=True)]
    all_gather x13 -> x4, blocking collectives: 378 us -> 68.9 us  [the longest x1 20.5 us: body(): lax.all_gather(small, 'tensor', axis=0)]
    all_gather x7 -> x5, waiting for transfers between devices: 114 us -> 0.08 us  [gather_dp(): return lax.all_gather(shard, 'dp', axis=axis, tiled=True)]
    ppermute x2 -> x28, waiting for transfers between devices: 4.23 us -> 111 us  [the longest x24 107 us: from_ahead(): lax.ppermute(rows, 'tensor', [((i + step) % count, i) for i in range(coun...]
    ppermute x2 -> x28, starting transfers between devices: 4.53 us -> 54.8 us  [the longest x24 44.6 us: from_ahead(): lax.ppermute(rows, 'tensor', [((i + step) % count, i) for i in range(coun...]
    unnamed x22 -> x15, waiting for transfers between devices: 28.2 us -> 38.9 us
    unnamed x2 -> x3, blocking collectives: 65.2 us -> 69.1 us
  transfers between devices with their start and end apart: 23 -> 41, of which waited for: 18 -> 21; matrix products, arithmetic and copies ran while one was open for 5% -> 23% of each run, Pallas kernels for 0% -> 0%
where the time goes in v1:
time: 588 us; the launch traced here: 578 us
  waiting for transfers between devices  223 us (38%)
  blocking collectives  138 us (23%)
  matrix products  57 us (10%)
  local copies, waits for them, and re-layouts  55.9 us (10%)
  starting transfers between devices  55.7 us (9%)
  other arithmetic  30.1 us (5%)
  between operations  17.8 us (3%)
    ppermute x24, waiting for transfers between devices, from_ahead(): lax.ppermute(rows, 'tensor', [((i + step) % count, i) for i in range(coun...  107 us
    reduce_scatter x3, waiting for transfers between devices, scatter_dp(): return lax.psum_scatter(whole, 'dp', scatter_dimension=0, tiled=True)  73.1 us
    unnamed x3, blocking collectives  69.1 us
    ppermute x24, starting transfers between devices, from_ahead(): lax.ppermute(rows, 'tensor', [((i + step) % count, i) for i in range(coun...  44.6 us
    unnamed x15, waiting for transfers between devices  38.9 us
    unnamed x239, local copies, waits for them, and re-layouts  29.2 us
    dot_general x10, matrix products, dot_plain(): return jnp.dot(left_side, right_side, preferred_element_type=jnp.float32)  23.3 us
    all_gather x1, blocking collectives, body(): lax.all_gather(small, 'tensor', axis=0)  20.5 us
  transfers between devices with their start and end apart: 41, of which 21 were waited for; matrix products, arithmetic and copies ran while one was open for 23% of the time, Pallas kernels for 0%

profile of v1, /device:TPU:0, one launch (start us, length us, event | category | flops | bytes accessed | tf_op | source)
XLA Modules:
  0.0 577.6 jit_solution(17167240754024267285)
XLA Ops:
  19.7 20.5 %all-gather.4 = bf16[4,10,48]{2,1,0:T(8,128)(2,1)S(1)} all-gather(bf16[1,10,48]{2,1,0:T(8,128)(2,1)S(1)} %bitcast.226), channel_id=2, replica_groups=mesh['dp'=8,'tensor'=4] {'tensor'}, dimensions={0}, use_global_device_ids=true | all-gather | bytes 4800 | tf_op jit(solution)/shard_map/all_gather | solution.py:167
  42.2 22.7 %all-reduce.2 = bf16[13568]{0:T(1024)(128)(2,1)S(1)} all-reduce(bf16[13568]{0:T(1024)(128)(2,1)S(1)} %dynamic-update-slice), channel_id=3, replica_groups=mesh['dp'=8,'tensor'=4] {'dp'}, use_global_device_ids=true, to_apply=%add.2 | all-reduce | flops 13568 | bytes 54272
  92.7 5.3 collective-permute-done.3
  98.0 8.4 %collective-permute-done.4 = bf16[64,1536]{1,0:T(8,128)(2,1)S(1)} collective-permute-done((bf16[64,1536]{1,0:T(8,128)(2,1)S(1)}, bf16[64,1536]{1,0:T(8,128)(2,1)S(1)}, u32[]{:S(2)}, u32[]{:S(2)}) %collective-permute-start.4) | collective-permute-done | bytes 196640 | tf_op jit(solution)/shard_map/ppermute | solution.py:79
  111.8 5.9 %collective-permute-done.8 = bf16[64,1536]{1,0:T(8,128)(2,1)S(1)} collective-permute-done((bf16[64,1536]{1,0:T(8,128)(2,1)S(1)}, bf16[64,1536]{1,0:T(8,128)(2,1)S(1)}, u32[]{:S(2)}, u32[]{:S(2)}) %collective-permute-start.8) | collective-permute-done | bytes 196640 | tf_op jit(solution)/shard_map/ppermute | solution.py:79
  117.7 5.9 %collective-permute-done.7 = bf16[64,1536]{1,0:T(8,128)(2,1)S(1)} collective-permute-done((bf16[64,1536]{1,0:T(8,128)(2,1)S(1)}, bf16[64,1536]{1,0:T(8,128)(2,1)S(1)}, u32[]{:S(2)}, u32[]{:S(2)}) %collective-permute-start.7) | collective-permute-done | bytes 196640 | tf_op jit(solution)/shard_map/ppermute | solution.py:79
  142.9 6.8 %collective-permute-done.10 = bf16[64,1536]{1,0:T(8,128)(2,1)S(1)} collective-permute-done((bf16[64,1536]{1,0:T(8,128)(2,1)S(1)}, bf16[64,1536]{1,0:T(8,128)(2,1)S(1)}, u32[]{:S(2)}, u32[]{:S(2)}) %collective-permute-start.10) | collective-permute-done | bytes 196640 | tf_op jit(solution)/shard_map/ppermute | solution.py:79
  151.0 16.6 %all_gather.39 = bf16[192,1536]{1,0:T(8,128)(2,1)S(1)} all-gather(bf16[48,1536]{1,0:T(8,128)(2,1)S(1)} %bitcast.219), channel_id=1, replica_groups=mesh['dp'=8,'tensor'=4] {'tensor'}, dimensions={0}, use_global_device_ids=true | all-gather | bytes 737280 | tf_op jit(solution)/shard_map/all_gather | solution.py:187
  167.5 16.3 %all_gather.41 = bf16[192,1536]{1,0:T(8,128)(2,1)S(1)} all-gather(bf16[48,1536]{1,0:T(8,128)(2,1)S(1)} %bitcast.220), channel_id=1, replica_groups=mesh['dp'=8,'tensor'=4] {'tensor'}, dimensions={0}, use_global_device_ids=true | all-gather | bytes 737280 | tf_op jit(solution)/shard_map/all_gather | solution.py:188
  183.8 15.5 %all_gather.42 = bf16[192,1536]{1,0:T(8,128)(2,1)S(1)} all-gather(bf16[48,1536]{1,0:T(8,128)(2,1)S(1)} %copy-done.52), channel_id=1, replica_groups=mesh['dp'=8,'tensor'=4] {'tensor'}, dimensions={0}, use_global_device_ids=true | all-gather | bytes 737280 | tf_op jit(solution)/shard_map/all_gather | solution.py:186
  244.4 26.2 %reduce-scatter.16.cloned.1.call-done = bf16[64,1536]{1,0:T(8,128)(2,1)} async-done(((bf16[512,1536]{1,0:T(8,128)(2,1)}), bf16[64,1536]{1,0:T(8,128)(2,1)}) %reduce-scatter.16.cloned.1.call-update) | async-done | bytes 196624 | tf_op jit(solution)/shard_map/reduce_scatter | solution.py:109
  277.0 15.8 %collective-permute-done.16 = bf16[64,1536]{1,0:T(8,128)(2,1)S(1)} collective-permute-done((bf16[64,1536]{1,0:T(8,128)(2,1)}, bf16[64,1536]{1,0:T(8,128)(2,1)S(1)}, u32[]{:S(2)}, u32[]{:S(2)}) %collective-permute-start.16) | collective-permute-done | bytes 196640 | tf_op jit(solution)/shard_map/ppermute | solution.py:79
  299.0 8.9 %collective-permute-start.19 = (bf16[64,1536]{1,0:T(8,128)(2,1)S(1)}, bf16[64,1536]{1,0:T(8,128)(2,1)S(1)}, u32[]{:S(2)}, u32[]{:S(2)}) collective-permute-start(bf16[64,1536]{1,0:T(8,128)(2,1)S(1)} %get-tuple-element.143), channel_id=1, source_target_pairs={{3,0},{0,1},{1,2},{2,3},{7,4},{4,5},{5,6},{6,7},{11,8},{8,9},{9,10... | collective-permute-start | bytes 589832 | tf_op jit(solution)/shard_map/ppermute | solution.py:79
  309.6 7.2 %collective-permute-done.19 = bf16[64,1536]{1,0:T(8,128)(2,1)S(1)} collective-permute-done((bf16[64,1536]{1,0:T(8,128)(2,1)S(1)}, bf16[64,1536]{1,0:T(8,128)(2,1)S(1)}, u32[]{:S(2)}, u32[]{:S(2)}) %collective-permute-start.19) | collective-permute-done | bytes 196640 | tf_op jit(solution)/shard_map/ppermute | solution.py:79
  316.7 8.4 %collective-permute-done.21 = bf16[64,1536]{1,0:T(8,128)(2,1)S(1)} collective-permute-done((bf16[64,1536]{1,0:T(8,128)(2,1)S(1)}, bf16[64,1536]{1,0:T(8,128)(2,1)S(1)}, u32[]{:S(2)}, u32[]{:S(2)}) %collective-permute-start.21) | collective-permute-done | bytes 196640 | tf_op jit(solution)/shard_map/ppermute | solution.py:79
  325.2 8.8 %collective-permute-done.20 = bf16[64,1536]{1,0:T(8,128)(2,1)S(1)} collective-permute-done((bf16[64,1536]{1,0:T(8,128)(2,1)S(1)}, bf16[64,1536]{1,0:T(8,128)(2,1)S(1)}, u32[]{:S(2)}, u32[]{:S(2)}) %collective-permute-start.20) | collective-permute-done | bytes 196640 | tf_op jit(solution)/shard_map/ppermute | solution.py:79
  339.9 5.5 collective-permute-done.24
  345.5 12.8 %collective-permute-done.23 = bf16[64,1536]{1,0:T(8,128)(2,1)S(1)} collective-permute-done((bf16[64,1536]{1,0:T(8,128)(2,1)S(1)}, bf16[64,1536]{1,0:T(8,128)(2,1)S(1)}, u32[]{:S(2)}, u32[]{:S(2)}) %collective-permute-start.23) | collective-permute-done | bytes 196640 | tf_op jit(solution)/shard_map/ppermute | solution.py:79
  380.1 6.6 %copy.180 = bf16[1536,1536]{1,0:T(8,128)(2,1)} copy(bf16[1536,1536]{0,1:T(8,128)(2,1)} %pad_maximum_fusion) | data formatting | bytes 9437184
  406.6 22.9 %all-reduce.3 = f32[8,1696]{1,0:T(8,128)S(1)} all-reduce(f32[8,1696]{1,0:T(8,128)S(1)} %concatenate.89), channel_id=9, replica_groups=mesh['dp'=8,'tensor'=4] {'dp'}, use_global_device_ids=true, to_apply=%region_26.29.clone | all-reduce | flops 13568 | bytes 108544
  431.8 23.4 %all-reduce.4 = f32[4,10,48]{2,0,1:T(4,128)S(1)} all-reduce(f32[4,10,48]{2,0,1:T(4,128)S(1)} %maximum_bitcast_fusion), channel_id=10, replica_groups=mesh['dp'=8,'tensor'=4] {'tensor'}, use_global_device_ids=true, to_apply=%region_31.34.clone | all-reduce | flops 1920 | bytes 15360
  467.3 6.0 %collective-permute-done.26 = bf16[64,1536]{1,0:T(8,128)(2,1)S(1)} collective-permute-done((bf16[64,1536]{1,0:T(8,128)(2,1)S(1)}, bf16[64,1536]{1,0:T(8,128)(2,1)S(1)}, u32[]{:S(2)}, u32[]{:S(2)}) %collective-permute-start.26) | collective-permute-done | bytes 196640 | tf_op jit(solution)/shard_map/ppermute | solution.py:79
  482.1 38.0 %reduce-scatter.28.cloned.1.call-done = bf16[192,1536]{1,0:T(8,128)(2,1)} async-done(((bf16[1536,1536]{1,0:T(8,128)(2,1)}), bf16[192,1536]{1,0:T(8,128)(2,1)}) %reduce-scatter.28.cloned.1.call-update) | async-done | bytes 589840
  523.8 46.9 %reduce-scatter.14.cloned.1.call-done = bf16[128,1536]{1,0:T(8,128)(2,1)} async-done(((bf16[1024,1536]{1,0:T(8,128)(2,1)}), bf16[128,1536]{1,0:T(8,128)(2,1)}) %reduce-scatter.14.cloned.1.call-update) | async-done | bytes 393232 | tf_op jit(solution)/shard_map/reduce_scatter | solution.py:109
  (504 shorter events, 198.6 us)
Async XLA Ops:
  7.2 64.2 %all-gather.11.cloned.1.call-start = ((), (), s32[]{:S(2)}) async-start(), calls=%async_computation.8 | async-start | bytes 3538944 | tf_op jit(solution)/shard_map/all_gather | solution.py:105
  9.2 114.5 %all-gather.13.cloned.1.call-start = ((), (), s32[]{:S(2)}) async-start(), calls=%async_computation.9 | async-start | bytes 5308416 | tf_op jit(solution)/shard_map/all_gather | solution.py:105
  11.1 188.2 %all-gather.19.cloned.1.call-start = ((), (), s32[]{:S(2)}) async-start(), calls=%async_computation.18 | async-start | bytes 3538944 | tf_op jit(solution)/shard_map/all_gather | solution.py:105
  11.9 195.8 %all-gather.17.cloned.1.call-start = ((), (), s32[]{:S(2)}) async-start(), calls=%async_computation.17 | async-start | bytes 3538944 | tf_op jit(solution)/shard_map/all_gather | solution.py:105
  11.9 57.0 %collective-permute-start.2 = (bf16[64,1536]{1,0:T(8,128)(2,1)S(1)}, bf16[64,1536]{1,0:T(8,128)(2,1)S(1)}, u32[]{:S(2)}, u32[]{:S(2)}) collective-permute-start(bf16[64,1536]{1,0:T(8,128)(2,1)S(1)} %bitcast.185), channel_id=1, source_target_pairs={{3,0},{0,1},{1,2},{2,3},{7,4},{4,5},{5,6},{6,7},{11,8},{8,9},{9,10... | collective-permute-start | bytes 589832 | tf_op jit(solution)/shard_map/ppermute | solution.py:79
  15.0 54.0 %collective-permute-start.1 = (bf16[64,1536]{1,0:T(8,128)(2,1)S(1)}, bf16[64,1536]{1,0:T(8,128)(2,1)S(1)}, u32[]{:S(2)}, u32[]{:S(2)}) collective-permute-start(bf16[64,1536]{1,0:T(8,128)(2,1)S(1)} %bitcast.186), channel_id=1, source_target_pairs={{2,0},{3,1},{0,2},{1,3},{6,4},{7,5},{4,6},{5,7},{10,8},{11,9},{8,1... | collective-permute-start | bytes 589832 | tf_op jit(solution)/shard_map/ppermute | solution.py:79
  17.6 51.4 %collective-permute-start = (bf16[64,1536]{1,0:T(8,128)(2,1)S(1)}, bf16[64,1536]{1,0:T(8,128)(2,1)S(1)}, u32[]{:S(2)}, u32[]{:S(2)}) collective-permute-start(bf16[64,1536]{1,0:T(8,128)(2,1)S(1)} %bitcast.187), channel_id=1, source_target_pairs={{1,0},{2,1},{3,2},{0,3},{5,4},{6,5},{7,6},{4,7},{9,8},{10,9},{11,1... | collective-permute-start | bytes 589832 | tf_op jit(solution)/shard_map/ppermute | solution.py:79
  19.0 192.4 %all-gather.15.cloned.1.call-start = ((), (), s32[]{:S(2)}) async-start(), calls=%async_computation.10 | async-start | bytes 1769472 | tf_op jit(solution)/shard_map/all_gather | solution.py:105
  150.5 120.1 %reduce-scatter.16.cloned.1.call-start = ((), (), s32[]{:S(2)}) async-start(), calls=%async_computation.12 | async-start | bytes 1769472 | tf_op jit(solution)/shard_map/reduce_scatter | solution.py:109
  230.2 161.3 %reduce-scatter.24.cloned.1.call-start = ((), (), s32[]{:S(2)}) async-start(), calls=%async_computation.16 | async-start | bytes 737280 | tf_op jit(solution)/shard_map/reduce_scatter | solution.py:113
  234.5 158.8 %reduce-scatter.22.cloned.1.call-start = ((), (), s32[]{:S(2)}) async-start(), calls=%async_computation.15 | async-start | bytes 737280 | tf_op jit(solution)/shard_map/reduce_scatter | solution.py:113
  238.6 156.3 %reduce-scatter.20.cloned.1.call-start = ((), (), s32[]{:S(2)}) async-start(), calls=%async_computation.14 | async-start | bytes 737280 | tf_op jit(solution)/shard_map/reduce_scatter | solution.py:113
  241.6 233.9 %reduce-scatter.18.cloned.1.call-start = ((), (), s32[]{:S(2)}) async-start(), calls=%async_computation.13 | async-start | bytes 3538944 | tf_op jit(solution)/shard_map/reduce_scatter | solution.py:109
  244.3 233.2 %reduce-scatter.26.cloned.1.call-start = ((), (), s32[]{:S(2)}) async-start(), calls=%async_computation.19 | async-start | bytes 3538944
  270.6 22.3 %collective-permute-start.18 = (bf16[64,1536]{1,0:T(8,128)(2,1)}, bf16[64,1536]{1,0:T(8,128)(2,1)S(1)}, u32[]{:S(2)}, u32[]{:S(2)}) collective-permute-start(bf16[64,1536]{1,0:T(8,128)(2,1)} %reduce-scatter.16.cloned.1.call-done), channel_id=1, source_target_pairs={{3,0},{0,1},{1,2},{2,3},{7,4},{4,5},{5,6},{6,7},{11,8},{8,9},{9,10... | collective-permute-start | bytes 589832 | tf_op jit(solution)/shard_map/ppermute | solution.py:79
  272.1 20.8 %collective-permute-start.17 = (bf16[64,1536]{1,0:T(8,128)(2,1)}, bf16[64,1536]{1,0:T(8,128)(2,1)S(1)}, u32[]{:S(2)}, u32[]{:S(2)}) collective-permute-start(bf16[64,1536]{1,0:T(8,128)(2,1)} %reduce-scatter.16.cloned.1.call-done), channel_id=1, source_target_pairs={{2,0},{3,1},{0,2},{1,3},{6,4},{7,5},{4,6},{5,7},{10,8},{11,9},{8,1... | collective-permute-start | bytes 589832 | tf_op jit(solution)/shard_map/ppermute | solution.py:79
  274.5 18.3 %collective-permute-start.16 = (bf16[64,1536]{1,0:T(8,128)(2,1)}, bf16[64,1536]{1,0:T(8,128)(2,1)S(1)}, u32[]{:S(2)}, u32[]{:S(2)}) collective-permute-start(bf16[64,1536]{1,0:T(8,128)(2,1)} %reduce-scatter.16.cloned.1.call-done), channel_id=1, source_target_pairs={{1,0},{2,1},{3,2},{0,3},{5,4},{6,5},{7,6},{4,7},{9,8},{10,9},{11,1... | collective-permute-start | bytes 589832 | tf_op jit(solution)/shard_map/ppermute | solution.py:79
  299.0 17.8 %collective-permute-start.19 = (bf16[64,1536]{1,0:T(8,128)(2,1)S(1)}, bf16[64,1536]{1,0:T(8,128)(2,1)S(1)}, u32[]{:S(2)}, u32[]{:S(2)}) collective-permute-start(bf16[64,1536]{1,0:T(8,128)(2,1)S(1)} %get-tuple-element.143), channel_id=1, source_target_pairs={{3,0},{0,1},{1,2},{2,3},{7,4},{4,5},{5,6},{6,7},{11,8},{8,9},{9,10... | collective-permute-start | bytes 589832 | tf_op jit(solution)/shard_map/ppermute | solution.py:79
  307.9 17.3 %collective-permute-start.21 = (bf16[64,1536]{1,0:T(8,128)(2,1)S(1)}, bf16[64,1536]{1,0:T(8,128)(2,1)S(1)}, u32[]{:S(2)}, u32[]{:S(2)}) collective-permute-start(bf16[64,1536]{1,0:T(8,128)(2,1)S(1)} %get-tuple-element.144), channel_id=1, source_target_pairs={{1,0},{2,1},{3,2},{0,3},{5,4},{6,5},{7,6},{4,7},{9,8},{10,9},{11,1... | collective-permute-start | bytes 589832 | tf_op jit(solution)/shard_map/ppermute | solution.py:79
  309.1 24.9 %collective-permute-start.20 = (bf16[64,1536]{1,0:T(8,128)(2,1)S(1)}, bf16[64,1536]{1,0:T(8,128)(2,1)S(1)}, u32[]{:S(2)}, u32[]{:S(2)}) collective-permute-start(bf16[64,1536]{1,0:T(8,128)(2,1)S(1)} %get-tuple-element.145), channel_id=1, source_target_pairs={{2,0},{3,1},{0,2},{1,3},{6,4},{7,5},{4,6},{5,7},{10,8},{11,9},{8,1... | collective-permute-start | bytes 589832 | tf_op jit(solution)/shard_map/ppermute | solution.py:79
  336.4 21.9 %collective-permute-start.23 = (bf16[64,1536]{1,0:T(8,128)(2,1)S(1)}, bf16[64,1536]{1,0:T(8,128)(2,1)S(1)}, u32[]{:S(2)}, u32[]{:S(2)}) collective-permute-start(bf16[64,1536]{1,0:T(8,128)(2,1)S(1)} %convert_element_type.319), channel_id=1, source_target_pairs={{2,0},{3,1},{0,2},{1,3},{6,4},{7,5},{4,6},{5,7},{10,8},{11,9},{8,1... | collective-permute-start | bytes 589832 | tf_op jit(solution)/shard_map/ppermute | solution.py:79
  339.7 18.5 %collective-permute-start.22 = (bf16[64,1536]{1,0:T(8,128)(2,1)S(1)}, bf16[64,1536]{1,0:T(8,128)(2,1)S(1)}, u32[]{:S(2)}, u32[]{:S(2)}) collective-permute-start(bf16[64,1536]{1,0:T(8,128)(2,1)S(1)} %convert_element_type.319), channel_id=1, source_target_pairs={{1,0},{2,1},{3,2},{0,3},{5,4},{6,5},{7,6},{4,7},{9,8},{10,9},{11,1... | collective-permute-start | bytes 589832 | tf_op jit(solution)/shard_map/ppermute | solution.py:79
  374.3 145.8 %reduce-scatter.28.cloned.1.call-start = ((), (), s32[]{:S(2)}) async-start(), calls=%async_computation.20 | async-start | bytes 5308416
  386.8 183.9 %reduce-scatter.14.cloned.1.call-start = ((), (), s32[]{:S(2)}) async-start(), calls=%async_computation.11 | async-start | bytes 3538944 | tf_op jit(solution)/shard_map/reduce_scatter | solution.py:109
  (122 other events, 1224.3 us)
Sparse Core Ops, SparseCore 0:
  10.5 35.0 all-gather.10
  48.0 38.9 all-gather.12
  88.9 32.3 all-gather.18
  123.0 32.3 all-gather.16
  157.6 25.6 all-gather.14
  230.3 40.2 reduce-scatter.15
  272.9 28.0 reduce-scatter.23
  303.2 28.0 reduce-scatter.21
  334.2 30.1 reduce-scatter.19
  367.6 45.2 reduce-scatter.17
  416.6 46.1 reduce-scatter.25
  466.2 53.8 reduce-scatter.27
  524.4 46.2 reduce-scatter.13

commit v2 on v1

v2 whole, which is shorter than its diff:
```python
import math

import jax
import jax.numpy as jnp
from jax import lax
from jax.experimental import pallas as pl
from jax.experimental.pallas import tpu as pltpu
from jax.sharding import PartitionSpec as P

KEYD = 64
VALD = 192
BASIS = 32
SPECIES = 2
SCALE = 1.0 / math.sqrt(KEYD)
LOW = jnp.bfloat16


def dot_plain(left_side, right_side):
    return jnp.dot(left_side, right_side, preferred_element_type=jnp.float32)


def dot_transposed(left_side, right_side):
    return lax.dot_general(
        left_side, right_side, (((1,), (1,)), ((), ())), preferred_element_type=jnp.float32
    )


def dot_leading(left_side, right_side):
    return lax.dot_general(
        left_side, right_side, (((0,), (0,)), ((), ())), preferred_element_type=jnp.float32
    )


def exact_gelu(values):
    return jax.nn.gelu(values, approximate=False)


def normalize(values):
    centred = values - jnp.mean(values, axis=-1, keepdims=True)
    variance = jnp.mean(centred * centred, axis=-1, keepdims=True)
    scale = lax.rsqrt(variance + 1e-05)
    return centred * scale, scale


def normalize_back(unit, scale, grad_unit):
    return scale * (
        grad_unit
        - jnp.mean(grad_unit, axis=-1, keepdims=True)
        - unit * jnp.mean(grad_unit * unit, axis=-1, keepdims=True)
    )


def basis_table(length, features):
    distance = jnp.arange(2 * length - 1).astype(jnp.float32) - (length - 1)
    halves = features // 2
    fraction = jnp.arange(halves).astype(jnp.float32) / (halves - 1)
    lifetimes = 3.0 * jnp.power(length / 3.0, fraction)
    decays = jnp.exp(-0.6931471805599453 * jnp.abs(distance)[:, None] / lifetimes[None, :])
    return jnp.concatenate([decays, jnp.sign(distance)[:, None] * decays], axis=1)


def dot_rows(left_side, right_side):
    return jnp.dot(left_side, right_side, preferred_element_type=jnp.float32)


def run_kernel(kernel, ins, outs, scalars=None, scratch=(), flops=0, name=None):
    whole = pl.BlockSpec(memory_space=pltpu.VMEM)
    specs = [whole] * len(ins)
    args = list(ins)
    if scalars is not None:
        specs = [pl.BlockSpec(memory_space=pltpu.SMEM)] + specs
        args = [scalars] + args
    shapes = [jax.ShapeDtypeStruct(shape, dtype) for shape, dtype in outs]
    moved = sum(x.size * x.dtype.itemsize for x in list(ins) + shapes)
    return pl.pallas_call(
        kernel,
        in_specs=specs,
        out_specs=[whole] * len(shapes),
        out_shape=shapes,
        scratch_shapes=scratch,
        compiler_params=pltpu.CompilerParams(vmem_limit_bytes=50 * 1024 * 1024),
        cost_estimate=pl.CostEstimate(flops=flops, bytes_accessed=moved, transcendentals=0),
        name=name,
    )(*args)


def lanes_of(head, width, shape):
    lane = lax.broadcasted_iota(jnp.int32, shape, len(shape) - 1)
    return (lane >= head * width) & (lane < (head + 1) * width)


def chunk_of(where_ref, step, count):
    return lax.rem(where_ref[1] + step, count)


def attention_forward(where, raw, row_params, rel_turned, blocks, local_heads):
    count, (own, width) = len(raw), raw[0].shape
    length = count * own
    rows, columns = blocks[0].shape
    keys, values = local_heads * KEYD, local_heads * VALD
    n_blocks = len(blocks)

    def kernel(where_ref, *refs):
        raw_refs, refs = refs[:count], refs[count:]
        species_ref, gain_ref, shift_ref, content_ref, position_ref, rel_ref = refs[:6]
        block_refs, refs = refs[6 : 6 + n_blocks], refs[6 + n_blocks :]
        own_ref, refs = refs[0], refs[1:]
        part_refs, refs = refs[: count - 1], refs[count - 1 :]
        (weight_ref, normed_ref, unit_ref, scale_ref, probs_ref, content_out, position_out) = refs[:7]
        key_out, value_out, mixed_out, total_ref = refs[7:]
        for m in range(n_blocks):
            spot = (where_ref[0] ^ m) * rows if n_blocks > 1 else 0
            weight_ref[pl.ds(pl.multiple_of(spot, rows), rows), :] = block_refs[m][...]
        for k in range(count):
            resid = raw_refs[k][...].astype(jnp.float32) + species_ref[...]
            unit, scale = normalize(resid)
            spot = pl.ds(pl.multiple_of(chunk_of(where_ref, k, count) * own, own), own)
            unit_ref[spot, :] = unit
            scale_ref[spot, :] = jnp.broadcast_to(scale, (own, 128))
            normed_ref[spot, :] = (unit * gain_ref[...] + shift_ref[...]).astype(LOW)
        normed = normed_ref[...]
        query = dot_rows(normed, weight_ref[:, :keys])
        content = (query + content_ref[...]).astype(LOW)
        position = (query + position_ref[...]).astype(LOW)
        key_low = dot_rows(normed, weight_ref[:, keys : 2 * keys]).astype(LOW)
        value_low = dot_rows(normed, weight_ref[:, 2 * keys : 2 * keys + values]).astype(LOW)
        content_out[...] = content
        position_out[...] = position
        key_out[...] = key_low
        value_out[...] = value_low
        mixed = jnp.zeros((length, values), jnp.float32)
        for h in range(local_heads):
            mine = lanes_of(h, KEYD, (length, keys))
            zero = jnp.zeros((), LOW)
            banded = dot_transposed(jnp.where(mine, position, zero), rel_ref[...])
            skewed = pltpu.roll(banded, length + 1, 1, stride=1, stride_axis=0)[:, :length]
            scores = (dot_transposed(jnp.where(mine, content, zero), key_low) + skewed) * SCALE
            exponent = jnp.exp(scores - jnp.max(scores, axis=-1, keepdims=True))
            probs = exponent / jnp.sum(exponent, axis=-1, keepdims=True)
            probs_ref[h] = probs
            mixed = jnp.where(
                lanes_of(h, VALD, (length, values)), dot_rows(probs.astype(LOW), value_low), mixed
            )
        mixed_out[...] = mixed.astype(LOW)
        total_ref[...] = dot_transposed(mixed.astype(LOW), weight_ref[:, 2 * keys + values :])
        for k in range(count):
            spot = pl.ds(pl.multiple_of(chunk_of(where_ref, k, count) * own, own), own)
            if k == 0:
                own_ref[...] = total_ref[spot, :]
            else:
                part_refs[k - 1][...] = total_ref[spot, :].astype(LOW)

    outs = (
        [((own, width), jnp.float32)]
        + [((own, width), LOW)] * (count - 1)
        + [
            ((width, columns), LOW),
            ((length, width), LOW),
            ((length, width), jnp.float32),
            ((length, 128), jnp.float32),
            ((local_heads, length, length), jnp.float32),
            ((length, keys), LOW),
            ((length, keys), LOW),
            ((length, keys), LOW),
            ((length, values), LOW),
            ((length, values), LOW),
        ]
    )
    found = run_kernel(
        kernel,
        list(raw) + list(row_params) + [rel_turned] + list(blocks),
        outs,
        scalars=where,
        scratch=[pltpu.VMEM((length, width), jnp.float32)],
        flops=2 * length * width * columns,
        name="attention_forward",
    )
    return found[:count], found[count:]


def attention_backward(where, grads, saved, rel_turned, basis_turned, local_heads):
    count, (own, width) = len(grads), grads[0].shape
    length = count * own
    weight, _, _, _, probs_all, content_all, position_all, key_all, value_all, _ = saved
    keys, values = local_heads * KEYD, local_heads * VALD
    narrow = 2 * keys + values

    def kernel(where_ref, *refs):
        grad_refs, refs = refs[:count], refs[count:]
        weight_ref, probs_ref, content_ref, position_ref, key_ref, value_ref = refs[:6]
        rel_ref, basis_ref = refs[6:8]
        own_ref, refs = refs[8], refs[9:]
        part_refs, refs = refs[: count - 1], refs[count - 1 :]
        attn_ref, heads_ref, total_ref, bias_ref, weight_out = refs
        for k in range(count):
            spot = pl.ds(pl.multiple_of(chunk_of(where_ref, k, count) * own, own), own)
            attn_ref[spot, :] = grad_refs[k][...]
        grad_mixed = dot_rows(attn_ref[...], weight_ref[:, narrow:]).astype(LOW)
        content, position = content_ref[...], position_ref[...]
        key_low, value_low = key_ref[...], value_ref[...]
        grad_content = jnp.zeros((length, keys), jnp.float32)
        grad_position = jnp.zeros((length, keys), jnp.float32)
        grad_key = jnp.zeros((length, keys), jnp.float32)
        grad_rel = jnp.zeros((2 * length, keys), jnp.float32)
        grad_value = jnp.zeros((length, values), jnp.float32)
        back = lax.broadcasted_iota(jnp.int32, (length, 2 * length), 0)
        for h in range(local_heads):
            mine = lanes_of(h, KEYD, (length, keys))
            ours = lanes_of(h, VALD, (length, values))
            probs = probs_ref[h]
            grad_probs = dot_transposed(
                jnp.where(ours, grad_mixed, jnp.zeros((), LOW)), value_low
            )
            centre = jnp.sum(probs * grad_probs, axis=-1, keepdims=True)
            grad_scores = (probs * (grad_probs - centre)).astype(LOW)
            grad_value = jnp.where(ours, dot_leading(probs.astype(LOW), grad_mixed), grad_value)
            grad_key = jnp.where(mine, dot_leading(grad_scores, content), grad_key)
            grad_content = jnp.where(mine, dot_rows(grad_scores, key_low), grad_content)
            band = jnp.concatenate(
                [grad_scores.astype(jnp.float32), jnp.zeros((length, length), jnp.float32)], axis=1
            )
            bit = 1
            while bit < length:
                turn = (length - 1 - back) & bit
                band = jnp.where(turn > 0, pltpu.roll(band, bit, 1), band)
                bit *= 2
            band = band.astype(LOW)
            grad_position = jnp.where(mine, dot_rows(band, rel_ref[...]), grad_position)
            grad_rel = jnp.where(
                lanes_of(h, KEYD, (2 * length, keys)), dot_leading(band, position), grad_rel
            )
        grad_content = grad_content * SCALE
        grad_position = grad_position * SCALE
        bias_ref[0:1, :] = jnp.sum(grad_content, axis=0, keepdims=True)
        bias_ref[1:2, :] = jnp.sum(grad_position, axis=0, keepdims=True)
        heads_ref[:, :keys] = (grad_content + grad_position).astype(LOW)
        heads_ref[:, keys : 2 * keys] = (grad_key * SCALE).astype(LOW)
        heads_ref[:, 2 * keys :] = grad_value.astype(LOW)
        weight_out[...] = dot_leading(basis_ref[...], (grad_rel * SCALE).astype(LOW))
        total_ref[...] = dot_transposed(heads_ref[...], weight_ref[:, :narrow])
        for k in range(count):
            spot = pl.ds(pl.multiple_of(chunk_of(where_ref, k, count) * own, own), own)
            if k == 0:
                own_ref[...] = total_ref[spot, :]
            else:
                part_refs[k - 1][...] = total_ref[spot, :].astype(LOW)

    outs = (
        [((own, width), jnp.float32)]
        + [((own, width), LOW)] * (count - 1)
        + [
            ((length, width), LOW),
            ((length, narrow), LOW),
            ((length, width), jnp.float32),
            ((2, keys), jnp.float32),
            ((BASIS, keys), jnp.float32),
        ]
    )
    found = run_kernel(
        kernel,
        list(grads)
        + [weight, probs_all, content_all, position_all, key_all, value_all]
        + [rel_turned, basis_turned],
        outs,
        scalars=where,
        flops=2 * length * width * (narrow + values),
        name="attention_backward",
    )
    return found[:count], found[count:]


def attention_weights(
    where, saved, grad_attn, grad_heads, grad_normed, gain, sums_two, bias_sums, rel_grad, n_blocks
):
    normed, unit_all, scale_all, mixed = saved[1], saved[2], saved[3], saved[9]
    width = normed.shape[1]
    rows = width // n_blocks
    narrow, values = grad_heads.shape[1], mixed.shape[1]
    columns = narrow + values
    keys = rel_grad.shape[1]
    spread = max(rows, keys)
    tall = 8 + -(-(2 + BASIS) // 8) * 8

    def kernel(where_ref, normed_ref, unit_ref, scale_ref, mixed_ref, attn_ref, *refs):
        heads_ref, grad_ref, gain_ref, two_ref, bias_ref, rel_ref = refs[:6]
        even_ref, odd_ref, small_even, small_odd, whole_ref, sums_ref = refs[6:]
        grad, unit = grad_ref[...], unit_ref[...]
        into = normalize_back(unit, scale_ref[:, :1], grad * gain_ref[...])
        sums_ref[0:1, :] = jnp.sum(grad * unit, axis=0, keepdims=True)
        sums_ref[1:2, :] = two_ref[0:1, :]
        sums_ref[2:3, :] = jnp.sum(grad, axis=0, keepdims=True)
        sums_ref[3:4, :] = two_ref[1:2, :]
        table = jnp.sum(into, axis=0, keepdims=True) + two_ref[2:3, :]
        for kind in range(SPECIES):
            sums_ref[4 + kind : 5 + kind, :] = jnp.where(where_ref[2] == kind, table, 0.0)
        sums = sums_ref[...]
        small_even[...] = jnp.zeros_like(small_even)
        small_odd[...] = jnp.zeros_like(small_odd)
        for m in range(n_blocks):
            spot = (where_ref[0] ^ m) if n_blocks > 1 else 0
            half = small_odd if m % 2 else small_even
            moved = pltpu.roll(sums, lax.rem(width - spot * rows, width), 1)
            half[m // 2, 0:8, :rows] = moved[:, :rows]
            turn = lax.rem(keys - spot * (KEYD // n_blocks), keys)
            half[m // 2, 8:10, :keys] = pltpu.roll(bias_ref[...], turn, 1)
            half[m // 2, 10 : 10 + BASIS, :keys] = pltpu.roll(rel_ref[...], turn, 1)
        whole_ref[:, :narrow] = dot_leading(normed_ref[...], heads_ref[...]).astype(LOW)
        whole_ref[:, narrow:] = dot_leading(attn_ref[...], mixed_ref[...]).astype(LOW)
        for m in range(n_blocks):
            spot = (where_ref[0] ^ m) * rows if n_blocks > 1 else 0
            half = odd_ref if m % 2 else even_ref
            half[m // 2] = whole_ref[pl.ds(pl.multiple_of(spot, rows), rows), :]

    half = max(n_blocks // 2, 1)
    return run_kernel(
        kernel,
        [normed, unit_all, scale_all, mixed, grad_attn, grad_heads, grad_normed, gain]
        + [sums_two, bias_sums, rel_grad],
        [((half, rows, columns), LOW)] * 2 + [((half, tall, spread), jnp.float32)] * 2,
        scalars=where,
        scratch=[pltpu.VMEM((width, columns), LOW), pltpu.VMEM((8, width), jnp.float32)],
        flops=2 * normed.shape[0] * width * columns,
        name="attention_weights",
    )


def unpack_small(where, blocks, basis_turned, width, local_heads):
    count, entries = blocks[0].shape
    n_blocks = len(blocks)
    total = n_blocks * count
    share = width // total
    n_rows = 8 + SPECIES
    group = width // n_blocks
    keys = local_heads * KEYD
    piece = keys // n_blocks
    part = KEYD // n_blocks
    length = basis_turned.shape[0]

    def kernel(where_ref, *refs):
        block_refs, basis_ref, refs = refs[:n_blocks], refs[n_blocks], refs[n_blocks + 1 :]
        row_refs, refs = refs[:5], refs[5:]
        taps_ref, bias_ref, rel_ref, content_ref, position_ref, found_ref, weight_ref = refs
        for m in range(n_blocks):
            found_ref[m * count : (m + 1) * count, :] = block_refs[m][...].astype(jnp.float32)

        def owner(shape):
            spot = lax.broadcasted_iota(jnp.int32, shape, 0)
            return (spot // count) ^ where_ref[0], lax.rem(spot % count + where_ref[1], count)

        def widen(start, size, span):
            column = lax.broadcasted_iota(jnp.int32, (size, span), 1)
            inner = lax.broadcasted_iota(jnp.int32, (size, span), 0)
            if size == share:
                chosen = column % share == inner
            else:
                chosen = (column // KEYD == inner // part) & (column % part == inner % part)
            return dot_rows(
                found_ref[:, start : start + size].astype(LOW),
                chosen.astype(jnp.float32).astype(LOW),
            )

        group_of, line_of = owner((total, width))
        column = lax.broadcasted_iota(jnp.int32, (total, width), 1) // share
        mask = group_of * count + line_of == column
        rows = [
            jnp.sum(jnp.where(mask, widen(r * share, share, width), 0.0), axis=0, keepdims=True)
            for r in range(4 + SPECIES)
        ]
        species = jnp.zeros((1, width), jnp.float32)
        for kind in range(SPECIES):
            species = jnp.where(where_ref[2] == kind, rows[4 + kind], species)
        for ref, row in zip(row_refs, rows[:4] + [species], strict=True):
            ref[...] = row
        group_of, line_of = owner((total, group))
        column = lax.broadcasted_iota(jnp.int32, (total, group), 1) // share
        mask = (group_of == where_ref[0]) & (line_of == column)
        rows = [
            jnp.sum(jnp.where(mask, widen(r * share, share, group), 0.0), axis=0, keepdims=True)
            for r in range(4 + SPECIES, n_rows)
        ]
        for r in range(3):
            taps_ref[r : r + 1, :] = rows[r]
        bias_ref[...] = rows[3]
        group_of, line_of = owner((total, keys))
        column = lax.broadcasted_iota(jnp.int32, (total, keys), 1) % KEYD // part
        mask = (line_of == where_ref[1]) & (group_of == column)
        start = n_rows * share
        for f in range(BASIS + 2):
            row = widen(start + f * piece, piece, keys)
            row = jnp.sum(jnp.where(mask, row, 0.0), axis=0, keepdims=True)
            if f < BASIS:
                weight_ref[f : f + 1, :] = row
            else:
                (content_ref if f == BASIS else position_ref)[...] = row
        rel_ref[...] = dot_rows(basis_ref[...], weight_ref[...].astype(LOW)).astype(LOW)

    found = run_kernel(
        kernel,
        list(blocks) + [basis_turned],
        [((1, width), jnp.float32)] * 5
        + [((3, group), jnp.float32), ((1, group), jnp.float32)]
        + [((length, keys), LOW)]
        + [((1, keys), jnp.float32)] * 2,
        scalars=where,
        scratch=[pltpu.VMEM((total, entries), jnp.float32), pltpu.VMEM((BASIS, keys), jnp.float32)],
        name="unpack_small",
    )
    return found[:5], found[5:]


def second_norm(own_part, parts, resid_in, gain, shift):
    own, width = own_part.shape

    def kernel(own_ref, *refs):
        part_refs, refs = refs[: len(parts)], refs[len(parts) :]
        raw_ref, species_ref, gain_ref, shift_ref, resid_ref, unit_ref, scale_ref, low_ref = refs
        total = own_ref[...]
        for ref in part_refs:
            total = total + ref[...].astype(jnp.float32)
        resid = raw_ref[...].astype(jnp.float32) + species_ref[...] + total
        unit, scale = normalize(resid)
        resid_ref[...] = resid
        unit_ref[...] = unit
        scale_ref[...] = jnp.broadcast_to(scale, (own, 128))
        low_ref[...] = (unit * gain_ref[...] + shift_ref[...]).astype(LOW)

    return run_kernel(
        kernel,
        [own_part] + list(parts) + list(resid_in) + [gain, shift],
        [
            ((own, width), jnp.float32),
            ((own, width), jnp.float32),
            ((own, 128), jnp.float32),
            ((own, width), LOW),
        ],
        name="second_norm",
    )


def second_norm_back(own_part, parts, unit, scale, gain, grad_resid):
    own, width = own_part.shape

    def kernel(own_ref, *refs):
        part_refs, refs = refs[: len(parts)], refs[len(parts) :]
        unit_ref, scale_ref, gain_ref, grad_ref, resid_ref, low_ref, sums_ref = refs
        total = own_ref[...]
        for ref in part_refs:
            total = total + ref[...].astype(jnp.float32)
        unit_rows = unit_ref[...]
        resid = grad_ref[...] + normalize_back(unit_rows, scale_ref[:, :1], total * gain_ref[...])
        resid_ref[...] = resid
        low_ref[...] = resid.astype(LOW)
        sums_ref[0:1, :] = jnp.sum(total * unit_rows, axis=0, keepdims=True)
        sums_ref[1:2, :] = jnp.sum(total, axis=0, keepdims=True)
        sums_ref[2:3, :] = jnp.sum(resid, axis=0, keepdims=True)

    return run_kernel(
        kernel,
        [own_part] + list(parts) + [unit, scale, gain, grad_resid],
        [((own, width), jnp.float32), ((own, width), LOW), ((3, width), jnp.float32)],
        name="second_norm_back",
    )


def first_norm_back(where, own_part, parts, unit_all, scale_all, gain, grad_resid):
    own, width = own_part.shape

    def kernel(where_ref, own_ref, *refs):
        part_refs, refs = refs[: len(parts)], refs[len(parts) :]
        unit_ref, scale_ref, gain_ref, grad_ref, out_ref = refs
        total = own_ref[...]
        for ref in part_refs:
            total = total + ref[...].astype(jnp.float32)
        spot = pl.ds(pl.multiple_of(where_ref[1] * own, own), own)
        out_ref[0] = grad_ref[...] + normalize_back(
            unit_ref[spot, :], scale_ref[spot, :1], total * gain_ref[...]
        )

    return run_kernel(
        kernel,
        [own_part] + list(parts) + [unit_all, scale_all, gain, grad_resid],
        [((1, own, width), jnp.float32)],
        scalars=where,
        name="first_norm_back",
    )[0]


def feed_forward_up(normed, weight):
    count, (own, width) = len(normed), normed[0].shape
    length = count * own
    hidden_count = weight.shape[1] // 2

    def kernel(*refs):
        normed_refs, weight_ref, own_ref, refs = refs[:count], refs[count], refs[count + 1], refs[count + 2 :]
        part_refs, (normed_out, hidden_out, slope_out) = refs[: count - 1], refs[count - 1 :]
        for k in range(count):
            normed_out[k * own : (k + 1) * own, :] = normed_refs[k][...]
        pre = dot_rows(normed_out[...], weight_ref[:, :hidden_count])
        below = 0.5 * (1.0 + lax.erf(pre * math.sqrt(0.5)))
        hidden_out[...] = (pre * below).astype(LOW)
        slope_out[...] = below + pre * jnp.exp(-0.5 * pre * pre) * (1.0 / math.sqrt(2.0 * math.pi))
        total = dot_transposed(hidden_out[...], weight_ref[:, hidden_count:])
        own_ref[...] = total[:own]
        for k in range(1, count):
            part_refs[k - 1][...] = total[k * own : (k + 1) * own].astype(LOW)

    found = run_kernel(
        kernel,
        list(normed) + [weight],
        [((own, width), jnp.float32)]
        + [((own, width), LOW)] * (count - 1)
        + [((length, width), LOW), ((length, hidden_count), LOW)]
        + [((length, hidden_count), jnp.float32)],
        flops=4 * length * width * hidden_count,
        name="feed_forward_up",
    )
    return found[:count], found[count:]


def feed_forward_back(grads, slope, weight):
    count, (own, width) = len(grads), grads[0].shape
    length = count * own
    hidden_count = weight.shape[1] // 2

    def kernel(*refs):
        grad_refs, (slope_ref, weight_ref, own_ref), refs = refs[:count], refs[count : count + 3], refs[count + 3 :]
        part_refs, (grad_out, pre_out) = refs[: count - 1], refs[count - 1 :]
        for k in range(count):
            grad_out[k * own : (k + 1) * own, :] = grad_refs[k][...]
        grad_hidden = dot_rows(grad_out[...], weight_ref[:, hidden_count:])
        pre_out[...] = (grad_hidden * slope_ref[...]).astype(LOW)
        total = dot_transposed(pre_out[...], weight_ref[:, :hidden_count])
        own_ref[...] = total[:own]
        for k in range(1, count):
            part_refs[k - 1][...] = total[k * own : (k + 1) * own].astype(LOW)

    found = run_kernel(
        kernel,
        list(grads) + [slope, weight],
        [((own, width), jnp.float32)]
        + [((own, width), LOW)] * (count - 1)
        + [((length, width), LOW), ((length, hidden_count), LOW)],
        flops=4 * length * width * hidden_count,
        name="feed_forward_back",
    )
    return found[:count], found[count:]


def feed_forward_weights(normed_all, grad_all, hidden, grad_pre):
    width = normed_all.shape[1]
    hidden_count = hidden.shape[1]

    def kernel(normed_ref, grad_ref, hidden_ref, pre_ref, out_ref):
        out_ref[:, :hidden_count] = dot_leading(normed_ref[...], pre_ref[...]).astype(LOW)
        out_ref[:, hidden_count:] = dot_leading(grad_ref[...], hidden_ref[...]).astype(LOW)

    return run_kernel(
        kernel,
        [normed_all, grad_all, hidden, grad_pre],
        [((width, 2 * hidden_count), LOW)],
        flops=4 * normed_all.shape[0] * width * hidden_count,
        name="feed_forward_weights",
    )[0]


def shifted(rows, first, last):
    count = rows.shape[0]
    place = lax.broadcasted_iota(jnp.int32, rows.shape, 0)
    before = jnp.where(place == 0, first, pltpu.roll(rows, 1, 0))
    after = jnp.where(place == count - 1, last, pltpu.roll(rows, count - 1, 0))
    return before, after


def group_weight(weight_ref, which, count, scratch_ref):
    share = weight_ref.shape[0] // (3 * count)
    for t in range(count):
        spot = (3 * t + which) * share
        scratch_ref[t * share : (t + 1) * share, :] = weight_ref[spot : spot + share, :]


def section_grad_deep(blocks, weight, count):
    fine, width = blocks[0].shape
    channels = weight.shape[0] // 3
    windows = len(blocks)

    def kernel(*refs):
        block_refs, refs = refs[:windows], refs[windows:]
        weight_ref, deep_ref, head_ref, tail_ref, point_ref = refs
        group_weight(weight_ref, 0, count, point_ref)
        for m in range(windows):
            deep = dot_transposed(block_refs[m][...], point_ref[...]).astype(LOW)
            deep_ref[m] = deep
            head_ref[m : m + 1, :] = deep[:1]
            tail_ref[m : m + 1, :] = deep[fine - 1 :]

    return run_kernel(
        kernel,
        list(blocks) + [weight],
        [((windows, fine, channels), LOW)] + [((windows, channels), LOW)] * 2,
        scratch=[pltpu.VMEM((channels, width), LOW)],
        flops=2 * windows * fine * width * channels,
        name="section_grad_deep",
    )


def section_grad_mix(deep, before, after, taps, weight, count):
    windows, fine, channels = deep.shape
    width = weight.shape[1]
    own = fine // 2

    def kernel(deep_ref, before_ref, after_ref, taps_ref, weight_ref, *refs):
        mix_ref, coarse_ref, even_ref, odd_ref, bias_ref, up_ref = refs
        group_weight(weight_ref, 1, count, up_ref)
        row = lax.broadcasted_iota(jnp.int32, (own, fine), 0)
        column = lax.broadcasted_iota(jnp.int32, (own, fine), 1)
        pool = (column // 2 == row).astype(jnp.float32).astype(LOW)
        bias = jnp.zeros((1, channels), jnp.float32)
        for m in range(windows):
            rows = deep_ref[m].astype(jnp.float32)
            previous, following = shifted(
                rows,
                before_ref[m : m + 1, :].astype(jnp.float32),
                after_ref[m : m + 1, :].astype(jnp.float32),
            )
            mix = (
                taps_ref[0:1, :] * following + taps_ref[1:2, :] * rows + taps_ref[2:3, :] * previous
            ).astype(LOW)
            mix_ref[m] = mix
            bias = bias + jnp.sum(mix.astype(jnp.float32), axis=0, keepdims=True)
            coarse = dot_rows(pool, mix).astype(LOW)
            coarse_ref[m] = coarse
            half = odd_ref if m % 2 else even_ref
            half[m // 2] = dot_rows(coarse, up_ref[...]).astype(LOW)
        bias_ref[...] = bias

    return run_kernel(
        kernel,
        [deep, before, after, taps, weight],
        [((windows, fine, channels), LOW), ((windows, own, channels), LOW)]
        + [((windows // 2, own, width), LOW)] * 2
        + [((1, channels), jnp.float32)],
        scratch=[pltpu.VMEM((channels, width), LOW)],
        flops=2 * windows * own * width * channels,
        name="section_grad_mix",
    )


def section_grad_encoder(mix, weight, count):
    windows, fine, channels = mix.shape
    width = weight.shape[1]

    def kernel(mix_ref, weight_ref, even_ref, odd_ref, lateral_ref):
        group_weight(weight_ref, 2, count, lateral_ref)
        for m in range(windows):
            half = odd_ref if m % 2 else even_ref
            half[m // 2] = dot_rows(mix_ref[m], lateral_ref[...]).astype(LOW)

    return run_kernel(
        kernel,
        [mix, weight],
        [((windows // 2, fine, width), LOW)] * 2,
        scratch=[pltpu.VMEM((channels, width), LOW)],
        flops=2 * windows * fine * width * channels,
        name="section_grad_encoder",
    )


def section_mixture(coarse_blocks, fine_blocks, weight, bias, count):
    fine, width = fine_blocks[0].shape
    own = fine // 2
    channels = weight.shape[0] // 3
    windows = len(fine_blocks)

    def kernel(*refs):
        coarse_refs, fine_refs, refs = refs[:windows], refs[windows : 2 * windows], refs[2 * windows :]
        weight_ref, bias_ref, mix_ref, head_ref, tail_ref, up_ref, lateral_ref = refs
        group_weight(weight_ref, 1, count, up_ref)
        group_weight(weight_ref, 2, count, lateral_ref)
        row = lax.broadcasted_iota(jnp.int32, (fine, own), 0)
        column = lax.broadcasted_iota(jnp.int32, (fine, own), 1)
        repeat = (row // 2 == column).astype(jnp.float32).astype(LOW)
        for m in range(windows):
            repeated = dot_rows(repeat, coarse_refs[m][...]).astype(LOW)
            mix = (
                dot_transposed(repeated, up_ref[...])
                + dot_transposed(fine_refs[m][...], lateral_ref[...])
                + bias_ref[...]
            ).astype(LOW)
            mix_ref[m] = mix
            head_ref[m : m + 1, :] = mix[:1]
            tail_ref[m : m + 1, :] = mix[fine - 1 :]

    return run_kernel(
        kernel,
        list(coarse_blocks) + list(fine_blocks) + [weight, bias],
        [((windows, fine, channels), LOW)] + [((windows, channels), LOW)] * 2,
        scratch=[pltpu.VMEM((channels, width), LOW)] * 2,
        flops=4 * windows * fine * width * channels,
        name="section_mixture",
    )


def section_deep(mix, before, after, taps, weight, grad_deep, count):
    windows, fine, channels = mix.shape
    width = weight.shape[1]

    def kernel(mix_ref, before_ref, after_ref, taps_ref, weight_ref, grad_ref, *refs):
        deep_ref, even_ref, odd_ref, sums_ref, point_ref = refs
        group_weight(weight_ref, 0, count, point_ref)
        sums = [jnp.zeros((1, channels), jnp.float32)] * 3
        for m in range(windows):
            rows = mix_ref[m].astype(jnp.float32)
            previous, following = shifted(
                rows,
                before_ref[m : m + 1, :].astype(jnp.float32),
                after_ref[m : m + 1, :].astype(jnp.float32),
            )
            deep = (
                taps_ref[0:1, :] * previous + taps_ref[1:2, :] * rows + taps_ref[2:3, :] * following
            ).astype(LOW)
            deep_ref[m] = deep
            half = odd_ref if m % 2 else even_ref
            half[m // 2] = dot_rows(deep, point_ref[...]).astype(LOW)
            grad = grad_ref[m].astype(jnp.float32)
            sums = [
                total + jnp.sum(part * grad, axis=0, keepdims=True)
                for total, part in zip(sums, (previous, rows, following), strict=True)
            ]
        for s, total in enumerate(sums):
            sums_ref[s : s + 1, :] = total

    return run_kernel(
        kernel,
        [mix, before, after, taps, weight, grad_deep],
        [((windows, fine, channels), LOW)]
        + [((windows // 2, fine, width), LOW)] * 2
        + [((3, channels), jnp.float32)],
        scratch=[pltpu.VMEM((channels, width), LOW)],
        flops=2 * windows * fine * width * channels,
        name="section_deep",
    )


def section_weights(deep, grad_coarse, grad_mix, cot_blocks, coarse_blocks, fine_blocks, count):
    windows, fine, channels = deep.shape
    width = cot_blocks[0].shape[1]
    share = channels // count

    def kernel(deep_ref, coarse_ref, mix_ref, *refs):
        cot_refs, refs = refs[:windows], refs[windows:]
        row_refs, refs = refs[:windows], refs[windows:]
        fine_refs, (out_ref,) = refs[:windows], refs[windows:]
        pairs = ((deep_ref, cot_refs), (coarse_ref, row_refs), (mix_ref, fine_refs))
        for which, (left_ref, right_refs) in enumerate(pairs):
            total = dot_leading(left_ref[0], right_refs[0][...])
            for m in range(1, windows):
                total = total + dot_leading(left_ref[m], right_refs[m][...])
            low = total.astype(LOW)
            for t in range(count):
                out_ref[t, which * share : (which + 1) * share, :] = low[t * share : (t + 1) * share]

    return run_kernel(
        kernel,
        [deep, grad_coarse, grad_mix] + list(cot_blocks) + list(coarse_blocks) + list(fine_blocks),
        [((count, 3 * share, width), LOW)],
        flops=5 * windows * fine * width * channels,
        name="section_weights",
    )[0]


def from_ahead(rows, step):
    count = lax.axis_size("tensor")
    return lax.ppermute(rows, "tensor", [((i + step) % count, i) for i in range(count)])


def spread_blocks(rows):
    return [rows] + [from_ahead(rows, k) for k in range(1, lax.axis_size("tensor"))]


def collect_blocks(parts):
    count = lax.axis_size("tensor")
    return [from_ahead(parts[k - 1], count - k) for k in range(1, count)]


def to_own(rows):
    return jnp.roll(rows, -lax.axis_index("tensor") * (rows.shape[0] // lax.axis_size("tensor")), 0)


def dp_flip(cells, mask):
    count = lax.axis_size("dp")
    return lax.ppermute(cells, "dp", [(i, i ^ mask) for i in range(count)])


def direct_dp():
    return lax.axis_size("dp") == 8


def gather_blocks(shard):
    blocks = {0: shard, 1: dp_flip(shard, 1)}
    for mask in (2, 4, 6):
        blocks[mask] = dp_flip(shard, mask)
    for mask in (2, 4, 6):
        blocks[mask + 1] = dp_flip(blocks[mask], 1)
    return [blocks[mask] for mask in range(8)]


def gather_rows(shard):
    if not direct_dp():
        return lax.all_gather(shard, "dp", axis=0, tiled=True)
    return jnp.concatenate(gather_blocks(shard), axis=0)


def scatter_halves(even, odd):
    if not direct_dp():
        return lax.psum_scatter(even[0], "dp", scatter_dimension=0, tiled=True).astype(jnp.float32)
    pairs = even.astype(jnp.float32) + dp_flip(odd, 1).astype(jnp.float32)
    total = pairs[0]
    for chip in range(1, even.shape[0]):
        total = total + dp_flip(pairs[chip].astype(even.dtype), 2 * chip).astype(jnp.float32)
    return total


def scatter_rows(parts):
    if not direct_dp():
        return lax.psum_scatter(parts, "dp", scatter_dimension=0, tiled=True).astype(jnp.float32)
    blocks = parts.reshape(8, -1, parts.shape[1])
    pairs = {
        mask: blocks[mask].astype(jnp.float32)
        + dp_flip(blocks[mask + 1], 1).astype(jnp.float32)
        for mask in (2, 4, 6, 0)
    }
    total = pairs[0]
    for mask in (2, 4, 6):
        total = total + dp_flip(pairs[mask].astype(parts.dtype), mask).astype(jnp.float32)
    return total


def gather_true(shard):
    if not direct_dp():
        return lax.all_gather(shard, "dp", axis=0, tiled=True)
    me = lax.axis_index("dp")
    rows = shard.shape[0]
    whole = jnp.zeros((8 * rows, shard.shape[1]), shard.dtype)
    for mask, block in enumerate(gather_blocks(shard)):
        whole = lax.dynamic_update_slice(whole, block, ((me ^ mask) * rows, 0))
    return whole


def scatter_true(whole):
    if not direct_dp():
        return lax.psum_scatter(whole, "dp", scatter_dimension=0, tiled=True).astype(jnp.float32)
    me = lax.axis_index("dp")
    rows = whole.shape[0] // 8
    blocks = [
        lax.dynamic_slice_in_dim(whole, (me ^ mask) * rows, rows, 0) for mask in range(8)
    ]
    return scatter_rows(jnp.concatenate(blocks, axis=0))


def gather_dp(shard):
    return lax.all_gather(shard, "dp", axis=0, tiled=True)


def scatter_dp(whole):
    return lax.psum_scatter(whole, "dp", scatter_dimension=0, tiled=True)


def scatter_tensor(whole):
    return lax.psum_scatter(whole, "tensor", scatter_dimension=0, tiled=True)


def gather_small(cells):
    count = lax.axis_size("tensor")
    line = jnp.stack([cells] + [from_ahead(cells, k) for k in range(1, count)], axis=0)
    if not direct_dp():
        line = jnp.roll(line, lax.axis_index("tensor"), 0)
        return lax.all_gather(line, "dp", axis=0)
    spots = jnp.arange(8 * count, dtype=jnp.int32)
    source = (spots // count ^ lax.axis_index("dp")) * count + (
        spots % count - lax.axis_index("tensor")
    ) % count
    found = jnp.concatenate(gather_blocks(line), axis=0)
    chosen = (source[:, None] == spots[None, :]).astype(LOW)
    return dot_plain(chosen, found).astype(LOW).reshape(8, count, -1)


def after(cells, *done):
    return lax.optimization_barrier((cells, done))[0]


def edges(head, tail):
    ends = lax.axis_size("tensor") - 1
    return (
        lax.ppermute(tail, "tensor", [(i, i + 1) for i in range(ends)]),
        lax.ppermute(head, "tensor", [(i + 1, i) for i in range(ends)]),
    )


def halo(cells):
    count = lax.axis_size("tensor")
    ends = count - 1
    before = lax.ppermute(cells[:, -1:], "tensor", [(i, i + 1) for i in range(ends)])
    after = lax.ppermute(cells[:, :1], "tensor", [(i + 1, i) for i in range(ends)])
    return jnp.concatenate([before, cells, after], axis=1)


def body_plain(
    activations,
    encoder,
    species,
    cotangent,
    norm_gain,
    norm_shift,
    species_table,
    query_weight,
    key_weight,
    value_weight,
    output_weight,
    expand_weight,
    contract_weight,
    position_weight,
    content_bias,
    position_bias,
    upsample_weight,
    lateral_weight,
    depthwise_weight,
    section_bias,
    pointwise_weight,
):
    windows = lax.axis_size("dp")
    count = lax.axis_size("tensor")
    own = activations.shape[1]
    length = own * count
    width = activations.shape[2]
    local_heads = query_weight.shape[1] // KEYD
    keys = local_heads * KEYD
    values = local_heads * VALD

    raw = spread_blocks(activations[0])
    attn_shard = jnp.concatenate([query_weight, key_weight, value_weight, output_weight.T], axis=1)
    attn_blocks = [gather_dp(attn_shard)]
    where = jnp.stack([lax.axis_index("dp"), lax.axis_index("tensor"), species[0]])

    small = jnp.concatenate(
        [norm_gain, norm_shift, species_table, depthwise_weight, section_bias[None]], axis=0
    )
    n_small = small.size
    n_position = position_weight.size
    n_bias = content_bias.size
    packed = gather_small(
        jnp.concatenate(
            [
                small.reshape(-1),
                position_weight.reshape(-1),
                content_bias.reshape(-1),
                position_bias.reshape(-1),
            ]
        )
    )
    small_all = packed[:, :, :n_small].reshape(windows, count, 10, -1)
    norm_all = jnp.transpose(small_all[:, :, :6], (2, 0, 1, 3)).reshape(6, width)
    norm_all = norm_all.astype(jnp.float32)
    gain_vals, shift_vals, table_rows = norm_all[:2], norm_all[2:4], norm_all[4:]
    small_group = lax.dynamic_index_in_dim(small_all, lax.axis_index("dp"), 0, False)
    small_group = jnp.swapaxes(small_group, 0, 1).reshape(10, -1).astype(jnp.float32)
    channels = small_group.shape[1]
    depth_taps = small_group[6:9]
    bias_section = small_group[9]
    heads_all = lax.dynamic_index_in_dim(packed, lax.axis_index("tensor"), 1, False)[:, n_small:]
    w_position = heads_all[:, :n_position].reshape(KEYD, BASIS, local_heads)
    bias_content = heads_all[:, n_position : n_position + n_bias].reshape(KEYD, local_heads)
    bias_position = heads_all[:, n_position + n_bias :].reshape(KEYD, local_heads)

    section_shard = jnp.concatenate([pointwise_weight, upsample_weight.T, lateral_weight.T], axis=0)
    w_section = lax.all_gather(section_shard, "tensor", axis=0).reshape(count, 3, -1, width)
    w_point = w_section[:, 0].reshape(channels, width)
    w_up = w_section[:, 1].reshape(channels, width)
    w_lat = w_section[:, 2].reshape(channels, width)
    cot_all = gather_dp(cotangent[0])
    ffn_shard = jnp.concatenate([expand_weight, contract_weight.T], axis=1)
    w_ffn = lax.all_gather(ffn_shard, "dp", axis=0, tiled=True)
    hidden_count = expand_weight.shape[1]
    enc_all = gather_dp(encoder[0])

    fine = 2 * own
    grad_deep = dot_transposed(cot_all, w_point).astype(LOW)
    grad_wide = halo(grad_deep.reshape(windows, fine, channels)).astype(jnp.float32)
    grad_mix = (
        depth_taps[0] * grad_wide[:, 2:]
        + depth_taps[1] * grad_wide[:, 1:-1]
        + depth_taps[2] * grad_wide[:, :-2]
    ).astype(LOW)
    grad_coarse = jnp.sum(
        grad_mix.astype(jnp.float32).reshape(windows * own, 2, channels), axis=1
    ).astype(LOW)
    grad_resid_two = scatter_dp(dot_plain(grad_coarse, w_up).astype(LOW)).astype(jnp.float32)
    grad_ffn = spread_blocks(grad_resid_two.astype(LOW))

    species_mask = (jnp.arange(SPECIES, dtype=jnp.int32) == species[0]).astype(jnp.float32)
    species_row = jnp.sum(species_mask[:, None] * table_rows, axis=0)
    content_flat = bias_content.astype(jnp.float32).T.reshape(1, -1)
    position_flat = bias_position.astype(jnp.float32).T.reshape(1, -1)
    basis_turned = jnp.pad(basis_table(length, BASIS).astype(LOW)[::-1], ((0, 1), (0, 0)))
    rel_weight = jnp.transpose(w_position, (1, 2, 0)).reshape(BASIS, -1)
    rel_turned = dot_plain(basis_turned, rel_weight).astype(LOW)
    attn_parts, saved = attention_forward(
        where,
        raw,
        [species_row[None], gain_vals[:1], shift_vals[:1], content_flat, position_flat],
        rel_turned,
        attn_blocks,
        local_heads,
    )
    resid_one, unit_two, scale_two, normed_two = second_norm(
        attn_parts[0],
        collect_blocks(attn_parts[1:]),
        [raw[0], species_row[None]],
        gain_vals[1:],
        shift_vals[1:],
    )

    contract_parts, (normed_two_all, hidden_low, slope) = feed_forward_up(
        spread_blocks(normed_two), w_ffn
    )
    ffn_parts, (grad_ffn_all, grad_hidden_pre) = feed_forward_back(grad_ffn, slope, w_ffn)
    grad_resid_one, grad_attn, sums_two = second_norm_back(
        ffn_parts[0],
        collect_blocks(ffn_parts[1:]),
        unit_two,
        scale_two,
        gain_vals[1:],
        grad_resid_two,
    )

    resid_two = resid_one + contract_parts[0]
    for block in collect_blocks(contract_parts[1:]):
        resid_two = resid_two + block.astype(jnp.float32)
    section_all = gather_dp(resid_two.astype(LOW))
    coarse = dot_transposed(section_all, w_up).reshape(windows, own, channels)
    section_mix = (
        jnp.repeat(coarse, 2, axis=1)
        + dot_transposed(enc_all, w_lat).reshape(windows, fine, channels)
        + bias_section
    ).astype(LOW)
    mix_wide = halo(section_mix).astype(jnp.float32)
    deep_rows = (
        depth_taps[0] * mix_wide[:, :-2]
        + depth_taps[1] * mix_wide[:, 1:-1]
        + depth_taps[2] * mix_wide[:, 2:]
    ).astype(LOW)
    deep_rows = deep_rows.reshape(windows * fine, channels)
    section_out = scatter_dp(dot_plain(deep_rows, w_point).astype(LOW)).astype(LOW)
    grad_mix_rows = grad_mix.reshape(windows * fine, channels)
    encoder_grad = scatter_dp(dot_plain(grad_mix_rows, w_lat).astype(LOW)).astype(jnp.float32)
    grad_centre = grad_wide[:, 1:-1]
    grad_section_small = jnp.stack(
        [jnp.sum(mix_wide[:, s : s + fine] * grad_centre, axis=(0, 1)) for s in range(3)]
        + [jnp.sum(grad_mix.astype(jnp.float32), axis=(0, 1))],
        axis=1,
    )
    section_cols = jnp.stack(
        [
            dot_leading(deep_rows, cot_all).astype(LOW).reshape(count, -1, width),
            dot_leading(grad_coarse, section_all).astype(LOW).reshape(count, -1, width),
            dot_leading(grad_mix_rows, enc_all).astype(LOW).reshape(count, -1, width),
        ],
        axis=1,
    )
    section_cols = scatter_tensor(section_cols)[0].astype(jnp.float32)

    ffn_out = scatter_dp(
        feed_forward_weights(normed_two_all, grad_ffn_all, hidden_low, grad_hidden_pre)
    ).astype(jnp.float32)

    head_parts, (grad_attn_all, grad_heads, grad_normed_part, bias_sums, rel_grad) = (
        attention_backward(
            where, spread_blocks(grad_attn), saved, rel_turned, basis_turned, local_heads
        )
    )
    grad_resid_in = first_norm_back(
        where,
        head_parts[0],
        collect_blocks(head_parts[1:]),
        saved[2],
        saved[3],
        gain_vals[:1],
        grad_resid_one,
    )
    weights, _, small, _ = attention_weights(
        where, saved, grad_attn_all, grad_heads, grad_normed_part, gain_vals[:1], sums_two,
        bias_sums, rel_grad, 1,
    )
    attn_out = scatter_dp(weights[0]).astype(jnp.float32)
    norm_cols = jnp.swapaxes(small[0, :6].reshape(6, windows, channels), 0, 1)
    head_cols = small[0, 8 : 10 + BASIS, :keys].reshape(2 + BASIS, local_heads, KEYD)
    head_cols = jnp.transpose(head_cols, (2, 0, 1))
    heads_cols = jnp.concatenate(
        [
            head_cols[:, 2:].reshape(windows, -1),
            head_cols[:, 0].reshape(windows, -1),
            head_cols[:, 1].reshape(windows, -1),
        ],
        axis=1,
    )
    small_out = scatter_dp(jnp.concatenate([norm_cols.reshape(windows, -1), heads_cols], axis=1))
    small_out = small_out[0]
    n_norm = 6 * channels
    group_cols = jnp.concatenate([small_out[:n_norm].reshape(6, channels), grad_section_small.T])
    group_cols = jnp.swapaxes(group_cols.reshape(10, count, -1), 0, 1).reshape(count, -1)
    group_cols = to_own(group_cols)
    norm_out = group_cols[0]
    for k in range(1, count):
        norm_out = norm_out + from_ahead(group_cols[k], count - k)
    norm_out = norm_out.reshape(10, -1)
    heads_out = small_out[n_norm:]
    return (
        section_out[None],
        grad_resid_in,
        encoder_grad[None],
        norm_out[0:2],
        norm_out[2:4],
        norm_out[4:6],
        attn_out[:, :keys],
        attn_out[:, keys : 2 * keys],
        attn_out[:, 2 * keys : 2 * keys + values],
        attn_out[:, 2 * keys + values :].T,
        ffn_out[:, :hidden_count],
        ffn_out[:, hidden_count:].T,
        heads_out[:n_position].reshape(position_weight.shape),
        heads_out[n_position : n_position + n_bias].reshape(content_bias.shape),
        heads_out[n_position + n_bias :].reshape(position_bias.shape),
        section_cols[1].T,
        section_cols[2].T,
        norm_out[6:9],
        norm_out[9],
        section_cols[0],
    )


def body_direct(
    activations,
    encoder,
    species,
    cotangent,
    norm_gain,
    norm_shift,
    species_table,
    query_weight,
    key_weight,
    value_weight,
    output_weight,
    expand_weight,
    contract_weight,
    position_weight,
    content_bias,
    position_bias,
    upsample_weight,
    lateral_weight,
    depthwise_weight,
    section_bias,
    pointwise_weight,
):
    count = lax.axis_size("tensor")
    own, width = activations.shape[1:]
    length = own * count
    local_heads = query_weight.shape[1] // KEYD
    keys = local_heads * KEYD
    values = local_heads * VALD
    hidden_count = expand_weight.shape[1]
    share = section_bias.shape[0]
    where = jnp.stack([lax.axis_index("dp"), lax.axis_index("tensor"), species[0]])

    packed = jnp.concatenate(
        [
            norm_gain.reshape(-1),
            norm_shift.reshape(-1),
            species_table.reshape(-1),
            depthwise_weight.reshape(-1),
            section_bias,
            jnp.transpose(position_weight, (1, 2, 0)).reshape(-1),
            content_bias.T.reshape(-1),
            position_bias.T.reshape(-1),
        ]
    )[None]
    line = jnp.concatenate(spread_blocks(packed), axis=0)
    raw = spread_blocks(activations[0])
    attn_shard = jnp.concatenate([query_weight, key_weight, value_weight, output_weight.T], axis=1)
    attn_blocks = gather_blocks(attn_shard)
    small_blocks = gather_blocks(line)
    section_shard = jnp.concatenate([pointwise_weight, upsample_weight.T, lateral_weight.T], axis=0)
    w_section = lax.all_gather(section_shard, "tensor", axis=0, tiled=True)
    small_blocks, raw, attn_blocks = lax.optimization_barrier((small_blocks, raw, attn_blocks))
    ffn_shard = jnp.concatenate([expand_weight, contract_weight.T], axis=1)
    w_ffn = lax.all_gather(ffn_shard, "dp", axis=0, tiled=True)

    basis_turned = jnp.pad(basis_table(length, BASIS).astype(LOW)[::-1], ((0, 1), (0, 0)))
    rows, (depth_taps, bias_section, rel_turned, content_flat, position_flat) = unpack_small(
        where, small_blocks, basis_turned, width, local_heads
    )
    gain_one, gain_two, shift_one, shift_two, species_row = rows
    attn_parts, saved = attention_forward(
        where,
        raw,
        [species_row, gain_one, shift_one, content_flat, position_flat],
        rel_turned,
        attn_blocks,
        local_heads,
    )
    attn_received = collect_blocks(attn_parts[1:])

    cot_blocks = gather_blocks(after(cotangent[0], attn_blocks))
    grad_deep, head, tail = section_grad_deep(cot_blocks, w_section, count)
    before, following = edges(head, tail)
    grad_mix, grad_coarse, even, odd, bias_grad = section_grad_mix(
        grad_deep, before, following, depth_taps, w_section, count
    )
    grad_resid_two = scatter_halves(even, odd)
    grad_ffn = spread_blocks(grad_resid_two.astype(LOW))

    resid_one, unit_two, scale_two, normed_two = second_norm(
        attn_parts[0], attn_received, [raw[0], species_row], gain_two, shift_two
    )
    contract_parts, (normed_two_all, hidden_low, slope) = feed_forward_up(
        spread_blocks(normed_two), w_ffn
    )
    ffn_parts, (grad_ffn_all, grad_hidden_pre) = feed_forward_back(grad_ffn, slope, w_ffn)
    grad_resid_one, grad_attn, sums_two = second_norm_back(
        ffn_parts[0], collect_blocks(ffn_parts[1:]), unit_two, scale_two, gain_two, grad_resid_two
    )

    enc_blocks = gather_blocks(after(encoder[0], grad_resid_two))
    resid_two = resid_one + contract_parts[0]
    for block in collect_blocks(contract_parts[1:]):
        resid_two = resid_two + block.astype(jnp.float32)
    section_blocks = gather_blocks(resid_two.astype(LOW))
    section_mix, head, tail = section_mixture(
        section_blocks, enc_blocks, w_section, bias_section, count
    )
    before, following = edges(head, tail)
    deep_rows, out_even, out_odd, taps_grad = section_deep(
        section_mix, before, following, depth_taps, w_section, grad_deep, count
    )
    encoder_grad = scatter_halves(*section_grad_encoder(grad_mix, w_section, count))
    section_out = scatter_halves(out_even, out_odd).astype(LOW)
    section_cols = section_weights(
        deep_rows, grad_coarse, grad_mix, cot_blocks, section_blocks, enc_blocks, count
    )
    section_cols = scatter_tensor(section_cols)[0].astype(jnp.float32)
    ffn_out = scatter_dp(
        feed_forward_weights(normed_two_all, grad_ffn_all, hidden_low, grad_hidden_pre)
    ).astype(jnp.float32)

    head_parts, (grad_attn_all, grad_heads, grad_normed_part, bias_sums, rel_grad) = (
        attention_backward(
            where, spread_blocks(grad_attn), saved, rel_turned, basis_turned, local_heads
        )
    )
    grad_resid_in = first_norm_back(
        where,
        head_parts[0],
        collect_blocks(head_parts[1:]),
        saved[2],
        saved[3],
        gain_one,
        grad_resid_one,
    )
    even, odd, small_even, small_odd = attention_weights(
        where,
        saved,
        grad_attn_all,
        grad_heads,
        grad_normed_part,
        gain_one,
        sums_two,
        bias_sums,
        rel_grad,
        len(attn_blocks),
    )
    small_out = scatter_halves(small_even, small_odd)
    attn_out = scatter_halves(even, odd)

    n_norm = 4 + SPECIES
    group = share * count
    group_cols = jnp.concatenate([small_out[:n_norm, :group], taps_grad, bias_grad], axis=0)
    norm_out = group_cols
    for k in range(1, count):
        norm_out = norm_out + from_ahead(group_cols, k)
    norm_out = lax.dynamic_slice_in_dim(norm_out, lax.axis_index("tensor") * share, share, 1)
    part = KEYD // lax.axis_size("dp")
    heads_out = small_out[8 : 10 + BASIS, :keys].reshape(2 + BASIS, local_heads, KEYD)[:, :, :part]
    heads_out = jnp.transpose(heads_out, (2, 0, 1))
    return (
        section_out[None],
        grad_resid_in,
        encoder_grad[None],
        norm_out[0:2],
        norm_out[2:4],
        norm_out[4:n_norm],
        attn_out[:, :keys],
        attn_out[:, keys : 2 * keys],
        attn_out[:, 2 * keys : 2 * keys + values],
        attn_out[:, 2 * keys + values :].T,
        ffn_out[:, :hidden_count],
        ffn_out[:, hidden_count:].T,
        heads_out[:, 2:],
        heads_out[:, 0],
        heads_out[:, 1],
        section_cols[share : 2 * share].T,
        section_cols[2 * share :].T,
        norm_out[n_norm : n_norm + 3],
        norm_out[n_norm + 3],
        section_cols[:share],
    )


def solution(mesh):
    rows = P("dp", "tensor", None)
    narrow = P(None, ("dp", "tensor"))
    split = P("dp", "tensor")
    turned = P("tensor", "dp")
    vector = P(("dp", "tensor"))
    tall = P(("dp", "tensor"), None)
    position = P("dp", None, "tensor")
    weights = (split, split, split, turned, split, turned, position, split, split)
    return jax.shard_map(
        body_direct if mesh.shape["dp"] == 8 else body_plain,
        mesh=mesh,
        in_specs=(rows, rows, P("dp"), rows, narrow, narrow, narrow)
        + weights
        + (narrow, narrow, narrow, vector, tall),
        out_specs=(rows, rows, rows, narrow, narrow, narrow)
        + weights
        + (narrow, narrow, narrow, vector, tall),
        check_vma=False,
    )
```

time: 588 us -> 435 us (0.74); the launches traced: 578 us -> 434 us
  blocking collectives: 138 us -> 0 us
  starting transfers between devices: 55.7 us -> 137 us
  Pallas kernels: 0 us -> 65.1 us
  waiting for transfers between devices: 223 us -> 160 us
  matrix products: 57 us -> 0 us
  local copies, waits for them, and re-layouts: 55.9 us -> 35.1 us
  other arithmetic: 30.1 us -> 20.8 us
    ppermute x4 -> x59, waiting for transfers between devices: 4.03 us -> 80.1 us  [the longest x55 73.6 us: dp_flip(): return lax.ppermute(cells, 'dp', [(i, i ^ mask) for i in range(count)])]
    reduce_scatter x3 -> x1, waiting for transfers between devices: 73.1 us -> 0.01 us  [scatter_dp(): return lax.psum_scatter(whole, 'dp', scatter_dimension=0, tiled=True)]
    unnamed x3 -> x0, blocking collectives: 69.1 us -> none
    all_gather x4 -> x0, blocking collectives: 68.9 us -> none  [the longest x1 20.5 us: body(): lax.all_gather(small, 'tensor', axis=0)]
    pallas_call x0 -> x16, Pallas kernels: none -> 65.1 us  [run_kernel(): pl.pallas_call(kernel, in_specs=specs, out_specs=[whole] * len(shapes), o...]
    dot_general x33 -> x0, matrix products: 57 us -> none  [the longest x10 23.3 us: dot_plain(): return jnp.dot(left_side, right_side, preferred_element_type=jnp.float32)]
    ppermute x4 -> x59, starting transfers between devices: 10.2 us -> 57.2 us  [the longest x55 47.1 us: dp_flip(): return lax.ppermute(cells, 'dp', [(i, i ^ mask) for i in range(count)])]
    unnamed x15 -> x4, waiting for transfers between devices: 38.9 us -> 0.07 us
  transfers between devices with their start and end apart: 41 -> 93, of which waited for: 21 -> 43; matrix products, arithmetic and copies ran while one was open for 23% -> 6% of each run, Pallas kernels for 0% -> 11%
where the time goes in v2:
time: 435 us; the launch traced here: 434 us
  waiting for transfers between devices  160 us (37%)
  starting transfers between devices  137 us (31%)
  Pallas kernels  65.1 us (15%)
  local copies, waits for them, and re-layouts  35.1 us (8%)
  other arithmetic  20.8 us (5%)
  between operations  15.6 us (4%)
    ppermute x30, starting transfers between devices, from_ahead(): lax.ppermute(rows, 'tensor', [((i + step) % count, i) for i in range(coun...  80.1 us
    ppermute x30, waiting for transfers between devices, from_ahead(): lax.ppermute(rows, 'tensor', [((i + step) % count, i) for i in range(coun...  79.8 us
    ppermute x55, waiting for transfers between devices, dp_flip(): return lax.ppermute(cells, 'dp', [(i, i ^ mask) for i in range(count)])  73.6 us
    pallas_call x16, Pallas kernels, run_kernel(): pl.pallas_call(kernel, in_specs=specs, out_specs=[whole] * len(shapes), o...  65.1 us
    ppermute x55, starting transfers between devices, dp_flip(): return lax.ppermute(cells, 'dp', [(i, i ^ mask) for i in range(count)])  47.1 us
    unnamed x207, local copies, waits for them, and re-layouts  23.2 us
  transfers between devices with their start and end apart: 93, of which 43 were waited for; matrix products, arithmetic and copies ran while one was open for 6% of the time, Pallas kernels for 11%

profile of v2, /device:TPU:0, one launch (start us, length us, event | category | flops | bytes accessed | tf_op | source)
XLA Modules:
  0.0 434.2 jit_solution(4077934958048975967)
XLA Ops:
  54.3 8.0 %collective-permute-done.11.refs_2_ = bf16[64,1536]{1,0:T(8,128)(2,1)S(1)} collective-permute-done((bf16[64,1536]{1,0:T(8,128)(2,1)S(1)}, bf16[64,1536]{1,0:T(8,128)(2,1)S(1)}, u32[]{:S(2)}, u32[]{:S(2)}) %collective-permute-start.11) | collective-permute-done | bytes 196640 | tf_op jit(solution)/shard_map/ppermute | solution.py:773
  74.9 9.5 %collective-permute-done.41.refs_6_ = bf16[128,1536]{1,0:T(8,128)(2,1)S(1)} collective-permute-done((bf16[128,1536]{1,0:T(8,128)(2,1)S(1)}, bf16[128,1536]{1,0:T(8,128)(2,1)S(1)}, u32[]{:S(2)}, u32[]{:S(2)}) %collective-permute-start.41) | collective-permute-done | bytes 393248 | tf_op jit(solution)/shard_map/ppermute | solution.py:791
  84.4 10.9 %collective-permute-done.39.refs_4_ = bf16[128,1536]{1,0:T(8,128)(2,1)S(1)} collective-permute-done((bf16[128,1536]{1,0:T(8,128)(2,1)S(1)}, bf16[128,1536]{1,0:T(8,128)(2,1)S(1)}, u32[]{:S(2)}, u32[]{:S(2)}) %collective-permute-start.39) | collective-permute-done | bytes 393248 | tf_op jit(solution)/shard_map/ppermute | solution.py:791
  118.2 6.5 %attention_forward.1 = (f32[64,1536]{1,0:T(8,128)S(1)}, bf16[64,1536]{1,0:T(8,128)(2,1)S(1)}, bf16[64,1536]{1,0:T(8,128)(2,1)S(1)}, bf16[64,1536]{1,0:T(8,128)(2...) custom-call(s32[3]{0:T(128)S(1)} %copy-done.73, ...), custom_call_target="tpu_custom_call" | custom-call | flops 805306368 | bytes 11815936 | tf_op jit(solution)/shard_map/attention_forward/pallas_call | solution.py:75
  125.3 4.9 %collective-permute-start.20 = (bf16[64,1536]{1,0:T(8,128)(2,1)S(1)}, bf16[64,1536]{1,0:T(8,128)(2,1)S(1)}, u32[]{:S(2)}, u32[]{:S(2)}) collective-permute-start(bf16[64,1536]{1,0:T(8,128)(2,1)S(1)} %get-tuple-element.143), channel_id=1, source_target_pairs={{3,0},{0,1},{1,2},{2,3},{7,4},{4,5},{5,6},{6,7},{11,8},{8,9},{9,10... | collective-permute-start | bytes 589832 | tf_op jit(solution)/shard_map/ppermute | solution.py:773
  139.0 6.5 %collective-permute-done.21.refs_1_ = bf16[64,1536]{1,0:T(8,128)(2,1)S(1)} collective-permute-done((bf16[64,1536]{1,0:T(8,128)(2,1)S(1)}, bf16[64,1536]{1,0:T(8,128)(2,1)S(1)}, u32[]{:S(2)}, u32[]{:S(2)}) %collective-permute-start.21) | collective-permute-done | bytes 196640 | tf_op jit(solution)/shard_map/ppermute | solution.py:773
  146.4 4.7 %collective-permute-start.25 = (bf16[64,1536]{1,0:T(8,128)(2,1)S(1)}, bf16[64,1536]{1,0:T(8,128)(2,1)S(1)}, u32[]{:S(2)}, u32[]{:S(2)}) collective-permute-start(bf16[64,1536]{1,0:T(8,128)(2,1)S(1)} %get-tuple-element.149.refs_0_), channel_id=1, source_target_pairs={{3,0},{0,1},{1,2},{2,3},{7,4},{4,5},{5,6},{6,7},{11,8},{8,9},{9,10... | collective-permute-start | bytes 589832 | tf_op jit(solution)/shard_map/ppermute | solution.py:773
  161.7 4.9 %collective-permute-done.24.refs_2_ = bf16[64,1536]{1,0:T(8,128)(2,1)S(1)} collective-permute-done((bf16[64,1536]{1,0:T(8,128)(2,1)S(1)}, bf16[64,1536]{1,0:T(8,128)(2,1)S(1)}, u32[]{:S(2)}, u32[]{:S(2)}) %collective-permute-start.24) | collective-permute-done | bytes 196640 | tf_op jit(solution)/shard_map/ppermute | solution.py:773
  186.2 6.5 %collective-permute-done.27 = bf16[64,1536]{1,0:T(8,128)(2,1)S(1)} collective-permute-done((bf16[64,1536]{1,0:T(8,128)(2,1)S(1)}, bf16[64,1536]{1,0:T(8,128)(2,1)S(1)}, u32[]{:S(2)}, u32[]{:S(2)}) %collective-permute-start.27) | collective-permute-done | bytes 196640 | tf_op jit(solution)/shard_map/ppermute | solution.py:773
  207.0 6.5 %section_mixture.1 = (bf16[8,128,192]{2,1,0:T(8,128)(2,1)}, bf16[8,192]{1,0:T(8,128)(2,1)S(1)}, bf16[8,192]{1,0:T(8,128)(2,1)S(1)}) custom-call(bf16[64,1536]{1,0:T(8,128)(2,1)S(1)} %add_convert_fusion.refs_0_.refs_8_, bf16[64,1536]{1,0:T(8,128)(2,1)S(1)} %collective-permute-done.29.refs_1_.refs_9_, ...), custom_call_target="tpu_custom_call" | custom-call | flops 1207959552 | bytes 6888192 | tf_op jit(solution)/shard_map/section_mixture/pallas_call | solution.py:75
  213.6 6.2 %collective-permute-start.56 = (bf16[8,192]{1,0:T(8,128)(2,1)S(1)}, bf16[8,192]{1,0:T(8,128)(2,1)S(1)}, u32[]{:S(2)}, u32[]{:S(2)}) collective-permute-start(bf16[8,192]{1,0:T(8,128)(2,1)S(1)} %get-tuple-element.164), channel_id=1, source_target_pairs={{0,1},{1,2},{2,3},{4,5},{5,6},{6,7},{8,9},{9,10},{10,11},{12,13},{... | collective-permute-start | bytes 9224 | tf_op jit(solution)/shard_map/ppermute | solution.py:894
  231.5 7.7 %section_weights.1 = bf16[4,144,1536]{2,1,0:T(8,128)(2,1)} custom-call(bf16[8,128,192]{2,1,0:T(8,128)(2,1)} %copy-done.31, bf16[8,64,192]{2,1,0:T(8,128)(2,1)S(1)} %copy-done.49, bf16[8,128,192]{2,1,0:T(8,128)(2,1)} %copy-done.1, bf16[128,1536]{1,0:T(8,128)(2,1)S(1)} %bitcast.118, bf16[128,1536]{1,0:T(8,128)(2,1)S(1)} %copy-done.11, ...), custom_call_target="tpu_custom_call" | custom-call | flops 1509949440 | bytes 10616832 | tf_op jit(solution)/shard_map/section_weights/pallas_call | solution.py:75
  250.8 7.8 %collective-permute-done.64.refs_3_ = bf16[64,1536]{1,0:T(8,128)(2,1)S(1)} collective-permute-done((bf16[64,1536]{1,0:T(8,128)(2,1)S(1)}, bf16[64,1536]{1,0:T(8,128)(2,1)S(1)}, u32[]{:S(2)}, u32[]{:S(2)}) %collective-permute-start.64) | collective-permute-done | bytes 196640 | tf_op jit(solution)/shard_map/ppermute | solution.py:773
  258.6 13.5 %collective-permute-done.63.refs_2_ = bf16[64,1536]{1,0:T(8,128)(2,1)S(1)} collective-permute-done((bf16[64,1536]{1,0:T(8,128)(2,1)S(1)}, bf16[64,1536]{1,0:T(8,128)(2,1)S(1)}, u32[]{:S(2)}, u32[]{:S(2)}) %collective-permute-start.63) | collective-permute-done | bytes 196640 | tf_op jit(solution)/shard_map/ppermute | solution.py:773
  272.6 5.0 %feed_forward_back.1 = (f32[64,1536]{1,0:T(8,128)S(1)}, bf16[64,1536]{1,0:T(8,128)(2,1)}, bf16[64,1536]{1,0:T(8,128)(2,1)}, bf16[64,1536]{1,0:T(8,128)(2,1)}, bf...) custom-call(bf16[64,1536]{1,0:T(8,128)(2,1)S(1)} %copy-done.23, ...), custom_call_target="tpu_custom_call" | custom-call | flops 1207959552 | bytes 8454144 | tf_op jit(solution)/shard_map/feed_forward_back/pallas_call | solution.py:75
  277.6 15.6 %collective-permute-start.65 = (bf16[64,1536]{1,0:T(8,128)(2,1)}, bf16[64,1536]{1,0:T(8,128)(2,1)S(1)}, u32[]{:S(2)}, u32[]{:S(2)}) collective-permute-start(bf16[64,1536]{1,0:T(8,128)(2,1)} %get-tuple-element.170), channel_id=1, source_target_pairs={{3,0},{0,1},{1,2},{2,3},{7,4},{4,5},{5,6},{6,7},{11,8},{8,9},{9,10... | collective-permute-start | bytes 589832 | tf_op jit(solution)/shard_map/ppermute | solution.py:773
  303.4 4.8 %collective-permute-done.66.refs_1_ = bf16[64,1536]{1,0:T(8,128)(2,1)S(1)} collective-permute-done((bf16[64,1536]{1,0:T(8,128)(2,1)}, bf16[64,1536]{1,0:T(8,128)(2,1)S(1)}, u32[]{:S(2)}, u32[]{:S(2)}) %collective-permute-start.66) | collective-permute-done | bytes 196640 | tf_op jit(solution)/shard_map/ppermute | solution.py:773
  309.6 4.8 %collective-permute-start.70 = (bf16[64,1536]{1,0:T(8,128)(2,1)S(1)}, bf16[64,1536]{1,0:T(8,128)(2,1)S(1)}, u32[]{:S(2)}, u32[]{:S(2)}) collective-permute-start(bf16[64,1536]{1,0:T(8,128)(2,1)S(1)} %get-tuple-element.175.refs_0_), channel_id=1, source_target_pairs={{3,0},{0,1},{1,2},{2,3},{7,4},{4,5},{5,6},{6,7},{11,8},{8,9},{9,10... | collective-permute-start | bytes 589832 | tf_op jit(solution)/shard_map/ppermute | solution.py:773
  322.4 6.0 %collective-permute-done.69.refs_2_ = bf16[64,1536]{1,0:T(8,128)(2,1)S(1)} collective-permute-done((bf16[64,1536]{1,0:T(8,128)(2,1)S(1)}, bf16[64,1536]{1,0:T(8,128)(2,1)S(1)}, u32[]{:S(2)}, u32[]{:S(2)}) %collective-permute-start.69) | collective-permute-done | bytes 196640 | tf_op jit(solution)/shard_map/ppermute | solution.py:773
  328.5 7.1 %attention_backward.1 = (f32[64,1536]{1,0:T(8,128)S(1)}, bf16[64,1536]{1,0:T(8,128)(2,1)}, bf16[64,1536]{1,0:T(8,128)(2,1)}, bf16[64,1536]{1,0:T(8,128)(2,1)}, b...) custom-call(s32[3]{0:T(128)S(1)} %copy-done.74, ...), custom_call_target="tpu_custom_call" | custom-call | flops 805306368 | bytes 8700928 | tf_op jit(solution)/shard_map/attention_backward/pallas_call | solution.py:75
  336.4 5.6 %attention_weights.1 = (bf16[4,192,1024]{2,1,0:T(8,128)(2,1)}, bf16[4,192,1024]{2,1,0:T(8,128)(2,1)}, f32[4,48,192]{2,1,0:T(8,128)S(1)}, f32[4,48,192]{2,1,0:T(8,128)S(1)}) custom-call(s32[3]{0:T(128)S(1)} %copy-done.74, bf16[256,1536]{1,0:T(8,128)(2,1)S(1)} %copy-done.24, f32[256,1536]{1,0:T(8,128)} %get-tuple-element.186.refs_3_.unit_ref, ...), custom_call_target="tpu_custom_call" | custom-call | flops 805306368 | bytes 8856576 | tf_op jit(solution)/shard_map/attention_weights/pallas_call | solution.py:75
  346.7 5.3 %collective-permute-done.77 = bf16[128,1536]{1,0:T(8,128)(2,1)} collective-permute-done((bf16[128,1536]{1,0:T(8,128)(2,1)}, bf16[128,1536]{1,0:T(8,128)(2,1)}, u32[]{:S(2)}, u32[]{:S(2)}) %collective-permute-start.77) | collective-permute-done | bytes 393248 | tf_op jit(solution)/shard_map/ppermute | solution.py:791
  398.9 7.9 %collective-permute-done.88 = bf16[192,1024]{1,0:T(8,128)(2,1)S(1)} collective-permute-done((bf16[192,1024]{1,0:T(8,128)(2,1)S(1)}, bf16[192,1024]{1,0:T(8,128)(2,1)S(1)}, u32[]{:S(2)}, u32[]{:S(2)}) %collective-permute-start.88) | collective-permute-done | bytes 393248 | tf_op jit(solution)/shard_map/ppermute | solution.py:791
  414.3 6.0 %collective-permute-done.61 = bf16[128,1536]{1,0:T(8,128)(2,1)S(1)} collective-permute-done((bf16[128,1536]{1,0:T(8,128)(2,1)S(1)}, bf16[128,1536]{1,0:T(8,128)(2,1)S(1)}, u32[]{:S(2)}, u32[]{:S(2)}) %collective-permute-start.61) | collective-permute-done | bytes 393248 | tf_op jit(solution)/shard_map/ppermute | solution.py:791
  (446 shorter events, 246.3 us)
Async XLA Ops:
  7.2 91.5 %all-gather.5.cloned.1.call-start = ((), (), s32[]{:S(2)}) async-start(), calls=%async_computation.3 | async-start | bytes 2211840 | tf_op jit(solution)/shard_map/all_gather | solution.py:1191
  9.3 158.6 %all-gather.3.cloned.1.call-start = ((), (), s32[]{:S(2)}) async-start(), calls=%async_computation.2 | async-start | bytes 5308416 | tf_op jit(solution)/shard_map/all_gather | solution.py:1194
  11.5 411.1 %reduce-scatter.5.cloned.1.call-start = ((), (), s32[]{:S(2)}) async-start(), calls=%async_computation.5 | async-start | bytes 2211840 | tf_op jit(solution)/shard_map/reduce_scatter | solution.py:869
  11.6 40.9 %collective-permute-start.18 = (bf16[192,1024]{1,0:T(8,128)(2,1)S(1)}, bf16[192,1024]{1,0:T(8,128)(2,1)S(1)}, u32[]{:S(2)}, u32[]{:S(2)}) collective-permute-start(bf16[192,1024]{1,0:T(8,128)(2,1)S(1)} %pad_maximum_fusion.2.refs_10_), channel_id=1, source_target_pairs={{0,24},{4,28},{8,16},{12,20},{16,8},{20,12},{24,0},{28,4},{1,25},{... | collective-permute-start | bytes 1179656 | tf_op jit(solution)/shard_map/ppermute | solution.py:791
  15.6 37.4 %collective-permute-start.16 = (bf16[192,1024]{1,0:T(8,128)(2,1)S(1)}, bf16[192,1024]{1,0:T(8,128)(2,1)S(1)}, u32[]{:S(2)}, u32[]{:S(2)}) collective-permute-start(bf16[192,1024]{1,0:T(8,128)(2,1)S(1)} %pad_maximum_fusion.2.refs_10_), channel_id=1, source_target_pairs={{0,16},{4,20},{8,24},{12,28},{16,0},{20,4},{24,8},{28,12},{1,17},{... | collective-permute-start | bytes 1179656 | tf_op jit(solution)/shard_map/ppermute | solution.py:791
  16.1 37.0 %collective-permute-start.14 = (bf16[192,1024]{1,0:T(8,128)(2,1)S(1)}, bf16[192,1024]{1,0:T(8,128)(2,1)S(1)}, u32[]{:S(2)}, u32[]{:S(2)}) collective-permute-start(bf16[192,1024]{1,0:T(8,128)(2,1)S(1)} %pad_maximum_fusion.2.refs_10_), channel_id=1, source_target_pairs={{0,8},{4,12},{8,0},{12,4},{16,24},{20,28},{24,16},{28,20},{1,9},{5... | collective-permute-start | bytes 1179656 | tf_op jit(solution)/shard_map/ppermute | solution.py:791
  16.2 35.6 %collective-permute-start.12 = (bf16[64,1536]{1,0:T(8,128)(2,1)S(1)}, bf16[64,1536]{1,0:T(8,128)(2,1)S(1)}, u32[]{:S(2)}, u32[]{:S(2)}) collective-permute-start(bf16[64,1536]{1,0:T(8,128)(2,1)S(1)} %bitcast.125), channel_id=1, source_target_pairs={{3,0},{0,1},{1,2},{2,3},{7,4},{4,5},{5,6},{6,7},{11,8},{8,9},{9,10... | collective-permute-start | bytes 589832 | tf_op jit(solution)/shard_map/ppermute | solution.py:773
  74.0 22.9 %collective-permute-start.37 = (bf16[128,1536]{1,0:T(8,128)(2,1)S(1)}, bf16[128,1536]{1,0:T(8,128)(2,1)S(1)}, u32[]{:S(2)}, u32[]{:S(2)}) collective-permute-start(bf16[128,1536]{1,0:T(8,128)(2,1)S(1)} %bitcast.115), channel_id=1, source_target_pairs={{0,8},{4,12},{8,0},{12,4},{16,24},{20,28},{24,16},{28,20},{1,9},{5... | collective-permute-start | bytes 1179656 | tf_op jit(solution)/shard_map/ppermute | solution.py:791
  74.9 22.9 %collective-permute-start.36 = (bf16[128,1536]{1,0:T(8,128)(2,1)S(1)}, bf16[128,1536]{1,0:T(8,128)(2,1)S(1)}, u32[]{:S(2)}, u32[]{:S(2)}) collective-permute-start(bf16[128,1536]{1,0:T(8,128)(2,1)S(1)} %bitcast.116), channel_id=1, source_target_pairs={{0,4},{4,0},{8,12},{12,8},{16,20},{20,16},{24,28},{28,24},{1,5},{5... | collective-permute-start | bytes 1179656 | tf_op jit(solution)/shard_map/ppermute | solution.py:791
  151.9 28.9 %collective-permute-start.54 = (bf16[128,1536]{1,0:T(8,128)(2,1)S(1)}, bf16[128,1536]{1,0:T(8,128)(2,1)}, u32[]{:S(2)}, u32[]{:S(2)}) collective-permute-start(bf16[128,1536]{1,0:T(8,128)(2,1)S(1)} %bitcast.120), channel_id=1, source_target_pairs={{0,24},{4,28},{8,16},{12,20},{16,8},{20,12},{24,0},{28,4},{1,25},{... | collective-permute-start | bytes 1179656 | tf_op jit(solution)/shard_map/ppermute | solution.py:791
  156.9 24.4 %collective-permute-start.52 = (bf16[128,1536]{1,0:T(8,128)(2,1)S(1)}, bf16[128,1536]{1,0:T(8,128)(2,1)S(1)}, u32[]{:S(2)}, u32[]{:S(2)}) collective-permute-start(bf16[128,1536]{1,0:T(8,128)(2,1)S(1)} %bitcast.121), channel_id=1, source_target_pairs={{0,16},{4,20},{8,24},{12,28},{16,0},{20,4},{24,8},{28,12},{1,17},{... | collective-permute-start | bytes 1179656 | tf_op jit(solution)/shard_map/ppermute | solution.py:791
  239.3 185.3 %reduce-scatter.3.cloned.1.call-start = ((), (), s32[]{:S(2)}) async-start(), calls=%async_computation.4 | async-start | bytes 5308416 | tf_op jit(solution)/shard_map/reduce_scatter | solution.py:865
  245.2 53.9 %collective-permute-start.74 = (bf16[4,128,1536]{2,1,0:T(8,128)(2,1)}, bf16[4,128,1536]{2,1,0:T(8,128)(2,1)}, u32[]{:S(2)}, u32[]{:S(2)}) collective-permute-start(bf16[4,128,1536]{2,1,0:T(8,128)(2,1)} %get-tuple-element.191), channel_id=1, source_target_pairs={{0,4},{4,0},{8,12},{12,8},{16,20},{20,16},{24,28},{28,24},{1,5},{5... | collective-permute-start | bytes 4718600 | tf_op jit(solution)/shard_map/ppermute | solution.py:791
  246.4 25.7 %collective-permute-start.63 = (bf16[64,1536]{1,0:T(8,128)(2,1)S(1)}, bf16[64,1536]{1,0:T(8,128)(2,1)S(1)}, u32[]{:S(2)}, u32[]{:S(2)}) collective-permute-start(bf16[64,1536]{1,0:T(8,128)(2,1)S(1)} %copy-done.23), channel_id=1, source_target_pairs={{2,0},{3,1},{0,2},{1,3},{6,4},{7,5},{4,6},{5,7},{10,8},{11,9},{8,1... | collective-permute-start | bytes 589832 | tf_op jit(solution)/shard_map/ppermute | solution.py:773
  247.9 24.6 %collective-permute-start.62 = (bf16[64,1536]{1,0:T(8,128)(2,1)S(1)}, bf16[64,1536]{1,0:T(8,128)(2,1)S(1)}, u32[]{:S(2)}, u32[]{:S(2)}) collective-permute-start(bf16[64,1536]{1,0:T(8,128)(2,1)S(1)} %copy-done.23), channel_id=1, source_target_pairs={{1,0},{2,1},{3,2},{0,3},{5,4},{6,5},{7,6},{4,7},{9,8},{10,9},{11,1... | collective-permute-start | bytes 589832 | tf_op jit(solution)/shard_map/ppermute | solution.py:773
  277.6 25.8 %collective-permute-start.65 = (bf16[64,1536]{1,0:T(8,128)(2,1)}, bf16[64,1536]{1,0:T(8,128)(2,1)S(1)}, u32[]{:S(2)}, u32[]{:S(2)}) collective-permute-start(bf16[64,1536]{1,0:T(8,128)(2,1)} %get-tuple-element.170), channel_id=1, source_target_pairs={{3,0},{0,1},{1,2},{2,3},{7,4},{4,5},{5,6},{6,7},{11,8},{8,9},{9,10... | collective-permute-start | bytes 589832 | tf_op jit(solution)/shard_map/ppermute | solution.py:773
  317.9 27.1 %collective-permute-start.75 = (bf16[128,1536]{1,0:T(8,128)(2,1)}, bf16[128,1536]{1,0:T(8,128)(2,1)}, u32[]{:S(2)}, u32[]{:S(2)}) collective-permute-start(bf16[128,1536]{1,0:T(8,128)(2,1)} %get-tuple-element.223), channel_id=1, source_target_pairs={{0,8},{4,12},{8,0},{12,4},{16,24},{20,28},{24,16},{28,20},{1,9},{5... | collective-permute-start | bytes 1179656 | tf_op jit(solution)/shard_map/ppermute | solution.py:791
  319.6 32.4 %collective-permute-start.77 = (bf16[128,1536]{1,0:T(8,128)(2,1)}, bf16[128,1536]{1,0:T(8,128)(2,1)}, u32[]{:S(2)}, u32[]{:S(2)}) collective-permute-start(bf16[128,1536]{1,0:T(8,128)(2,1)} %get-tuple-element.224), channel_id=1, source_target_pairs={{0,24},{4,28},{8,16},{12,20},{16,8},{20,12},{24,0},{28,4},{1,25},{... | collective-permute-start | bytes 1179656 | tf_op jit(solution)/shard_map/ppermute | solution.py:791
  321.0 31.4 %collective-permute-start.76 = (bf16[128,1536]{1,0:T(8,128)(2,1)}, bf16[128,1536]{1,0:T(8,128)(2,1)}, u32[]{:S(2)}, u32[]{:S(2)}) collective-permute-start(bf16[128,1536]{1,0:T(8,128)(2,1)} %get-tuple-element.225), channel_id=1, source_target_pairs={{0,16},{4,20},{8,24},{12,28},{16,0},{20,4},{24,8},{28,12},{1,17},{... | collective-permute-start | bytes 1179656 | tf_op jit(solution)/shard_map/ppermute | solution.py:791
  342.0 41.1 %collective-permute-start.85 = (bf16[4,192,1024]{2,1,0:T(8,128)(2,1)}, bf16[4,192,1024]{2,1,0:T(8,128)(2,1)}, u32[]{:S(2)}, u32[]{:S(2)}) collective-permute-start(bf16[4,192,1024]{2,1,0:T(8,128)(2,1)} %get-tuple-element.205), channel_id=1, source_target_pairs={{0,4},{4,0},{8,12},{12,8},{16,20},{20,16},{24,28},{28,24},{1,5},{5... | collective-permute-start | bytes 4718600 | tf_op jit(solution)/shard_map/ppermute | solution.py:791
  360.5 28.4 %collective-permute-start.58 = (bf16[4,128,1536]{2,1,0:T(8,128)(2,1)}, bf16[4,128,1536]{2,1,0:T(8,128)(2,1)}, u32[]{:S(2)}, u32[]{:S(2)}) collective-permute-start(bf16[4,128,1536]{2,1,0:T(8,128)(2,1)} %get-tuple-element.167), channel_id=1, source_target_pairs={{0,4},{4,0},{8,12},{12,8},{16,20},{20,16},{24,28},{28,24},{1,5},{5... | collective-permute-start | bytes 4718600 | tf_op jit(solution)/shard_map/ppermute | solution.py:791
  390.9 23.4 %collective-permute-start.59 = (bf16[128,1536]{1,0:T(8,128)(2,1)S(1)}, bf16[128,1536]{1,0:T(8,128)(2,1)S(1)}, u32[]{:S(2)}, u32[]{:S(2)}) collective-permute-start(bf16[128,1536]{1,0:T(8,128)(2,1)S(1)} %get-tuple-element.226), channel_id=1, source_target_pairs={{0,8},{4,12},{8,0},{12,4},{16,24},{20,28},{24,16},{28,20},{1,9},{5... | collective-permute-start | bytes 1179656 | tf_op jit(solution)/shard_map/ppermute | solution.py:791
  392.7 27.6 %collective-permute-start.61 = (bf16[128,1536]{1,0:T(8,128)(2,1)S(1)}, bf16[128,1536]{1,0:T(8,128)(2,1)S(1)}, u32[]{:S(2)}, u32[]{:S(2)}) collective-permute-start(bf16[128,1536]{1,0:T(8,128)(2,1)S(1)} %get-tuple-element.227), channel_id=1, source_target_pairs={{0,24},{4,28},{8,16},{12,20},{16,8},{20,12},{24,0},{28,4},{1,25},{... | collective-permute-start | bytes 1179656 | tf_op jit(solution)/shard_map/ppermute | solution.py:791
  397.4 24.3 %collective-permute-start.60 = (bf16[128,1536]{1,0:T(8,128)(2,1)S(1)}, bf16[128,1536]{1,0:T(8,128)(2,1)S(1)}, u32[]{:S(2)}, u32[]{:S(2)}) collective-permute-start(bf16[128,1536]{1,0:T(8,128)(2,1)S(1)} %get-tuple-element.228), channel_id=1, source_target_pairs={{0,16},{4,20},{8,24},{12,28},{16,0},{20,4},{24,8},{28,12},{1,17},{... | collective-permute-start | bytes 1179656 | tf_op jit(solution)/shard_map/ppermute | solution.py:791
  (172 other events, 1807.4 us)
Sparse Core Ops, SparseCore 0:
  10.2 43.3 all-gather.4
  56.0 49.2 all-gather.2
  239.4 52.6 reduce-scatter.4
  299.2 69.3 reduce-scatter.2

commit v3 on v2

--- a/solution.py
+++ b/solution.py
@@ -63,7 +63,7 @@
     return jnp.dot(left_side, right_side, preferred_element_type=jnp.float32)
 
 
-def run_kernel(kernel, ins, outs, scalars=None, scratch=(), flops=0, name=None):
+def run_kernel(kernel, ins, outs, scalars=None, scratch=(), flops=0, name=None, spare=8):
     whole = pl.BlockSpec(memory_space=pltpu.VMEM)
     specs = [whole] * len(ins)
     args = list(ins)
@@ -72,13 +72,15 @@
         args = [scalars] + args
     shapes = [jax.ShapeDtypeStruct(shape, dtype) for shape, dtype in outs]
     moved = sum(x.size * x.dtype.itemsize for x in list(ins) + shapes)
+    held = sum(math.prod(x.shape) * jnp.dtype(x.dtype).itemsize for x in scratch)
+    room = 56 * 1024 * 1024
     return pl.pallas_call(
         kernel,
         in_specs=specs,
         out_specs=[whole] * len(shapes),
         out_shape=shapes,
         scratch_shapes=scratch,
-        compiler_params=pltpu.CompilerParams(vmem_limit_bytes=50 * 1024 * 1024),
+        compiler_params=pltpu.CompilerParams(vmem_limit_bytes=room),
         cost_estimate=pl.CostEstimate(flops=flops, bytes_accessed=moved, transcendentals=0),
         name=name,
     )(*args)
@@ -96,9 +98,9 @@
 def attention_forward(where, raw, row_params, rel_turned, blocks, local_heads):
     count, (own, width) = len(raw), raw[0].shape
     length = count * own
-    rows, columns = blocks[0].shape
+    n_blocks, columns = len(blocks), blocks[0].shape[1]
+    rows = width // n_blocks
     keys, values = local_heads * KEYD, local_heads * VALD
-    n_blocks = len(blocks)
 
     def kernel(where_ref, *refs):
         raw_refs, refs = refs[:count], refs[count:]
@@ -110,7 +112,7 @@
         key_out, value_out, mixed_out, total_ref = refs[7:]
         for m in range(n_blocks):
             spot = (where_ref[0] ^ m) * rows if n_blocks > 1 else 0
-            weight_ref[pl.ds(pl.multiple_of(spot, rows), rows), :] = block_refs[m][...]
+            weight_ref[pl.ds(pl.multiple_of(spot, rows), rows), :] = block_refs[m][:rows, :]
         for k in range(count):
             resid = raw_refs[k][...].astype(jnp.float32) + species_ref[...]
             unit, scale = normalize(resid)
@@ -324,10 +326,10 @@
     )
 
 
-def unpack_small(where, blocks, basis_turned, width, local_heads):
-    count, entries = blocks[0].shape
-    n_blocks = len(blocks)
-    total = n_blocks * count
+def unpack_small(where, blocks, basis_turned, width, local_heads, count):
+    half, entries = blocks[0].shape
+    total = 2 * half
+    n_blocks = total // count
     share = width // total
     n_rows = 8 + SPECIES
     group = width // n_blocks
@@ -337,15 +339,16 @@
     length = basis_turned.shape[0]
 
     def kernel(where_ref, *refs):
-        block_refs, basis_ref, refs = refs[:n_blocks], refs[n_blocks], refs[n_blocks + 1 :]
+        block_refs, basis_ref, refs = refs[:2], refs[2], refs[3:]
         row_refs, refs = refs[:5], refs[5:]
         taps_ref, bias_ref, rel_ref, content_ref, position_ref, found_ref, weight_ref = refs
-        for m in range(n_blocks):
-            found_ref[m * count : (m + 1) * count, :] = block_refs[m][...].astype(jnp.float32)
+        for core in range(2):
+            found_ref[core * half : (core + 1) * half, :] = block_refs[core][...].astype(jnp.float32)
 
         def owner(shape):
             spot = lax.broadcasted_iota(jnp.int32, shape, 0)
-            return (spot // count) ^ where_ref[0], lax.rem(spot % count + where_ref[1], count)
+            block = 2 * (spot % half // count) + spot // half
+            return block ^ where_ref[0], lax.rem(spot % count + where_ref[1], count)
 
         def widen(start, size, span):
             column = lax.broadcasted_iota(jnp.int32, (size, span), 1)
@@ -485,14 +488,13 @@
     )[0]
 
 
-def feed_forward_up(normed, weight):
+def feed_forward_up(where, normed, weight):
     count, (own, width) = len(normed), normed[0].shape
     length = count * own
     hidden_count = weight.shape[1] // 2
 
-    def kernel(*refs):
-        normed_refs, weight_ref, own_ref, refs = refs[:count], refs[count], refs[count + 1], refs[count + 2 :]
-        part_refs, (normed_out, hidden_out, slope_out) = refs[: count - 1], refs[count - 1 :]
+    def kernel(where_ref, *refs):
+        normed_refs, (weight_ref, part_ref, normed_out, hidden_out, slope_out) = refs[:count], refs[count:]
         for k in range(count):
             normed_out[k * own : (k + 1) * own, :] = normed_refs[k][...]
         pre = dot_rows(normed_out[...], weight_ref[:, :hidden_count])
@@ -500,21 +502,19 @@
         hidden_out[...] = (pre * below).astype(LOW)
         slope_out[...] = below + pre * jnp.exp(-0.5 * pre * pre) * (1.0 / math.sqrt(2.0 * math.pi))
         total = dot_transposed(hidden_out[...], weight_ref[:, hidden_count:])
-        own_ref[...] = total[:own]
-        for k in range(1, count):
-            part_refs[k - 1][...] = total[k * own : (k + 1) * own].astype(LOW)
-
-    found = run_kernel(
+        for k in range(count):
+            spot = pl.ds(pl.multiple_of(chunk_of(where_ref, k, count) * own, own), own)
+            part_ref[spot, :] = total[k * own : (k + 1) * own].astype(LOW)
+
+    return run_kernel(
         kernel,
         list(normed) + [weight],
-        [((own, width), jnp.float32)]
-        + [((own, width), LOW)] * (count - 1)
-        + [((length, width), LOW), ((length, hidden_count), LOW)]
-        + [((length, hidden_count), jnp.float32)],
+        [((length, width), LOW)] * 2
+        + [((length, hidden_count), LOW), ((length, hidden_count), jnp.float32)],
+        scalars=where,
         flops=4 * length * width * hidden_count,
         name="feed_forward_up",
     )
-    return found[:count], found[count:]
 
 
 def feed_forward_back(grads, slope, weight):
@@ -546,21 +546,29 @@
     return found[:count], found[count:]
 
 
-def feed_forward_weights(normed_all, grad_all, hidden, grad_pre):
+def feed_forward_weights(where, normed_all, grad_all, hidden, grad_pre, n_blocks):
     width = normed_all.shape[1]
     hidden_count = hidden.shape[1]
-
-    def kernel(normed_ref, grad_ref, hidden_ref, pre_ref, out_ref):
-        out_ref[:, :hidden_count] = dot_leading(normed_ref[...], pre_ref[...]).astype(LOW)
-        out_ref[:, hidden_count:] = dot_leading(grad_ref[...], hidden_ref[...]).astype(LOW)
-
+    rows = width // n_blocks
+
+    def kernel(where_ref, normed_ref, grad_ref, hidden_ref, pre_ref, even_ref, odd_ref, whole_ref):
+        whole_ref[:, :hidden_count] = dot_leading(normed_ref[...], pre_ref[...]).astype(LOW)
+        whole_ref[:, hidden_count:] = dot_leading(grad_ref[...], hidden_ref[...]).astype(LOW)
+        for m in range(n_blocks):
+            spot = (where_ref[0] ^ m) * rows if n_blocks > 1 else 0
+            half = odd_ref if m % 2 else even_ref
+            half[m // 2] = whole_ref[pl.ds(pl.multiple_of(spot, rows), rows), :]
+
+    half = max(n_blocks // 2, 1)
     return run_kernel(
         kernel,
         [normed_all, grad_all, hidden, grad_pre],
-        [((width, 2 * hidden_count), LOW)],
+        [((half, rows, 2 * hidden_count), LOW)] * 2,
+        scalars=where,
+        scratch=[pltpu.VMEM((width, 2 * hidden_count), LOW)],
         flops=4 * normed_all.shape[0] * width * hidden_count,
         name="feed_forward_weights",
-    )[0]
+    )
 
 
 def shifted(rows, first, last):
@@ -571,24 +579,21 @@
     return before, after
 
 
-def group_weight(weight_ref, which, count, scratch_ref):
-    share = weight_ref.shape[0] // (3 * count)
-    for t in range(count):
-        spot = (3 * t + which) * share
-        scratch_ref[t * share : (t + 1) * share, :] = weight_ref[spot : spot + share, :]
-
-
 def section_grad_deep(blocks, weight, count):
     fine, width = blocks[0].shape
     channels = weight.shape[0] // 3
+    share = channels // count
     windows = len(blocks)
 
     def kernel(*refs):
-        block_refs, refs = refs[:windows], refs[windows:]
-        weight_ref, deep_ref, head_ref, tail_ref, point_ref = refs
-        group_weight(weight_ref, 0, count, point_ref)
+        block_refs, weight_ref, refs = refs[:windows], refs[windows], refs[windows + 1 :]
+        deep_ref, head_ref, tail_ref, *whole_refs = refs
+        for which, ref in enumerate(whole_refs):
+            for t in range(count):
+                spot = (3 * t + which) * share
+                ref[t * share : (t + 1) * share, :] = weight_ref[spot : spot + share, :]
         for m in range(windows):
-            deep = dot_transposed(block_refs[m][...], point_ref[...]).astype(LOW)
+            deep = dot_transposed(block_refs[m][...], whole_refs[0][...]).astype(LOW)
             deep_ref[m] = deep
             head_ref[m : m + 1, :] = deep[:1]
             tail_ref[m : m + 1, :] = deep[fine - 1 :]
@@ -596,21 +601,21 @@
     return run_kernel(
         kernel,
         list(blocks) + [weight],
-        [((windows, fine, channels), LOW)] + [((windows, channels), LOW)] * 2,
-        scratch=[pltpu.VMEM((channels, width), LOW)],
+        [((windows, fine, channels), LOW)]
+        + [((windows, channels), LOW)] * 2
+        + [((channels, width), LOW)] * 3,
         flops=2 * windows * fine * width * channels,
         name="section_grad_deep",
     )
 
 
-def section_grad_mix(deep, before, after, taps, weight, count):
+def section_grad_mix(deep, before, after, taps, up):
     windows, fine, channels = deep.shape
-    width = weight.shape[1]
+    width = up.shape[1]
     own = fine // 2
 
-    def kernel(deep_ref, before_ref, after_ref, taps_ref, weight_ref, *refs):
-        mix_ref, coarse_ref, even_ref, odd_ref, bias_ref, up_ref = refs
-        group_weight(weight_ref, 1, count, up_ref)
+    def kernel(deep_ref, before_ref, after_ref, taps_ref, up_ref, *refs):
+        mix_ref, coarse_ref, even_ref, odd_ref, bias_ref = refs
         row = lax.broadcasted_iota(jnp.int32, (own, fine), 0)
         column = lax.broadcasted_iota(jnp.int32, (own, fine), 1)
         pool = (column // 2 == row).astype(jnp.float32).astype(LOW)
@@ -635,47 +640,42 @@
 
     return run_kernel(
         kernel,
-        [deep, before, after, taps, weight],
+        [deep, before, after, taps, up],
         [((windows, fine, channels), LOW), ((windows, own, channels), LOW)]
         + [((windows // 2, own, width), LOW)] * 2
         + [((1, channels), jnp.float32)],
-        scratch=[pltpu.VMEM((channels, width), LOW)],
         flops=2 * windows * own * width * channels,
         name="section_grad_mix",
     )
 
 
-def section_grad_encoder(mix, weight, count):
+def section_grad_encoder(mix, lateral):
     windows, fine, channels = mix.shape
-    width = weight.shape[1]
-
-    def kernel(mix_ref, weight_ref, even_ref, odd_ref, lateral_ref):
-        group_weight(weight_ref, 2, count, lateral_ref)
+    width = lateral.shape[1]
+
+    def kernel(mix_ref, lateral_ref, even_ref, odd_ref):
         for m in range(windows):
             half = odd_ref if m % 2 else even_ref
             half[m // 2] = dot_rows(mix_ref[m], lateral_ref[...]).astype(LOW)
 
     return run_kernel(
         kernel,
-        [mix, weight],
+        [mix, lateral],
         [((windows // 2, fine, width), LOW)] * 2,
-        scratch=[pltpu.VMEM((channels, width), LOW)],
         flops=2 * windows * fine * width * channels,
         name="section_grad_encoder",
     )
 
 
-def section_mixture(coarse_blocks, fine_blocks, weight, bias, count):
-    fine, width = fine_blocks[0].shape
-    own = fine // 2
-    channels = weight.shape[0] // 3
-    windows = len(fine_blocks)
+def section_mixture(coarse_blocks, fine_blocks, up, lateral, bias):
+    own, width = coarse_blocks[0].shape
+    fine = 2 * own
+    channels = lateral.shape[0]
+    windows = len(coarse_blocks)
 
     def kernel(*refs):
         coarse_refs, fine_refs, refs = refs[:windows], refs[windows : 2 * windows], refs[2 * windows :]
-        weight_ref, bias_ref, mix_ref, head_ref, tail_ref, up_ref, lateral_ref = refs
-        group_weight(weight_ref, 1, count, up_ref)
-        group_weight(weight_ref, 2, count, lateral_ref)
+        up_ref, lateral_ref, bias_ref, mix_ref, head_ref, tail_ref = refs
         row = lax.broadcasted_iota(jnp.int32, (fine, own), 0)
         column = lax.broadcasted_iota(jnp.int32, (fine, own), 1)
         repeat = (row // 2 == column).astype(jnp.float32).astype(LOW)
@@ -692,21 +692,19 @@
 
     return run_kernel(
         kernel,
-        list(coarse_blocks) + list(fine_blocks) + [weight, bias],
+        list(coarse_blocks) + list(fine_blocks) + [up, lateral, bias],
         [((windows, fine, channels), LOW)] + [((windows, channels), LOW)] * 2,
-        scratch=[pltpu.VMEM((channels, width), LOW)] * 2,
         flops=4 * windows * fine * width * channels,
         name="section_mixture",
     )
 
 
-def section_deep(mix, before, after, taps, weight, grad_deep, count):
+def section_deep(mix, before, after, taps, point, grad_deep):
     windows, fine, channels = mix.shape
-    width = weight.shape[1]
-
-    def kernel(mix_ref, before_ref, after_ref, taps_ref, weight_ref, grad_ref, *refs):
-        deep_ref, even_ref, odd_ref, sums_ref, point_ref = refs
-        group_weight(weight_ref, 0, count, point_ref)
+    width = point.shape[1]
+
+    def kernel(mix_ref, before_ref, after_ref, taps_ref, point_ref, grad_ref, *refs):
+        deep_ref, even_ref, odd_ref, sums_ref = refs
         sums = [jnp.zeros((1, channels), jnp.float32)] * 3
         for m in range(windows):
             rows = mix_ref[m].astype(jnp.float32)
@@ -731,11 +729,10 @@
 
     return run_kernel(
         kernel,
-        [mix, before, after, taps, weight, grad_deep],
+        [mix, before, after, taps, point, grad_deep],
         [((windows, fine, channels), LOW)]
         + [((windows // 2, fine, width), LOW)] * 2
         + [((3, channels), jnp.float32)],
-        scratch=[pltpu.VMEM((channels, width), LOW)],
         flops=2 * windows * fine * width * channels,
         name="section_deep",
     )
@@ -791,70 +788,47 @@
     return lax.ppermute(cells, "dp", [(i, i ^ mask) for i in range(count)])
 
 
-def direct_dp():
-    return lax.axis_size("dp") == 8
-
-
-def gather_blocks(shard):
-    blocks = {0: shard, 1: dp_flip(shard, 1)}
-    for mask in (2, 4, 6):
-        blocks[mask] = dp_flip(shard, mask)
-    for mask in (2, 4, 6):
-        blocks[mask + 1] = dp_flip(blocks[mask], 1)
-    return [blocks[mask] for mask in range(8)]
-
-
-def gather_rows(shard):
-    if not direct_dp():
-        return lax.all_gather(shard, "dp", axis=0, tiled=True)
-    return jnp.concatenate(gather_blocks(shard), axis=0)
-
-
-def scatter_halves(even, odd):
-    if not direct_dp():
-        return lax.psum_scatter(even[0], "dp", scatter_dimension=0, tiled=True).astype(jnp.float32)
-    pairs = even.astype(jnp.float32) + dp_flip(odd, 1).astype(jnp.float32)
-    total = pairs[0]
-    for chip in range(1, even.shape[0]):
-        total = total + dp_flip(pairs[chip].astype(even.dtype), 2 * chip).astype(jnp.float32)
-    return total
-
-
-def scatter_rows(parts):
-    if not direct_dp():
-        return lax.psum_scatter(parts, "dp", scatter_dimension=0, tiled=True).astype(jnp.float32)
-    blocks = parts.reshape(8, -1, parts.shape[1])
-    pairs = {
-        mask: blocks[mask].astype(jnp.float32)
-        + dp_flip(blocks[mask + 1], 1).astype(jnp.float32)
-        for mask in (2, 4, 6, 0)
-    }
-    total = pairs[0]
-    for mask in (2, 4, 6):
-        total = total + dp_flip(pairs[mask].astype(parts.dtype), mask).astype(jnp.float32)
-    return total
-
-
-def gather_true(shard):
-    if not direct_dp():
-        return lax.all_gather(shard, "dp", axis=0, tiled=True)
-    me = lax.axis_index("dp")
-    rows = shard.shape[0]
-    whole = jnp.zeros((8 * rows, shard.shape[1]), shard.dtype)
-    for mask, block in enumerate(gather_blocks(shard)):
-        whole = lax.dynamic_update_slice(whole, block, ((me ^ mask) * rows, 0))
-    return whole
-
-
-def scatter_true(whole):
-    if not direct_dp():
-        return lax.psum_scatter(whole, "dp", scatter_dimension=0, tiled=True).astype(jnp.float32)
-    me = lax.axis_index("dp")
-    rows = whole.shape[0] // 8
-    blocks = [
-        lax.dynamic_slice_in_dim(whole, (me ^ mask) * rows, rows, 0) for mask in range(8)
-    ]
-    return scatter_rows(jnp.concatenate(blocks, axis=0))
+def half_rows(cells, axis=0):
+    return cells.shape[axis] // 32 * 16
+
+
+def both_cores(*chips):
+    return [block for chip in chips for block in (chip, dp_flip(chip, 1))]
+
+
+def chips_of(shard):
+    return [shard] + [dp_flip(shard, mask) for mask in (2, 4, 6)]
+
+
+def send_sum(cells, mask, dtype):
+    return dp_flip(cells.astype(dtype), mask).astype(jnp.float32)
+
+
+def core_pairs(even, odd):
+    return even.astype(jnp.float32) + dp_flip(odd, 1).astype(jnp.float32)
+
+
+def corner_sums(pairs, dtype):
+    half = half_rows(pairs, 1)
+    return send_sum(pairs[3, :half], 2, dtype), send_sum(pairs[3, half:], 4, dtype)
+
+
+def chip_sums(pairs, corners, dtype):
+    half = half_rows(pairs, 1)
+    near = jnp.concatenate([pairs[1, :half], pairs[1, half:] + corners[1]], axis=0)
+    far = jnp.concatenate([pairs[2, :half] + corners[0], pairs[2, half:]], axis=0)
+    return pairs[0] + send_sum(near, 2, dtype) + send_sum(far, 4, dtype)
+
+
+def direct_sums(pairs, dtype):
+    return pairs[0] + sum(send_sum(pairs[chip], 2 * chip, dtype) for chip in (1, 2, 3))
+
+
+def scatter_halves(even, odd, small=False):
+    pairs, dtype = core_pairs(even, odd), even.dtype
+    if small:
+        return direct_sums(pairs, dtype)
+    return chip_sums(pairs, corner_sums(pairs, dtype), dtype)
 
 
 def gather_dp(shard):
@@ -870,22 +844,12 @@
 
 
 def gather_small(cells):
-    count = lax.axis_size("tensor")
-    line = jnp.stack([cells] + [from_ahead(cells, k) for k in range(1, count)], axis=0)
-    if not direct_dp():
-        line = jnp.roll(line, lax.axis_index("tensor"), 0)
-        return lax.all_gather(line, "dp", axis=0)
-    spots = jnp.arange(8 * count, dtype=jnp.int32)
-    source = (spots // count ^ lax.axis_index("dp")) * count + (
-        spots % count - lax.axis_index("tensor")
-    ) % count
-    found = jnp.concatenate(gather_blocks(line), axis=0)
-    chosen = (source[:, None] == spots[None, :]).astype(LOW)
-    return dot_plain(chosen, found).astype(LOW).reshape(8, count, -1)
-
-
-def after(cells, *done):
-    return lax.optimization_barrier((cells, done))[0]
+    line = jnp.stack(spread_blocks(cells), axis=0)
+    return lax.all_gather(jnp.roll(line, lax.axis_index("tensor"), 0), "dp", axis=0)
+
+
+def join(*arrays):
+    return lax.optimization_barrier(arrays)
 
 
 def edges(head, tail):
@@ -1019,8 +983,8 @@
         shift_vals[1:],
     )
 
-    contract_parts, (normed_two_all, hidden_low, slope) = feed_forward_up(
-        spread_blocks(normed_two), w_ffn
+    contract_part, normed_two_all, hidden_low, slope = feed_forward_up(
+        where, spread_blocks(normed_two), w_ffn
     )
     ffn_parts, (grad_ffn_all, grad_hidden_pre) = feed_forward_back(grad_ffn, slope, w_ffn)
     grad_resid_one, grad_attn, sums_two = second_norm_back(
@@ -1032,9 +996,7 @@
         grad_resid_two,
     )
 
-    resid_two = resid_one + contract_parts[0]
-    for block in collect_blocks(contract_parts[1:]):
-        resid_two = resid_two + block.astype(jnp.float32)
+    resid_two = resid_one + scatter_tensor(contract_part).astype(jnp.float32)
     section_all = gather_dp(resid_two.astype(LOW))
     coarse = dot_transposed(section_all, w_up).reshape(windows, own, channels)
     section_mix = (
@@ -1069,7 +1031,9 @@
     section_cols = scatter_tensor(section_cols)[0].astype(jnp.float32)
 
     ffn_out = scatter_dp(
-        feed_forward_weights(normed_two_all, grad_ffn_all, hidden_low, grad_hidden_pre)
+        feed_forward_weights(
+            where, normed_two_all, grad_ffn_all, hidden_low, grad_hidden_pre, 1
+        )[0][0]
     ).astype(jnp.float32)
 
     head_parts, (grad_attn_all, grad_heads, grad_normed_part, bias_sums, rel_grad) = (
@@ -1182,20 +1146,21 @@
             position_bias.T.reshape(-1),
         ]
     )[None]
-    line = jnp.concatenate(spread_blocks(packed), axis=0)
-    raw = spread_blocks(activations[0])
     attn_shard = jnp.concatenate([query_weight, key_weight, value_weight, output_weight.T], axis=1)
-    attn_blocks = gather_blocks(attn_shard)
-    small_blocks = gather_blocks(line)
+    attn_chips = chips_of(attn_shard)
+    line = spread_blocks(packed)
     section_shard = jnp.concatenate([pointwise_weight, upsample_weight.T, lateral_weight.T], axis=0)
     w_section = lax.all_gather(section_shard, "tensor", axis=0, tiled=True)
-    small_blocks, raw, attn_blocks = lax.optimization_barrier((small_blocks, raw, attn_blocks))
-    ffn_shard = jnp.concatenate([expand_weight, contract_weight.T], axis=1)
-    w_ffn = lax.all_gather(ffn_shard, "dp", axis=0, tiled=True)
-
+    line, rows = join(line, activations[0])
+    raw = spread_blocks(rows)
+    small_chips = jnp.concatenate(chips_of(jnp.concatenate(line, axis=0)), axis=0)
+    small_blocks = [small_chips, dp_flip(small_chips, 1)]
+    attn_blocks = both_cores(*attn_chips)
+    attn_blocks, small_blocks, raw, cot = join(attn_blocks, small_blocks, raw, cotangent[0])
+    cot_chips = chips_of(cot)
     basis_turned = jnp.pad(basis_table(length, BASIS).astype(LOW)[::-1], ((0, 1), (0, 0)))
     rows, (depth_taps, bias_section, rel_turned, content_flat, position_flat) = unpack_small(
-        where, small_blocks, basis_turned, width, local_heads
+        where, small_blocks, basis_turned, width, local_heads, count
     )
     gain_one, gain_two, shift_one, shift_two, species_row = rows
     attn_parts, saved = attention_forward(
@@ -1206,63 +1171,78 @@
         attn_blocks,
         local_heads,
     )
+    attn_parts, cot_chips = join(attn_parts, cot_chips)
+
     attn_received = collect_blocks(attn_parts[1:])
-
-    cot_blocks = gather_blocks(after(cotangent[0], attn_blocks))
-    grad_deep, head, tail = section_grad_deep(cot_blocks, w_section, count)
+    cot_blocks = both_cores(*cot_chips)
+    grad_deep, head, tail, w_point, w_up, w_lateral = section_grad_deep(
+        cot_blocks, w_section, count
+    )
     before, following = edges(head, tail)
-    grad_mix, grad_coarse, even, odd, bias_grad = section_grad_mix(
-        grad_deep, before, following, depth_taps, w_section, count
-    )
-    grad_resid_two = scatter_halves(even, odd)
-    grad_ffn = spread_blocks(grad_resid_two.astype(LOW))
+    attn_received, before, following, expand, contract = join(
+        attn_received, before, following, expand_weight, contract_weight
+    )
 
     resid_one, unit_two, scale_two, normed_two = second_norm(
         attn_parts[0], attn_received, [raw[0], species_row], gain_two, shift_two
     )
-    contract_parts, (normed_two_all, hidden_low, slope) = feed_forward_up(
-        spread_blocks(normed_two), w_ffn
-    )
+    normed_two, before, following, expand, contract = join(
+        normed_two, before, following, expand, contract
+    )
+    w_ffn = gather_dp(jnp.concatenate([expand, contract.T], axis=1))
+    normed_blocks = spread_blocks(normed_two)
+    grad_mix, grad_coarse, even, odd, bias_grad = section_grad_mix(
+        grad_deep, before, following, depth_taps, w_up
+    )
+    grad_resid_two = direct_sums(core_pairs(even, odd), LOW)
+    normed_blocks, grad_resid_two, enc = join(normed_blocks, grad_resid_two, encoder[0])
+
+    grad_ffn = spread_blocks(grad_resid_two.astype(LOW))
+    contract_part, normed_two_all, hidden_low, slope = feed_forward_up(where, normed_blocks, w_ffn)
+    enc_chips = chips_of(enc)
+    grad_ffn, contract_part, enc_chips = join(grad_ffn, contract_part, enc_chips)
+
+    contract_sum = scatter_tensor(contract_part)
+    enc_blocks = both_cores(*enc_chips)
     ffn_parts, (grad_ffn_all, grad_hidden_pre) = feed_forward_back(grad_ffn, slope, w_ffn)
+    ffn_received = collect_blocks(ffn_parts[1:])
+    ffn_grads = feed_forward_weights(
+        where, normed_two_all, grad_ffn_all, hidden_low, grad_hidden_pre, 1
+    )[0][0]
+    enc_pairs = core_pairs(*section_grad_encoder(grad_mix, w_lateral))
+    coarse_chips = chips_of((resid_one + contract_sum.astype(jnp.float32)).astype(LOW))
+    ffn_received, ffn_grads, enc_pairs, enc_blocks, coarse_chips = join(
+        ffn_received, ffn_grads, enc_pairs, enc_blocks, coarse_chips
+    )
+
     grad_resid_one, grad_attn, sums_two = second_norm_back(
-        ffn_parts[0], collect_blocks(ffn_parts[1:]), unit_two, scale_two, gain_two, grad_resid_two
-    )
-
-    enc_blocks = gather_blocks(after(encoder[0], grad_resid_two))
-    resid_two = resid_one + contract_parts[0]
-    for block in collect_blocks(contract_parts[1:]):
-        resid_two = resid_two + block.astype(jnp.float32)
-    section_blocks = gather_blocks(resid_two.astype(LOW))
+        ffn_parts[0], ffn_received, unit_two, scale_two, gain_two, grad_resid_two
+    )
+    grad_attn, ffn_grads, coarse_chips = join(grad_attn, ffn_grads, coarse_chips)
+    grad_attn_blocks = spread_blocks(grad_attn)
+    ffn_out = scatter_dp(ffn_grads).astype(jnp.float32)
+    encoder_grad = chip_sums(enc_pairs, corner_sums(enc_pairs, LOW), LOW)
+    coarse_blocks = both_cores(*coarse_chips)
     section_mix, head, tail = section_mixture(
-        section_blocks, enc_blocks, w_section, bias_section, count
+        coarse_blocks, enc_blocks, w_up, w_lateral, bias_section
     )
     before, following = edges(head, tail)
-    deep_rows, out_even, out_odd, taps_grad = section_deep(
-        section_mix, before, following, depth_taps, w_section, grad_deep, count
-    )
-    encoder_grad = scatter_halves(*section_grad_encoder(grad_mix, w_section, count))
-    section_out = scatter_halves(out_even, out_odd).astype(LOW)
-    section_cols = section_weights(
-        deep_rows, grad_coarse, grad_mix, cot_blocks, section_blocks, enc_blocks, count
-    )
-    section_cols = scatter_tensor(section_cols)[0].astype(jnp.float32)
-    ffn_out = scatter_dp(
-        feed_forward_weights(normed_two_all, grad_ffn_all, hidden_low, grad_hidden_pre)
-    ).astype(jnp.float32)
+    grad_attn_blocks, encoder_grad, before, following = join(
+        grad_attn_blocks, encoder_grad, before, following
+    )
 
     head_parts, (grad_attn_all, grad_heads, grad_normed_part, bias_sums, rel_grad) = (
         attention_backward(
-            where, spread_blocks(grad_attn), saved, rel_turned, basis_turned, local_heads
+            where, grad_attn_blocks, saved, rel_turned, basis_turned, local_heads
         )
     )
-    grad_resid_in = first_norm_back(
-        where,
-        head_parts[0],
-        collect_blocks(head_parts[1:]),
-        saved[2],
-        saved[3],
-        gain_one,
-        grad_resid_one,
+    head_parts, before, following = join(head_parts, before, following)
+    head_received = collect_blocks(head_parts[1:])
+    deep_rows, out_even, out_odd, taps_grad = section_deep(
+        section_mix, before, following, depth_taps, w_point, grad_deep
+    )
+    cols_part = section_weights(
+        deep_rows, grad_coarse, grad_mix, cot_blocks, coarse_blocks, enc_blocks, count
     )
     even, odd, small_even, small_odd = attention_weights(
         where,
@@ -1276,8 +1256,17 @@
         rel_grad,
         len(attn_blocks),
     )
-    small_out = scatter_halves(small_even, small_odd)
+    head_received, ffn_out, out_even, out_odd, even, odd, small_even, small_odd, cols_part = join(
+        head_received, ffn_out, out_even, out_odd, even, odd, small_even, small_odd, cols_part
+    )
+
+    section_cols = scatter_tensor(cols_part)[0].astype(jnp.float32)
+    grad_resid_in = first_norm_back(
+        where, head_parts[0], head_received, saved[2], saved[3], gain_one, grad_resid_one
+    )
+    section_out = scatter_halves(out_even, out_odd).astype(LOW)
     attn_out = scatter_halves(even, odd)
+    small_out = scatter_halves(small_even, small_odd, small=True)
 
     n_norm = 4 + SPECIES
     group = share * count

time: 435 us -> 364 us (0.84)
  starting transfers between devices: 137 us -> 97.8 us
  waiting for transfers between devices: 160 us -> 133 us
  local copies, waits for them, and re-layouts: 35.1 us -> 14.6 us
  Pallas kernels: 65.1 us -> 83 us
    ppermute x30 -> x27, starting transfers between devices: 80.1 us -> 41.5 us  [from_ahead(): lax.ppermute(rows, 'tensor', [((i + step) % count, i) for i in range(coun...]
    ppermute x55, waiting for transfers between devices: 73.6 us -> 43.3 us  [dp_flip(): return lax.ppermute(cells, 'dp', [(i, i ^ mask) for i in range(count)])]
    ppermute x30 -> x27, waiting for transfers between devices: 79.8 us -> 52.2 us  [from_ahead(): lax.ppermute(rows, 'tensor', [((i + step) % count, i) for i in range(coun...]
    reduce_scatter x1 -> x2, waiting for transfers between devices: 0.01 us -> 22.2 us  [scatter_tensor(): return lax.psum_scatter(whole, 'tensor', scatter_dimension=0, tiled=True)]
    unnamed x207 -> x151, local copies, waits for them, and re-layouts: 23.2 us -> 4.26 us
    pallas_call x16, Pallas kernels: 65.1 us -> 83 us  [run_kernel(): pl.pallas_call(kernel, in_specs=specs, out_specs=[whole] * len(shapes), o...]
    all_gather x1, waiting for transfers between devices: 0.01 us -> 12.4 us  [gather_dp(): return lax.all_gather(shard, 'dp', axis=0, tiled=True)]
  transfers between devices with their start and end apart: 93 -> 91, of which waited for: 43 -> 39; matrix products, arithmetic and copies ran while one was open for 6% -> 7% of each run, Pallas kernels for 11% -> 21%
where the time goes in v3:
time: 364 us
  waiting for transfers between devices  133 us (37%)
  starting transfers between devices  97.8 us (27%)
  Pallas kernels  83 us (23%)
  other arithmetic  20.2 us (6%)
  between operations  15.6 us (4%)
  local copies, waits for them, and re-layouts  14.6 us (4%)
    pallas_call x16, Pallas kernels, run_kernel(): pl.pallas_call(kernel, in_specs=specs, out_specs=[whole] * len(shapes), o...  83 us
    ppermute x27, waiting for transfers between devices, from_ahead(): lax.ppermute(rows, 'tensor', [((i + step) % count, i) for i in range(coun...  52.2 us
    ppermute x55, starting transfers between devices, dp_flip(): return lax.ppermute(cells, 'dp', [(i, i ^ mask) for i in range(count)])  46.3 us
    ppermute x55, waiting for transfers between devices, dp_flip(): return lax.ppermute(cells, 'dp', [(i, i ^ mask) for i in range(count)])  43.3 us
    ppermute x27, starting transfers between devices, from_ahead(): lax.ppermute(rows, 'tensor', [((i + step) % count, i) for i in range(coun...  41.5 us
    reduce_scatter x2, waiting for transfers between devices, scatter_tensor(): return lax.psum_scatter(whole, 'tensor', scatter_dimension=0, tiled=True)  22.2 us
    all_gather x1, waiting for transfers between devices, gather_dp(): return lax.all_gather(shard, 'dp', axis=0, tiled=True)  12.4 us
  transfers between devices with their start and end apart: 91, of which 39 were waited for; matrix products, arithmetic and copies ran while one was open for 7% of the time, Pallas kernels for 21%

profile of v3, /device:TPU:0, one launch (start us, length us, event | category | flops | bytes accessed | tf_op | source)
XLA Modules:
  0.0 363.7 jit_solution(6846914389182227519)
XLA Ops:
  15.8 4.1 %collective-permute-start.7 = (bf16[1,1024]{1,0:T(2,128)(2,1)S(1)}, bf16[1,1024]{1,0:T(2,128)(2,1)S(1)}, u32[]{:S(2)}, u32[]{:S(2)}) collective-permute-start(bf16[1,1024]{1,0:T(2,128)(2,1)S(1)} %broadcast_in_dim.12), channel_id=1, source_target_pairs={{1,0},{2,1},{3,2},{0,3},{5,4},{6,5},{7,6},{4,7},{9,8},{10,9},{11,1... | collective-permute-start | bytes 6152 | tf_op jit(solution)/shard_map/ppermute | solution.py:770
  44.6 19.9 %collective-permute-done.15.refs_2_ = bf16[64,1536]{1,0:T(8,128)(2,1)S(1)} collective-permute-done((bf16[64,1536]{1,0:T(8,128)(2,1)S(1)}, bf16[64,1536]{1,0:T(8,128)(2,1)S(1)}, u32[]{:S(2)}, u32[]{:S(2)}) %collective-permute-start.15) | collective-permute-done | bytes 196640 | tf_op jit(solution)/shard_map/ppermute | solution.py:770
  65.2 8.6 %collective-permute-done.16.refs_3_ = bf16[64,1536]{1,0:T(8,128)(2,1)S(1)} collective-permute-done((bf16[64,1536]{1,0:T(8,128)(2,1)S(1)}, bf16[64,1536]{1,0:T(8,128)(2,1)S(1)}, u32[]{:S(2)}, u32[]{:S(2)}) %collective-permute-start.16) | collective-permute-done | bytes 196640 | tf_op jit(solution)/shard_map/ppermute | solution.py:770
  83.1 7.9 %attention_forward.1 = (f32[64,1536]{1,0:T(8,128)}, bf16[64,1536]{1,0:T(8,128)(2,1)}, bf16[64,1536]{1,0:T(8,128)(2,1)}, bf16[64,1536]{1,0:T(8,128)(2,1)}, bf16[1...) custom-call(s32[3]{0:T(128)} %pad_add_fusion.where_ref, ...), custom_call_target="tpu_custom_call" | custom-call | flops 805306368 | bytes 11815936 | tf_op jit(solution)/shard_map/attention_forward/pallas_call | solution.py:77
  100.5 5.2 %section_grad_deep.1 = (bf16[8,128,192]{2,1,0:T(8,128)(2,1)}, bf16[8,192]{1,0:T(8,128)(2,1)}, bf16[8,192]{1,0:T(8,128)(2,1)}, bf16[192,1536]{1,0:T(8,128)(2,1)},...) custom-call(bf16[128,1536]{1,0:T(8,128)(2,1)} %bitcast.139, bf16[128,1536]{1,0:T(8,128)(2,1)} %copy-done.11, ...), custom_call_target="tpu_custom_call" | custom-call | flops 603979776 | bytes 7084032 | tf_op jit(solution)/shard_map/section_grad_deep/pallas_call | solution.py:77
  118.3 4.3 %section_grad_mix.1 = (bf16[8,128,192]{2,1,0:T(8,128)(2,1)}, bf16[8,64,192]{2,1,0:T(8,128)(2,1)}, bf16[4,64,1536]{2,1,0:T(8,128)(2,1)}, bf16[4,64,1536]{2,1,0:T(8,128)(2,1)}, f32[1,192]{1,0:T(1,128)}) custom-call(bf16[8,128,192]{2,1,0:T(8,128)(2,1)} %get-tuple-element.248.deep_ref.grad_ref, bf16[8,192]{1,0:T(8,128)(2,1)} %copy-done.60, ...), custom_call_target="tpu_custom_call" | custom-call | flops 301989888 | bytes 3154944 | tf_op jit(solution)/shard_map/section_grad_mix/pallas_call | solution.py:77
  139.2 3.8 %collective-permute-start.31 = (bf16[64,1536]{1,0:T(8,128)(2,1)S(1)}, bf16[64,1536]{1,0:T(8,128)(2,1)S(1)}, u32[]{:S(2)}, u32[]{:S(2)}) collective-permute-start(bf16[64,1536]{1,0:T(8,128)(2,1)S(1)} %copy-done.39), channel_id=1, source_target_pairs={{3,0},{0,1},{1,2},{2,3},{7,4},{4,5},{5,6},{6,7},{11,8},{8,9},{9,10... | collective-permute-start | bytes 589832 | tf_op jit(solution)/shard_map/ppermute | solution.py:770
  144.7 8.2 %collective-permute-done.30.refs_2_ = bf16[64,1536]{1,0:T(8,128)(2,1)S(1)} collective-permute-done((bf16[64,1536]{1,0:T(8,128)(2,1)S(1)}, bf16[64,1536]{1,0:T(8,128)(2,1)S(1)}, u32[]{:S(2)}, u32[]{:S(2)}) %collective-permute-start.30) | collective-permute-done | bytes 196640 | tf_op jit(solution)/shard_map/ppermute | solution.py:770
  159.7 3.9 %section_grad_encoder.1 = (bf16[4,128,1536]{2,1,0:T(8,128)(2,1)}, bf16[4,128,1536]{2,1,0:T(8,128)(2,1)}) custom-call(bf16[8,128,192]{2,1,0:T(8,128)(2,1)} %get-tuple-element.278.mix_ref, bf16[192,1536]{1,0:T(8,128)(2,1)} %get-tuple-element.279.lateral_ref.refs_17_), custom_call_target="tpu_custom_call" | custom-call | flops 603979776 | bytes 4128768 | tf_op jit(solution)/shard_map/section_grad_encoder/pallas_call | solution.py:77
  163.6 12.4 %all-gather.5.cloned.1.call-done.refs_4_.refs_5_ = bf16[1536,1536]{1,0:T(8,128)(2,1)} async-done(((bf16[192,1536]{1,0:T(8,128)(2,1)}), bf16[1536,1536]{1,0:T(8,128)(2,1)}) %all-gather.5.cloned.1.call-update) | async-done | bytes 4718608 | tf_op jit(solution)/shard_map/all_gather | solution.py:835
  176.1 5.5 %feed_forward_up.1 = (bf16[256,1536]{1,0:T(8,128)(2,1)}, bf16[256,1536]{1,0:T(8,128)(2,1)}, bf16[256,768]{1,0:T(8,128)(2,1)}, f32[256,768]{1,0:T(8,128)}) custom-call(s32[3]{0:T(128)} %pad_add_fusion.where_ref, bf16[64,1536]{1,0:T(8,128)(2,1)} %get-tuple-element.256.refs_0_, bf16[64,1536]{1,0:T(8,128)(2,1)} %copy-done.43, bf16[64,1536]{1,0:T(8,128)(2,1)} %copy-done.44, ...), custom_call_target="tpu_custom_call" | custom-call | flops 1207959552 | bytes 8257536 | tf_op jit(solution)/shard_map/feed_forward_up/pallas_call | solution.py:77
  182.6 5.8 %feed_forward_back.1 = (f32[64,1536]{1,0:T(8,128)}, bf16[64,1536]{1,0:T(8,128)(2,1)}, bf16[64,1536]{1,0:T(8,128)(2,1)}, bf16[64,1536]{1,0:T(8,128)(2,1)}, bf16[2...) custom-call(bf16[64,1536]{1,0:T(8,128)(2,1)} %copy-done.21, bf16[64,1536]{1,0:T(8,128)(2,1)} %copy-done.42, ...), custom_call_target="tpu_custom_call" | custom-call | flops 1207959552 | bytes 8454144 | tf_op jit(solution)/shard_map/feed_forward_back/pallas_call | solution.py:77
  189.9 4.2 %collective-permute-start.43 = (bf16[64,1536]{1,0:T(8,128)(2,1)}, bf16[64,1536]{1,0:T(8,128)(2,1)}, u32[]{:S(2)}, u32[]{:S(2)}) collective-permute-start(bf16[64,1536]{1,0:T(8,128)(2,1)} %get-tuple-element.271), channel_id=1, source_target_pairs={{2,0},{3,1},{0,2},{1,3},{6,4},{7,5},{4,6},{5,7},{10,8},{11,9},{8,1... | collective-permute-start | bytes 589832 | tf_op jit(solution)/shard_map/ppermute | solution.py:770
  196.4 22.2 %reduce-scatter.4.cloned.1.call-done = bf16[64,1536]{1,0:T(8,128)(2,1)} async-done(((bf16[256,1536]{1,0:T(8,128)(2,1)}), bf16[64,1536]{1,0:T(8,128)(2,1)}) %reduce-scatter.4.cloned.1.call-update) | async-done | bytes 196624 | tf_op jit(solution)/shard_map/reduce_scatter | solution.py:843
  226.9 5.2 %feed_forward_weights.1 = (bf16[1,1536,1536]{2,1,0:T(8,128)(2,1)}, bf16[1,1536,1536]{2,1,0:T(8,128)(2,1)}) custom-call(s32[3]{0:T(128)} %pad_add_fusion.where_ref, bf16[256,1536]{1,0:T(8,128)(2,1)} %get-tuple-element.273.normed_ref, bf16[256,1536]{1,0:T(8,128)(2,1)} %get-tuple-element.274.grad_ref, bf16[256,768]{1,0:T(8,128)(2,1)} %get-tuple-element.275.hidden_ref, ...), custom_call_target="tpu_custom_call" | custom-call | flops 1207959552 | bytes 11796480 | tf_op jit(solution)/shard_map/feed_forward_weights/pallas_call | solution.py:77
  247.6 4.2 %collective-permute-start.53 = (bf16[64,1536]{1,0:T(8,128)(2,1)S(1)}, bf16[64,1536]{1,0:T(8,128)(2,1)S(1)}, u32[]{:S(2)}, u32[]{:S(2)}) collective-permute-start(bf16[64,1536]{1,0:T(8,128)(2,1)S(1)} %copy-done.54), channel_id=1, source_target_pairs={{1,0},{2,1},{3,2},{0,3},{5,4},{6,5},{7,6},{4,7},{9,8},{10,9},{11,1... | collective-permute-start | bytes 589832 | tf_op jit(solution)/shard_map/ppermute | solution.py:770
  252.7 7.6 %section_mixture.1 = (bf16[8,128,192]{2,1,0:T(8,128)(2,1)}, bf16[8,192]{1,0:T(8,128)(2,1)}, bf16[8,192]{1,0:T(8,128)(2,1)}) custom-call(bf16[64,1536]{1,0:T(8,128)(2,1)} %copy-done.1, bf16[64,1536]{1,0:T(8,128)(2,1)} %copy-done.27, bf16[64,1536]{1,0:T(8,128)(2,1)} %copy-done.22, bf16[64,1536]{1,0:T(8,128)(2,1)} %copy-done.28, bf16[64,1536]{1,0:T(8,128)(2,1)} %copy-done.23, ...), custom_call_target="tpu_custom_call" | custom-call | flops 1207959552 | bytes 6298368 | tf_op jit(solution)/shard_map/section_mixture/pallas_call | solution.py:77
  260.3 4.6 %collective-permute-start.64 = (bf16[8,192]{1,0:T(8,128)(2,1)}, bf16[8,192]{1,0:T(8,128)(2,1)S(1)}, u32[]{:S(2)}, u32[]{:S(2)}) collective-permute-start(bf16[8,192]{1,0:T(8,128)(2,1)} %get-tuple-element.314), channel_id=1, source_target_pairs={{0,1},{1,2},{2,3},{4,5},{5,6},{6,7},{8,9},{9,10},{10,11},{12,13},{... | collective-permute-start | bytes 9224 | tf_op jit(solution)/shard_map/ppermute | solution.py:858
  270.6 7.9 %attention_backward.1 = (f32[64,1536]{1,0:T(8,128)}, bf16[64,1536]{1,0:T(8,128)(2,1)}, bf16[64,1536]{1,0:T(8,128)(2,1)}, bf16[64,1536]{1,0:T(8,128)(2,1)}, bf16[...) custom-call(s32[3]{0:T(128)} %pad_add_fusion.where_ref, ...), custom_call_target="tpu_custom_call" | custom-call | flops 805306368 | bytes 8700928 | tf_op jit(solution)/shard_map/attention_backward/pallas_call | solution.py:77
  283.3 6.3 %attention_weights.1 = (bf16[4,192,1024]{2,1,0:T(8,128)(2,1)}, bf16[4,192,1024]{2,1,0:T(8,128)(2,1)}, f32[4,48,192]{2,1,0:T(8,128)}, f32[4,48,192]{2,1,0:T(8,128)}) custom-call(s32[3]{0:T(128)} %pad_add_fusion.where_ref, bf16[256,1536]{1,0:T(8,128)(2,1)} %get-tuple-element.342.normed_ref, f32[256,1536]{1,0:T(8,128)} %get-tuple-element.343.unit_ref.refs_3_, ...), custom_call_target="tpu_custom_call" | custom-call | flops 805306368 | bytes 8856576 | tf_op jit(solution)/shard_map/attention_weights/pallas_call | solution.py:77
  289.7 4.2 %section_deep.1 = (bf16[8,128,192]{2,1,0:T(8,128)(2,1)}, bf16[4,128,1536]{2,1,0:T(8,128)(2,1)}, bf16[4,128,1536]{2,1,0:T(8,128)(2,1)}, f32[3,192]{1,0:T(4,128)}) custom-call(bf16[8,128,192]{2,1,0:T(8,128)(2,1)} %get-tuple-element.336.mix_ref, bf16[8,192]{1,0:T(8,128)(2,1)} %copy-done.67, bf16[8,192]{1,0:T(8,128)(2,1)} %copy-done.68, ...), custom_call_target="tpu_custom_call" | custom-call | flops 603979776 | bytes 4925952 | tf_op jit(solution)/shard_map/section_deep/pallas_call | solution.py:77
  293.8 8.8 %section_weights.1 = bf16[4,144,1536]{2,1,0:T(8,128)(2,1)} custom-call(bf16[8,128,192]{2,1,0:T(8,128)(2,1)} %get-tuple-element.356.deep_ref, bf16[8,64,192]{2,1,0:T(8,128)(2,1)} %get-tuple-element.357.coarse_ref, bf16[8,128,192]{2,1,0:T(8,128)(2,1)} %get-tuple-element.278.mix_ref, bf16[128,1536]{1,0:T(8,128)(2,1)} %bitcast.140, ...), custom_call_target="tpu_custom_call" | custom-call | flops 1509949440 | bytes 10616832 | tf_op jit(solution)/shard_map/section_weights/pallas_call | solution.py:77
  341.7 5.8 %collective-permute-done.85 = bf16[192,1024]{1,0:T(8,128)(2,1)S(1)} collective-permute-done((bf16[192,1024]{1,0:T(8,128)(2,1)S(1)}, bf16[192,1024]{1,0:T(8,128)(2,1)S(1)}, u32[]{:S(2)}, u32[]{:S(2)}) %collective-permute-start.85) | collective-permute-done | bytes 393248 | tf_op jit(solution)/shard_map/ppermute | solution.py:788
  350.5 3.7 %collective-permute-done.73 = bf16[128,1536]{1,0:T(8,128)(2,1)S(1)} collective-permute-done((bf16[128,1536]{1,0:T(8,128)(2,1)S(1)}, bf16[128,1536]{1,0:T(8,128)(2,1)S(1)}, u32[]{:S(2)}, u32[]{:S(2)}) %collective-permute-start.73) | collective-permute-done | bytes 393248 | tf_op jit(solution)/shard_map/ppermute | solution.py:788
  (398 shorter events, 173.9 us)
Async XLA Ops:
  7.3 92.3 %all-gather.3.cloned.1.call-start = ((), (), s32[]{:S(2)}) async-start(), calls=%async_computation.3 | async-start | bytes 2211840 | tf_op jit(solution)/shard_map/all_gather | solution.py:1153
  9.3 166.7 %all-gather.5.cloned.1.call-start = ((), (), s32[]{:S(2)}) async-start(), calls=%async_computation.4 | async-start | bytes 5308416 | tf_op jit(solution)/shard_map/all_gather | solution.py:835
  10.4 33.2 %collective-permute-start.1 = (bf16[192,1024]{1,0:T(8,128)(2,1)S(1)}, bf16[192,1024]{1,0:T(8,128)(2,1)S(1)}, u32[]{:S(2)}, u32[]{:S(2)}) collective-permute-start(bf16[192,1024]{1,0:T(8,128)(2,1)S(1)} %pad_maximum_fusion.2.refs_10_), channel_id=1, source_target_pairs={{0,8},{4,12},{8,0},{12,4},{16,24},{20,28},{24,16},{28,20},{1,9},{5... | collective-permute-start | bytes 1179656 | tf_op jit(solution)/shard_map/ppermute | solution.py:788
  13.4 30.7 %collective-permute-start.3 = (bf16[192,1024]{1,0:T(8,128)(2,1)S(1)}, bf16[192,1024]{1,0:T(8,128)(2,1)S(1)}, u32[]{:S(2)}, u32[]{:S(2)}) collective-permute-start(bf16[192,1024]{1,0:T(8,128)(2,1)S(1)} %pad_maximum_fusion.2.refs_10_), channel_id=1, source_target_pairs={{0,16},{4,20},{8,24},{12,28},{16,0},{20,4},{24,8},{28,12},{1,17},{... | collective-permute-start | bytes 1179656 | tf_op jit(solution)/shard_map/ppermute | solution.py:788
  14.9 29.3 %collective-permute-start.5 = (bf16[192,1024]{1,0:T(8,128)(2,1)S(1)}, bf16[192,1024]{1,0:T(8,128)(2,1)S(1)}, u32[]{:S(2)}, u32[]{:S(2)}) collective-permute-start(bf16[192,1024]{1,0:T(8,128)(2,1)S(1)} %pad_maximum_fusion.2.refs_10_), channel_id=1, source_target_pairs={{0,24},{4,28},{8,16},{12,20},{16,8},{20,12},{24,0},{28,4},{1,25},{... | collective-permute-start | bytes 1179656 | tf_op jit(solution)/shard_map/ppermute | solution.py:788
  43.6 30.2 %collective-permute-start = (bf16[192,1024]{1,0:T(8,128)(2,1)S(1)}, bf16[192,1024]{1,0:T(8,128)(2,1)S(1)}, u32[]{:S(2)}, u32[]{:S(2)}) collective-permute-start(bf16[192,1024]{1,0:T(8,128)(2,1)S(1)} %pad_maximum_fusion.2.refs_10_), channel_id=1, source_target_pairs={{0,4},{4,0},{8,12},{12,8},{16,20},{20,16},{24,28},{28,24},{1,5},{5... | collective-permute-start | bytes 1179656 | tf_op jit(solution)/shard_map/ppermute | solution.py:788
  43.6 30.2 %collective-permute-start.2 = (bf16[192,1024]{1,0:T(8,128)(2,1)S(1)}, bf16[192,1024]{1,0:T(8,128)(2,1)S(1)}, u32[]{:S(2)}, u32[]{:S(2)}) collective-permute-start(bf16[192,1024]{1,0:T(8,128)(2,1)S(1)} %collective-permute-done.1.refs_12_), channel_id=1, source_target_pairs={{0,4},{4,0},{8,12},{12,8},{16,20},{20,16},{24,28},{28,24},{1,5},{5... | collective-permute-start | bytes 1179656 | tf_op jit(solution)/shard_map/ppermute | solution.py:788
  44.1 29.7 %collective-permute-start.4 = (bf16[192,1024]{1,0:T(8,128)(2,1)S(1)}, bf16[192,1024]{1,0:T(8,128)(2,1)S(1)}, u32[]{:S(2)}, u32[]{:S(2)}) collective-permute-start(bf16[192,1024]{1,0:T(8,128)(2,1)S(1)} %collective-permute-done.3.refs_14_), channel_id=1, source_target_pairs={{0,4},{4,0},{8,12},{12,8},{16,20},{20,16},{24,28},{28,24},{1,5},{5... | collective-permute-start | bytes 1179656 | tf_op jit(solution)/shard_map/ppermute | solution.py:788
  44.2 29.6 %collective-permute-start.6 = (bf16[192,1024]{1,0:T(8,128)(2,1)S(1)}, bf16[192,1024]{1,0:T(8,128)(2,1)S(1)}, u32[]{:S(2)}, u32[]{:S(2)}) collective-permute-start(bf16[192,1024]{1,0:T(8,128)(2,1)S(1)} %collective-permute-done.5.refs_16_), channel_id=1, source_target_pairs={{0,4},{4,0},{8,12},{12,8},{16,20},{20,16},{24,28},{28,24},{1,5},{5... | collective-permute-start | bytes 1179656 | tf_op jit(solution)/shard_map/ppermute | solution.py:788
  118.2 100.5 %reduce-scatter.4.cloned.1.call-start = ((), (), s32[]{:S(2)}) async-start(), calls=%async_computation.5 | async-start | bytes 983040 | tf_op jit(solution)/shard_map/reduce_scatter | solution.py:843
  153.0 28.9 %collective-permute-start.39 = (bf16[128,1536]{1,0:T(8,128)(2,1)S(1)}, bf16[128,1536]{1,0:T(8,128)(2,1)S(1)}, u32[]{:S(2)}, u32[]{:S(2)}) collective-permute-start(bf16[128,1536]{1,0:T(8,128)(2,1)S(1)} %bitcast.135), channel_id=1, source_target_pairs={{0,8},{4,12},{8,0},{12,4},{16,24},{20,28},{24,16},{28,20},{1,9},{5... | collective-permute-start | bytes 1179656 | tf_op jit(solution)/shard_map/ppermute | solution.py:788
  154.2 27.7 %collective-permute-start.40 = (bf16[128,1536]{1,0:T(8,128)(2,1)S(1)}, bf16[128,1536]{1,0:T(8,128)(2,1)}, u32[]{:S(2)}, u32[]{:S(2)}) collective-permute-start(bf16[128,1536]{1,0:T(8,128)(2,1)S(1)} %bitcast.136), channel_id=1, source_target_pairs={{0,16},{4,20},{8,24},{12,28},{16,0},{20,4},{24,8},{28,12},{1,17},{... | collective-permute-start | bytes 1179656 | tf_op jit(solution)/shard_map/ppermute | solution.py:788
  155.1 27.4 %collective-permute-start.41 = (bf16[128,1536]{1,0:T(8,128)(2,1)S(1)}, bf16[128,1536]{1,0:T(8,128)(2,1)}, u32[]{:S(2)}, u32[]{:S(2)}) collective-permute-start(bf16[128,1536]{1,0:T(8,128)(2,1)S(1)} %bitcast.137), channel_id=1, source_target_pairs={{0,24},{4,28},{8,16},{12,20},{16,8},{20,12},{24,0},{28,4},{1,25},{... | collective-permute-start | bytes 1179656 | tf_op jit(solution)/shard_map/ppermute | solution.py:788
  156.6 25.0 %collective-permute-start.37 = (bf16[64,1536]{1,0:T(8,128)(2,1)S(1)}, bf16[64,1536]{1,0:T(8,128)(2,1)S(1)}, u32[]{:S(2)}, u32[]{:S(2)}) collective-permute-start(bf16[64,1536]{1,0:T(8,128)(2,1)S(1)} %convert_element_type.164.refs_0_), channel_id=1, source_target_pairs={{2,0},{3,1},{0,2},{1,3},{6,4},{7,5},{4,6},{5,7},{10,8},{11,9},{8,1... | collective-permute-start | bytes 589832 | tf_op jit(solution)/shard_map/ppermute | solution.py:770
  182.5 120.1 %reduce-scatter.6.cloned.1.call-start = ((), (), s32[]{:S(2)}) async-start(), calls=%async_computation.6 | async-start | bytes 5308416 | tf_op jit(solution)/shard_map/reduce_scatter | solution.py:839
  188.4 31.4 %collective-permute-start.42 = (bf16[64,1536]{1,0:T(8,128)(2,1)}, bf16[64,1536]{1,0:T(8,128)(2,1)S(1)}, u32[]{:S(2)}, u32[]{:S(2)}) collective-permute-start(bf16[64,1536]{1,0:T(8,128)(2,1)} %get-tuple-element.270), channel_id=1, source_target_pairs={{3,0},{0,1},{1,2},{2,3},{7,4},{4,5},{5,6},{6,7},{11,8},{8,9},{9,10... | collective-permute-start | bytes 589832 | tf_op jit(solution)/shard_map/ppermute | solution.py:770
  189.9 30.0 %collective-permute-start.43 = (bf16[64,1536]{1,0:T(8,128)(2,1)}, bf16[64,1536]{1,0:T(8,128)(2,1)}, u32[]{:S(2)}, u32[]{:S(2)}) collective-permute-start(bf16[64,1536]{1,0:T(8,128)(2,1)} %get-tuple-element.271), channel_id=1, source_target_pairs={{2,0},{3,1},{0,2},{1,3},{6,4},{7,5},{4,6},{5,7},{10,8},{11,9},{8,1... | collective-permute-start | bytes 589832 | tf_op jit(solution)/shard_map/ppermute | solution.py:770
  194.1 26.4 %collective-permute-start.44 = (bf16[64,1536]{1,0:T(8,128)(2,1)}, bf16[64,1536]{1,0:T(8,128)(2,1)}, u32[]{:S(2)}, u32[]{:S(2)}) collective-permute-start(bf16[64,1536]{1,0:T(8,128)(2,1)} %get-tuple-element.272), channel_id=1, source_target_pairs={{1,0},{2,1},{3,2},{0,3},{5,4},{6,5},{7,6},{4,7},{9,8},{10,9},{11,1... | collective-permute-start | bytes 589832 | tf_op jit(solution)/shard_map/ppermute | solution.py:770
  195.8 25.9 %collective-permute-start.46 = (bf16[128,1536]{1,0:T(8,128)(2,1)S(1)}, bf16[128,1536]{1,0:T(8,128)(2,1)S(1)}, u32[]{:S(2)}, u32[]{:S(2)}) collective-permute-start(bf16[128,1536]{1,0:T(8,128)(2,1)S(1)} %bitcast.138), channel_id=1, source_target_pairs={{0,4},{4,0},{8,12},{12,8},{16,20},{20,16},{24,28},{28,24},{1,5},{5... | collective-permute-start | bytes 1179656 | tf_op jit(solution)/shard_map/ppermute | solution.py:788
  195.9 28.0 %collective-permute-start.47 = (bf16[128,1536]{1,0:T(8,128)(2,1)S(1)}, bf16[128,1536]{1,0:T(8,128)(2,1)S(1)}, u32[]{:S(2)}, u32[]{:S(2)}) collective-permute-start(bf16[128,1536]{1,0:T(8,128)(2,1)S(1)} %collective-permute-done.39.refs_10_.refs_18_), channel_id=1, source_target_pairs={{0,4},{4,0},{8,12},{12,8},{16,20},{20,16},{24,28},{28,24},{1,5},{5... | collective-permute-start | bytes 1179656 | tf_op jit(solution)/shard_map/ppermute | solution.py:788
  236.4 118.8 %reduce-scatter.8.cloned.1.call-start = ((), (), s32[]{:S(2)}) async-start(), calls=%async_computation.7 | async-start | bytes 2211840 | tf_op jit(solution)/shard_map/reduce_scatter | solution.py:843
  278.5 25.3 %collective-permute-start.66 = (bf16[64,1536]{1,0:T(8,128)(2,1)}, bf16[64,1536]{1,0:T(8,128)(2,1)S(1)}, u32[]{:S(2)}, u32[]{:S(2)}) collective-permute-start(bf16[64,1536]{1,0:T(8,128)(2,1)} %get-tuple-element.332), channel_id=1, source_target_pairs={{3,0},{0,1},{1,2},{2,3},{7,4},{4,5},{5,6},{6,7},{11,8},{8,9},{9,10... | collective-permute-start | bytes 589832 | tf_op jit(solution)/shard_map/ppermute | solution.py:770
  279.2 24.7 %collective-permute-start.67 = (bf16[64,1536]{1,0:T(8,128)(2,1)}, bf16[64,1536]{1,0:T(8,128)(2,1)S(1)}, u32[]{:S(2)}, u32[]{:S(2)}) collective-permute-start(bf16[64,1536]{1,0:T(8,128)(2,1)} %get-tuple-element.333), channel_id=1, source_target_pairs={{2,0},{3,1},{0,2},{1,3},{6,4},{7,5},{4,6},{5,7},{10,8},{11,9},{8,1... | collective-permute-start | bytes 589832 | tf_op jit(solution)/shard_map/ppermute | solution.py:770
  304.0 24.8 %collective-permute-start.69 = (bf16[4,128,1536]{2,1,0:T(8,128)(2,1)}, bf16[4,128,1536]{2,1,0:T(8,128)(2,1)S(1)}, u32[]{:S(2)}, u32[]{:S(2)}) collective-permute-start(bf16[4,128,1536]{2,1,0:T(8,128)(2,1)} %get-tuple-element.359), channel_id=1, source_target_pairs={{0,4},{4,0},{8,12},{12,8},{16,20},{20,16},{24,28},{28,24},{1,5},{5... | collective-permute-start | bytes 4718600 | tf_op jit(solution)/shard_map/ppermute | solution.py:788
  (142 other events, 1580.0 us)
Sparse Core Ops, SparseCore 0:
  10.3 55.6 all-gather.2
  118.3 57.7 all-gather.4
  182.6 35.9 reduce-scatter.3
  236.5 54.4 reduce-scatter.5
  312.0 37.5 reduce-scatter.7

commit v4 on v3

--- a/solution.py
+++ b/solution.py
@@ -63,27 +63,47 @@
     return jnp.dot(left_side, right_side, preferred_element_type=jnp.float32)
 
 
-def run_kernel(kernel, ins, outs, scalars=None, scratch=(), flops=0, name=None, spare=8):
+def run_kernel(kernel, ins, outs, scalars=None, scratch=(), far=(), far_outs=()):
     whole = pl.BlockSpec(memory_space=pltpu.VMEM)
-    specs = [whole] * len(ins)
-    args = list(ins)
+    outside = pl.BlockSpec(memory_space=pl.ANY)
+    specs = [outside] * len(far) + [whole] * len(ins)
+    args = list(far) + list(ins)
     if scalars is not None:
         specs = [pl.BlockSpec(memory_space=pltpu.SMEM)] + specs
         args = [scalars] + args
-    shapes = [jax.ShapeDtypeStruct(shape, dtype) for shape, dtype in outs]
-    moved = sum(x.size * x.dtype.itemsize for x in list(ins) + shapes)
-    held = sum(math.prod(x.shape) * jnp.dtype(x.dtype).itemsize for x in scratch)
-    room = 56 * 1024 * 1024
+    shapes = [jax.ShapeDtypeStruct(shape, dtype) for shape, dtype in list(outs) + list(far_outs)]
     return pl.pallas_call(
         kernel,
         in_specs=specs,
-        out_specs=[whole] * len(shapes),
+        out_specs=[whole] * len(outs) + [outside] * len(far_outs),
         out_shape=shapes,
         scratch_shapes=scratch,
-        compiler_params=pltpu.CompilerParams(vmem_limit_bytes=room),
-        cost_estimate=pl.CostEstimate(flops=flops, bytes_accessed=moved, transcendentals=0),
-        name=name,
+        compiler_params=pltpu.CompilerParams(vmem_limit_bytes=53 * 1024 * 1024),
+        name=kernel.__qualname__.split(".")[0],
     )(*args)
+
+
+def start_copies(pairs, sems, first=0):
+    copies = [
+        pltpu.make_async_copy(source, target, sems.at[first + n])
+        for n, (source, target) in enumerate(pairs)
+    ]
+    for copy in copies:
+        copy.start()
+    return copies
+
+
+def wait_copies(copies):
+    for copy in copies:
+        copy.wait()
+
+
+def halves(windows, shape, dtype):
+    return [(shape, dtype)] * windows
+
+
+def place(m, windows):
+    return m // 2 + m % 2 * (windows // 2)
 
 
 def lanes_of(head, width, shape):
@@ -95,8 +115,8 @@
     return lax.rem(where_ref[1] + step, count)
 
 
-def attention_forward(where, raw, row_params, rel_turned, blocks, local_heads):
-    count, (own, width) = len(raw), raw[0].shape
+def attention_forward(where, raw, row_params, rel_turned, blocks, local_heads, own):
+    count, width = len(raw), raw[0].shape[1]
     length = count * own
     n_blocks, columns = len(blocks), blocks[0].shape[1]
     rows = width // n_blocks
@@ -114,7 +134,7 @@
             spot = (where_ref[0] ^ m) * rows if n_blocks > 1 else 0
             weight_ref[pl.ds(pl.multiple_of(spot, rows), rows), :] = block_refs[m][:rows, :]
         for k in range(count):
-            resid = raw_refs[k][...].astype(jnp.float32) + species_ref[...]
+            resid = raw_refs[k][:own, :].astype(jnp.float32) + species_ref[...]
             unit, scale = normalize(resid)
             spot = pl.ds(pl.multiple_of(chunk_of(where_ref, k, count) * own, own), own)
             unit_ref[spot, :] = unit
@@ -174,29 +194,29 @@
         outs,
         scalars=where,
         scratch=[pltpu.VMEM((length, width), jnp.float32)],
-        flops=2 * length * width * columns,
-        name="attention_forward",
     )
     return found[:count], found[count:]
 
 
-def attention_backward(where, grads, saved, rel_turned, basis_turned, local_heads):
-    count, (own, width) = len(grads), grads[0].shape
+def attention_backward(
+    where, grads, saved, rel_turned, basis_turned, gain, sums_two, local_heads, own
+):
+    count, width = len(grads), grads[0].shape[1]
     length = count * own
-    weight, _, _, _, probs_all, content_all, position_all, key_all, value_all, _ = saved
+    weight, _, unit_all, scale_all, probs_all, content_all, position_all, key_all, value_all, _ = saved
     keys, values = local_heads * KEYD, local_heads * VALD
     narrow = 2 * keys + values
 
     def kernel(where_ref, *refs):
         grad_refs, refs = refs[:count], refs[count:]
         weight_ref, probs_ref, content_ref, position_ref, key_ref, value_ref = refs[:6]
-        rel_ref, basis_ref = refs[6:8]
-        own_ref, refs = refs[8], refs[9:]
+        rel_ref, basis_ref, unit_ref, scale_ref, gain_ref, two_ref = refs[6:12]
+        own_ref, refs = refs[12], refs[13:]
         part_refs, refs = refs[: count - 1], refs[count - 1 :]
-        attn_ref, heads_ref, total_ref, bias_ref, weight_out = refs
+        attn_ref, heads_ref, bias_ref, weight_out, sums_ref, total_ref = refs
         for k in range(count):
             spot = pl.ds(pl.multiple_of(chunk_of(where_ref, k, count) * own, own), own)
-            attn_ref[spot, :] = grad_refs[k][...]
+            attn_ref[spot, :] = grad_refs[k][:own, :]
         grad_mixed = dot_rows(attn_ref[...], weight_ref[:, narrow:]).astype(LOW)
         content, position = content_ref[...], position_ref[...]
         key_low, value_low = key_ref[...], value_ref[...]
@@ -205,7 +225,10 @@
         grad_key = jnp.zeros((length, keys), jnp.float32)
         grad_rel = jnp.zeros((2 * length, keys), jnp.float32)
         grad_value = jnp.zeros((length, values), jnp.float32)
-        back = lax.broadcasted_iota(jnp.int32, (length, 2 * length), 0)
+        row = lax.broadcasted_iota(jnp.int32, (length, length), 0)
+        column = lax.broadcasted_iota(jnp.int32, (length, length), 1)
+        reverse = (row + column == length - 1).astype(jnp.float32).astype(LOW)
+        position_reversed = dot_rows(reverse, position).astype(LOW)
         for h in range(local_heads):
             mine = lanes_of(h, KEYD, (length, keys))
             ours = lanes_of(h, VALD, (length, values))
@@ -218,18 +241,18 @@
             grad_value = jnp.where(ours, dot_leading(probs.astype(LOW), grad_mixed), grad_value)
             grad_key = jnp.where(mine, dot_leading(grad_scores, content), grad_key)
             grad_content = jnp.where(mine, dot_rows(grad_scores, key_low), grad_content)
-            band = jnp.concatenate(
-                [grad_scores.astype(jnp.float32), jnp.zeros((length, length), jnp.float32)], axis=1
-            )
-            bit = 1
-            while bit < length:
-                turn = (length - 1 - back) & bit
-                band = jnp.where(turn > 0, pltpu.roll(band, bit, 1), band)
-                bit *= 2
-            band = band.astype(LOW)
-            grad_position = jnp.where(mine, dot_rows(band, rel_ref[...]), grad_position)
+            band = dot_rows(reverse, grad_scores)
+            band = jnp.concatenate([band, jnp.zeros((length, length), jnp.float32)], axis=1)
+            band = pltpu.roll(band, 0, 1, stride=1, stride_axis=0).astype(LOW)
+            turned = dot_rows(band, rel_ref[...])
+            high = turned.astype(LOW)
+            low = (turned - high.astype(jnp.float32)).astype(LOW)
+            turned = dot_rows(reverse, high) + dot_rows(reverse, low)
+            grad_position = jnp.where(mine, turned, grad_position)
             grad_rel = jnp.where(
-                lanes_of(h, KEYD, (2 * length, keys)), dot_leading(band, position), grad_rel
+                lanes_of(h, KEYD, (2 * length, keys)),
+                dot_leading(band, position_reversed),
+                grad_rel,
             )
         grad_content = grad_content * SCALE
         grad_position = grad_position * SCALE
@@ -239,96 +262,97 @@
         heads_ref[:, keys : 2 * keys] = (grad_key * SCALE).astype(LOW)
         heads_ref[:, 2 * keys :] = grad_value.astype(LOW)
         weight_out[...] = dot_leading(basis_ref[...], (grad_rel * SCALE).astype(LOW))
-        total_ref[...] = dot_transposed(heads_ref[...], weight_ref[:, :narrow])
+        grad = dot_transposed(heads_ref[...], weight_ref[:, :narrow])
+        total_ref[...] = grad
+        unit = unit_ref[...]
+        into = normalize_back(unit, scale_ref[:, :1], grad * gain_ref[...])
+        table = jnp.sum(into, axis=0, keepdims=True) + two_ref[2:3, :]
+        sums_ref[...] = jnp.zeros_like(sums_ref)
+        sums_ref[0:1, :] = jnp.sum(grad * unit, axis=0, keepdims=True)
+        sums_ref[1:2, :] = two_ref[0:1, :]
+        sums_ref[2:3, :] = jnp.sum(grad, axis=0, keepdims=True)
+        sums_ref[3:4, :] = two_ref[1:2, :]
+        for kind in range(SPECIES):
+            sums_ref[4 + kind : 5 + kind, :] = jnp.where(where_ref[2] == kind, table, 0.0)
         for k in range(count):
             spot = pl.ds(pl.multiple_of(chunk_of(where_ref, k, count) * own, own), own)
             if k == 0:
                 own_ref[...] = total_ref[spot, :]
             else:
-                part_refs[k - 1][...] = total_ref[spot, :].astype(LOW)
+                part_refs[k - 1][:own, :] = total_ref[spot, :].astype(LOW)
+                part_refs[k - 1][own:, :] = sums_ref[...].astype(LOW)
 
     outs = (
         [((own, width), jnp.float32)]
-        + [((own, width), LOW)] * (count - 1)
+        + [((own + 16, width), LOW)] * (count - 1)
         + [
             ((length, width), LOW),
             ((length, narrow), LOW),
-            ((length, width), jnp.float32),
             ((2, keys), jnp.float32),
             ((BASIS, keys), jnp.float32),
+            ((16, width), jnp.float32),
         ]
     )
     found = run_kernel(
         kernel,
         list(grads)
         + [weight, probs_all, content_all, position_all, key_all, value_all]
-        + [rel_turned, basis_turned],
+        + [rel_turned, basis_turned, unit_all, scale_all, gain, sums_two],
         outs,
         scalars=where,
-        flops=2 * length * width * (narrow + values),
-        name="attention_backward",
+        scratch=[pltpu.VMEM((length, width), jnp.float32)],
     )
     return found[:count], found[count:]
 
 
 def attention_weights(
-    where, saved, grad_attn, grad_heads, grad_normed, gain, sums_two, bias_sums, rel_grad, n_blocks
+    where, saved, grad_attn, grad_heads, own_sums, received, bias_sums, rel_grad, n_blocks
 ):
-    normed, unit_all, scale_all, mixed = saved[1], saved[2], saved[3], saved[9]
+    normed, mixed = saved[1], saved[9]
     width = normed.shape[1]
     rows = width // n_blocks
     narrow, values = grad_heads.shape[1], mixed.shape[1]
     columns = narrow + values
     keys = rel_grad.shape[1]
-    spread = max(rows, keys)
-    tall = 8 + -(-(2 + BASIS) // 8) * 8
-
-    def kernel(where_ref, normed_ref, unit_ref, scale_ref, mixed_ref, attn_ref, *refs):
-        heads_ref, grad_ref, gain_ref, two_ref, bias_ref, rel_ref = refs[:6]
-        even_ref, odd_ref, small_even, small_odd, whole_ref, sums_ref = refs[6:]
-        grad, unit = grad_ref[...], unit_ref[...]
-        into = normalize_back(unit, scale_ref[:, :1], grad * gain_ref[...])
-        sums_ref[0:1, :] = jnp.sum(grad * unit, axis=0, keepdims=True)
-        sums_ref[1:2, :] = two_ref[0:1, :]
-        sums_ref[2:3, :] = jnp.sum(grad, axis=0, keepdims=True)
-        sums_ref[3:4, :] = two_ref[1:2, :]
-        table = jnp.sum(into, axis=0, keepdims=True) + two_ref[2:3, :]
-        for kind in range(SPECIES):
-            sums_ref[4 + kind : 5 + kind, :] = jnp.where(where_ref[2] == kind, table, 0.0)
-        sums = sums_ref[...]
-        small_even[...] = jnp.zeros_like(small_even)
-        small_odd[...] = jnp.zeros_like(small_odd)
-        for m in range(n_blocks):
-            spot = (where_ref[0] ^ m) if n_blocks > 1 else 0
-            half = small_odd if m % 2 else small_even
-            moved = pltpu.roll(sums, lax.rem(width - spot * rows, width), 1)
-            half[m // 2, 0:8, :rows] = moved[:, :rows]
-            turn = lax.rem(keys - spot * (KEYD // n_blocks), keys)
-            half[m // 2, 8:10, :keys] = pltpu.roll(bias_ref[...], turn, 1)
-            half[m // 2, 10 : 10 + BASIS, :keys] = pltpu.roll(rel_ref[...], turn, 1)
+    count = len(received) + 1
+
+    def kernel(where_ref, normed_ref, mixed_ref, attn_ref, heads_ref, own_ref, *refs):
+        received_refs, refs = refs[: count - 1], refs[count - 1 :]
+        bias_ref, rel_ref, half_refs, whole_ref = refs[0], refs[1], refs[2:-1], refs[-1]
+        sums = own_ref[...]
+        for ref in received_refs:
+            sums = sums + ref[ref.shape[0] - 16 :, :].astype(jnp.float32)
+        sums = sums[:8]
         whole_ref[:, :narrow] = dot_leading(normed_ref[...], heads_ref[...]).astype(LOW)
         whole_ref[:, narrow:] = dot_leading(attn_ref[...], mixed_ref[...]).astype(LOW)
         for m in range(n_blocks):
-            spot = (where_ref[0] ^ m) * rows if n_blocks > 1 else 0
-            half = odd_ref if m % 2 else even_ref
-            half[m // 2] = whole_ref[pl.ds(pl.multiple_of(spot, rows), rows), :]
-
-    half = max(n_blocks // 2, 1)
+            spot = (where_ref[0] ^ m) if n_blocks > 1 else 0
+            half = half_refs[place(m, n_blocks)]
+            half[:rows, :] = whole_ref[pl.ds(pl.multiple_of(spot * rows, rows), rows), :]
+            if n_blocks == 1:
+                continue
+            moved = pltpu.roll(sums, lax.rem(width - spot * rows, width), 1)[:, :256]
+            turn = lax.rem(keys - spot * (KEYD // n_blocks), keys)
+            rel = pltpu.roll(rel_ref[...], turn, 1)
+            bias = pltpu.roll(bias_ref[...], turn, 1)
+            bias = jnp.concatenate([bias, jnp.zeros((6, keys), jnp.float32)], axis=0)
+            bias = jnp.concatenate([bias, jnp.zeros((8, 256 - keys), jnp.float32)], axis=1)
+            half[rows:, :256] = jnp.concatenate([moved, bias], axis=0).astype(LOW)
+            half[rows:, 256 : 256 + keys] = rel[:16].astype(LOW)
+            half[rows:, 256 + keys : 256 + 2 * keys] = rel[16:].astype(LOW)
+            half[rows:, 256 + 2 * keys :] = jnp.zeros((16, columns - 256 - 2 * keys), LOW)
+
     return run_kernel(
         kernel,
-        [normed, unit_all, scale_all, mixed, grad_attn, grad_heads, grad_normed, gain]
-        + [sums_two, bias_sums, rel_grad],
-        [((half, rows, columns), LOW)] * 2 + [((half, tall, spread), jnp.float32)] * 2,
+        [normed, mixed, grad_attn, grad_heads, own_sums] + list(received) + [bias_sums, rel_grad],
+        halves(n_blocks, (rows + (16 if n_blocks > 1 else 0), columns), LOW),
         scalars=where,
-        scratch=[pltpu.VMEM((width, columns), LOW), pltpu.VMEM((8, width), jnp.float32)],
-        flops=2 * normed.shape[0] * width * columns,
-        name="attention_weights",
-    )
-
-
-def unpack_small(where, blocks, basis_turned, width, local_heads, count):
-    half, entries = blocks[0].shape
-    total = 2 * half
+        scratch=[pltpu.VMEM((width, columns), LOW)],
+    )
+
+
+def unpack_small(where, found, basis_turned, width, local_heads, count):
+    total = found.shape[0]
     n_blocks = total // count
     share = width // total
     n_rows = 8 + SPECIES
@@ -339,16 +363,13 @@
     length = basis_turned.shape[0]
 
     def kernel(where_ref, *refs):
-        block_refs, basis_ref, refs = refs[:2], refs[2], refs[3:]
+        found_ref, basis_ref, refs = refs[0], refs[1], refs[2:]
         row_refs, refs = refs[:5], refs[5:]
-        taps_ref, bias_ref, rel_ref, content_ref, position_ref, found_ref, weight_ref = refs
-        for core in range(2):
-            found_ref[core * half : (core + 1) * half, :] = block_refs[core][...].astype(jnp.float32)
+        taps_ref, bias_ref, rel_ref, content_ref, position_ref, weight_ref = refs
 
         def owner(shape):
             spot = lax.broadcasted_iota(jnp.int32, shape, 0)
-            block = 2 * (spot % half // count) + spot // half
-            return block ^ where_ref[0], lax.rem(spot % count + where_ref[1], count)
+            return spot // count, lax.rem(spot % count + where_ref[1], count)
 
         def widen(start, size, span):
             column = lax.broadcasted_iota(jnp.int32, (size, span), 1)
@@ -358,7 +379,7 @@
             else:
                 chosen = (column // KEYD == inner // part) & (column % part == inner % part)
             return dot_rows(
-                found_ref[:, start : start + size].astype(LOW),
+                found_ref[:, start : start + size],
                 chosen.astype(jnp.float32).astype(LOW),
             )
 
@@ -399,14 +420,13 @@
 
     found = run_kernel(
         kernel,
-        list(blocks) + [basis_turned],
+        [found, basis_turned],
         [((1, width), jnp.float32)] * 5
         + [((3, group), jnp.float32), ((1, group), jnp.float32)]
         + [((length, keys), LOW)]
         + [((1, keys), jnp.float32)] * 2,
         scalars=where,
-        scratch=[pltpu.VMEM((total, entries), jnp.float32), pltpu.VMEM((BASIS, keys), jnp.float32)],
-        name="unpack_small",
+        scratch=[pltpu.VMEM((BASIS, keys), jnp.float32)],
     )
     return found[:5], found[5:]
 
@@ -436,7 +456,6 @@
             ((own, 128), jnp.float32),
             ((own, width), LOW),
         ],
-        name="second_norm",
     )
 
 
@@ -461,7 +480,6 @@
         kernel,
         [own_part] + list(parts) + [unit, scale, gain, grad_resid],
         [((own, width), jnp.float32), ((own, width), LOW), ((3, width), jnp.float32)],
-        name="second_norm_back",
     )
 
 
@@ -473,7 +491,7 @@
         unit_ref, scale_ref, gain_ref, grad_ref, out_ref = refs
         total = own_ref[...]
         for ref in part_refs:
-            total = total + ref[...].astype(jnp.float32)
+            total = total + ref[:own, :].astype(jnp.float32)
         spot = pl.ds(pl.multiple_of(where_ref[1] * own, own), own)
         out_ref[0] = grad_ref[...] + normalize_back(
             unit_ref[spot, :], scale_ref[spot, :1], total * gain_ref[...]
@@ -484,7 +502,6 @@
         [own_part] + list(parts) + [unit_all, scale_all, gain, grad_resid],
         [((1, own, width), jnp.float32)],
         scalars=where,
-        name="first_norm_back",
     )[0]
 
 
@@ -512,8 +529,6 @@
         [((length, width), LOW)] * 2
         + [((length, hidden_count), LOW), ((length, hidden_count), jnp.float32)],
         scalars=where,
-        flops=4 * length * width * hidden_count,
-        name="feed_forward_up",
     )
 
 
@@ -540,8 +555,6 @@
         [((own, width), jnp.float32)]
         + [((own, width), LOW)] * (count - 1)
         + [((length, width), LOW), ((length, hidden_count), LOW)],
-        flops=4 * length * width * hidden_count,
-        name="feed_forward_back",
     )
     return found[:count], found[count:]
 
@@ -551,23 +564,22 @@
     hidden_count = hidden.shape[1]
     rows = width // n_blocks
 
-    def kernel(where_ref, normed_ref, grad_ref, hidden_ref, pre_ref, even_ref, odd_ref, whole_ref):
+    def kernel(where_ref, normed_ref, grad_ref, hidden_ref, pre_ref, *refs):
+        half_refs, whole_ref = refs[:-1], refs[-1]
         whole_ref[:, :hidden_count] = dot_leading(normed_ref[...], pre_ref[...]).astype(LOW)
         whole_ref[:, hidden_count:] = dot_leading(grad_ref[...], hidden_ref[...]).astype(LOW)
         for m in range(n_blocks):
             spot = (where_ref[0] ^ m) * rows if n_blocks > 1 else 0
-            half = odd_ref if m % 2 else even_ref
-            half[m // 2] = whole_ref[pl.ds(pl.multiple_of(spot, rows), rows), :]
-
-    half = max(n_blocks // 2, 1)
+            half_refs[place(m, n_blocks)][...] = whole_ref[
+                pl.ds(pl.multiple_of(spot, rows), rows), :
+            ]
+
     return run_kernel(
         kernel,
         [normed_all, grad_all, hidden, grad_pre],
-        [((half, rows, 2 * hidden_count), LOW)] * 2,
+        halves(n_blocks, (rows, 2 * hidden_count), LOW),
         scalars=where,
         scratch=[pltpu.VMEM((width, 2 * hidden_count), LOW)],
-        flops=4 * normed_all.shape[0] * width * hidden_count,
-        name="feed_forward_weights",
     )
 
 
@@ -579,189 +591,223 @@
     return before, after
 
 
-def section_grad_deep(blocks, weight, count):
-    fine, width = blocks[0].shape
+def section_gradient(where, blocks, weight, taps, count):
+    width = blocks[0].shape[1]
+    fine = blocks[0].shape[0] - 16
+    own = fine // 2
     channels = weight.shape[0] // 3
     share = channels // count
     windows = len(blocks)
-
-    def kernel(*refs):
-        block_refs, weight_ref, refs = refs[:windows], refs[windows], refs[windows + 1 :]
-        deep_ref, head_ref, tail_ref, *whole_refs = refs
+    rows = windows * fine
+
+    def kernel(where_ref, *refs):
+        block_refs, weight_ref, taps_ref, refs = (
+            refs[:windows], refs[windows], refs[windows + 1], refs[windows + 2 :]
+        )
+        deep_ref, mix_ref, coarse_ref, bias_ref, refs = *refs[:4], refs[4:]
+        half_refs, whole_refs, (rows_ref, sems) = refs[:windows], refs[windows:-2], refs[-2:]
+        copies = start_copies(
+            [
+                (block_refs[m].at[:fine, :], rows_ref.at[m * fine : (m + 1) * fine, :])
+                for m in range(windows)
+            ]
+            + [
+                (block_refs[m].at[fine:, :], rows_ref.at[pl.ds(rows + 16 * m, 16), :])
+                for m in range(windows)
+            ],
+            sems,
+        )
         for which, ref in enumerate(whole_refs):
             for t in range(count):
                 spot = (3 * t + which) * share
                 ref[t * share : (t + 1) * share, :] = weight_ref[spot : spot + share, :]
-        for m in range(windows):
-            deep = dot_transposed(block_refs[m][...], whole_refs[0][...]).astype(LOW)
-            deep_ref[m] = deep
-            head_ref[m : m + 1, :] = deep[:1]
-            tail_ref[m : m + 1, :] = deep[fine - 1 :]
-
-    return run_kernel(
-        kernel,
-        list(blocks) + [weight],
-        [((windows, fine, channels), LOW)]
-        + [((windows, channels), LOW)] * 2
-        + [((channels, width), LOW)] * 3,
-        flops=2 * windows * fine * width * channels,
-        name="section_grad_deep",
-    )
-
-
-def section_grad_mix(deep, before, after, taps, up):
-    windows, fine, channels = deep.shape
-    width = up.shape[1]
-    own = fine // 2
-
-    def kernel(deep_ref, before_ref, after_ref, taps_ref, up_ref, *refs):
-        mix_ref, coarse_ref, even_ref, odd_ref, bias_ref = refs
         row = lax.broadcasted_iota(jnp.int32, (own, fine), 0)
         column = lax.broadcasted_iota(jnp.int32, (own, fine), 1)
         pool = (column // 2 == row).astype(jnp.float32).astype(LOW)
         bias = jnp.zeros((1, channels), jnp.float32)
+        wait_copies(copies)
+        deep = dot_transposed(rows_ref[...], whole_refs[0][...]).astype(LOW)
+        deep_ref[...] = deep[:rows]
         for m in range(windows):
-            rows = deep_ref[m].astype(jnp.float32)
+            edge = deep[rows + 16 * m : rows + 16 * (m + 1)].astype(jnp.float32)
+            own_rows = deep[m * fine : (m + 1) * fine].astype(jnp.float32)
+            previous, following = shifted(
+                own_rows,
+                jnp.where(where_ref[1] > 0, edge[0:1], 0.0),
+                jnp.where(where_ref[1] < count - 1, edge[1:2], 0.0),
+            )
+            mix = (
+                taps_ref[0:1, :] * following
+                + taps_ref[1:2, :] * own_rows
+                + taps_ref[2:3, :] * previous
+            ).astype(LOW)
+            mix_ref[m * fine : (m + 1) * fine, :] = mix
+            bias = bias + jnp.sum(mix.astype(jnp.float32), axis=0, keepdims=True)
+            coarse_ref[m * own : (m + 1) * own, :] = dot_rows(pool, mix).astype(LOW)
+        bias_ref[...] = bias
+        part = dot_rows(coarse_ref[...], whole_refs[1][...]).astype(LOW)
+        for m in range(windows):
+            half_refs[place(m, windows)][...] = part[m * own : (m + 1) * own]
+
+    return run_kernel(
+        kernel,
+        [weight, taps],
+        [((rows, channels), LOW)] * 2
+        + [((windows * own, channels), LOW)]
+        + [((1, channels), jnp.float32)]
+        + halves(windows, (own, width), LOW)
+        + [((channels, width), LOW)] * 3,
+        scalars=where,
+        scratch=[
+            pltpu.VMEM((rows + 16 * windows, width), LOW),
+            pltpu.SemaphoreType.DMA((2 * windows,)),
+        ],
+        far=blocks,
+    )
+
+
+def section_grad_encoder(where, mix, lateral, windows):
+    rows = mix.shape[0]
+    fine = rows // windows
+    width = lateral.shape[1]
+
+    def kernel(where_ref, mix_ref, lateral_ref, out_ref):
+        part = dot_rows(mix_ref[...], lateral_ref[...]).astype(LOW)
+        for m in range(windows):
+            spot = pl.ds(pl.multiple_of((where_ref[0] ^ m) * fine, fine), fine)
+            out_ref[spot, :] = part[m * fine : (m + 1) * fine]
+
+    return run_kernel(kernel, [mix, lateral], [((rows, width), LOW)], scalars=where)[0]
+
+
+def section_forward(
+    where, coarse_blocks, fine_blocks, up, lateral, point, bias, taps, grad_deep, count
+):
+    windows = len(fine_blocks)
+    fine, (channels, width) = grad_deep.shape[0] // windows, up.shape
+    own = fine // 2
+    long, short = fine_blocks[0].shape[0], coarse_blocks[0].shape[0]
+
+    def kernel(where_ref, *refs):
+        coarse_refs, fine_refs, refs = refs[:windows], refs[windows : 2 * windows], refs[2 * windows :]
+        up_ref, lateral_ref, point_ref, bias_ref, taps_ref, grad_ref = refs[:6]
+        deep_ref, sums_ref, half_refs = refs[6], refs[7], refs[8:-3]
+        short_ref, long_ref, sems = refs[-3:]
+        copies = start_copies(
+            [
+                (coarse_refs[m], short_ref.at[m * short : (m + 1) * short, :])
+                for m in range(windows)
+            ]
+            + [
+                (fine_refs[m], long_ref.at[m * long : (m + 1) * long, :]) for m in range(windows)
+            ],
+            sems,
+        )
+        row = lax.broadcasted_iota(jnp.int32, (long, short), 0)
+        column = lax.broadcasted_iota(jnp.int32, (long, short), 1)
+        source = jnp.where(row < fine, row // 2, row - fine + own)
+        repeat = (source == column).astype(jnp.float32).astype(LOW)
+        wait_copies(copies[:windows])
+        coarse = dot_transposed(short_ref[...], up_ref[...])
+        high = coarse.astype(LOW)
+        low = (coarse - high.astype(jnp.float32)).astype(LOW)
+        wait_copies(copies[windows:])
+        lateral_part = dot_transposed(long_ref[...], lateral_ref[...])
+        sums = [jnp.zeros((1, channels), jnp.float32)] * 3
+        for m in range(windows):
+            spot = slice(m * short, (m + 1) * short)
+            mix = (
+                dot_rows(repeat, high[spot])
+                + dot_rows(repeat, low[spot])
+                + lateral_part[m * long : (m + 1) * long]
+                + bias_ref[...]
+            ).astype(LOW).astype(jnp.float32)
+            rows = mix[:fine]
             previous, following = shifted(
                 rows,
-                before_ref[m : m + 1, :].astype(jnp.float32),
-                after_ref[m : m + 1, :].astype(jnp.float32),
+                jnp.where(where_ref[1] > 0, mix[fine : fine + 1], 0.0),
+                jnp.where(where_ref[1] < count - 1, mix[fine + 1 : fine + 2], 0.0),
             )
-            mix = (
-                taps_ref[0:1, :] * following + taps_ref[1:2, :] * rows + taps_ref[2:3, :] * previous
-            ).astype(LOW)
-            mix_ref[m] = mix
-            bias = bias + jnp.sum(mix.astype(jnp.float32), axis=0, keepdims=True)
-            coarse = dot_rows(pool, mix).astype(LOW)
-            coarse_ref[m] = coarse
-            half = odd_ref if m % 2 else even_ref
-            half[m // 2] = dot_rows(coarse, up_ref[...]).astype(LOW)
-        bias_ref[...] = bias
-
-    return run_kernel(
-        kernel,
-        [deep, before, after, taps, up],
-        [((windows, fine, channels), LOW), ((windows, own, channels), LOW)]
-        + [((windows // 2, own, width), LOW)] * 2
-        + [((1, channels), jnp.float32)],
-        flops=2 * windows * own * width * channels,
-        name="section_grad_mix",
-    )
-
-
-def section_grad_encoder(mix, lateral):
-    windows, fine, channels = mix.shape
-    width = lateral.shape[1]
-
-    def kernel(mix_ref, lateral_ref, even_ref, odd_ref):
-        for m in range(windows):
-            half = odd_ref if m % 2 else even_ref
-            half[m // 2] = dot_rows(mix_ref[m], lateral_ref[...]).astype(LOW)
-
-    return run_kernel(
-        kernel,
-        [mix, lateral],
-        [((windows // 2, fine, width), LOW)] * 2,
-        flops=2 * windows * fine * width * channels,
-        name="section_grad_encoder",
-    )
-
-
-def section_mixture(coarse_blocks, fine_blocks, up, lateral, bias):
-    own, width = coarse_blocks[0].shape
-    fine = 2 * own
-    channels = lateral.shape[0]
-    windows = len(coarse_blocks)
-
-    def kernel(*refs):
-        coarse_refs, fine_refs, refs = refs[:windows], refs[windows : 2 * windows], refs[2 * windows :]
-        up_ref, lateral_ref, bias_ref, mix_ref, head_ref, tail_ref = refs
-        row = lax.broadcasted_iota(jnp.int32, (fine, own), 0)
-        column = lax.broadcasted_iota(jnp.int32, (fine, own), 1)
-        repeat = (row // 2 == column).astype(jnp.float32).astype(LOW)
-        for m in range(windows):
-            repeated = dot_rows(repeat, coarse_refs[m][...]).astype(LOW)
-            mix = (
-                dot_transposed(repeated, up_ref[...])
-                + dot_transposed(fine_refs[m][...], lateral_ref[...])
-                + bias_ref[...]
-            ).astype(LOW)
-            mix_ref[m] = mix
-            head_ref[m : m + 1, :] = mix[:1]
-            tail_ref[m : m + 1, :] = mix[fine - 1 :]
-
-    return run_kernel(
-        kernel,
-        list(coarse_blocks) + list(fine_blocks) + [up, lateral, bias],
-        [((windows, fine, channels), LOW)] + [((windows, channels), LOW)] * 2,
-        flops=4 * windows * fine * width * channels,
-        name="section_mixture",
-    )
-
-
-def section_deep(mix, before, after, taps, point, grad_deep):
-    windows, fine, channels = mix.shape
-    width = point.shape[1]
-
-    def kernel(mix_ref, before_ref, after_ref, taps_ref, point_ref, grad_ref, *refs):
-        deep_ref, even_ref, odd_ref, sums_ref = refs
-        sums = [jnp.zeros((1, channels), jnp.float32)] * 3
-        for m in range(windows):
-            rows = mix_ref[m].astype(jnp.float32)
-            previous, following = shifted(
-                rows,
-                before_ref[m : m + 1, :].astype(jnp.float32),
-                after_ref[m : m + 1, :].astype(jnp.float32),
-            )
-            deep = (
+            spot = slice(m * fine, (m + 1) * fine)
+            deep_ref[spot, :] = (
                 taps_ref[0:1, :] * previous + taps_ref[1:2, :] * rows + taps_ref[2:3, :] * following
             ).astype(LOW)
-            deep_ref[m] = deep
-            half = odd_ref if m % 2 else even_ref
-            half[m // 2] = dot_rows(deep, point_ref[...]).astype(LOW)
-            grad = grad_ref[m].astype(jnp.float32)
+            grad = grad_ref[spot, :].astype(jnp.float32)
             sums = [
                 total + jnp.sum(part * grad, axis=0, keepdims=True)
                 for total, part in zip(sums, (previous, rows, following), strict=True)
             ]
         for s, total in enumerate(sums):
             sums_ref[s : s + 1, :] = total
+        part = dot_rows(deep_ref[...], point_ref[...]).astype(LOW)
+        for m in range(windows):
+            half_refs[place(m, windows)][...] = part[m * fine : (m + 1) * fine]
 
     return run_kernel(
         kernel,
-        [mix, before, after, taps, point, grad_deep],
-        [((windows, fine, channels), LOW)]
-        + [((windows // 2, fine, width), LOW)] * 2
-        + [((3, channels), jnp.float32)],
-        flops=2 * windows * fine * width * channels,
-        name="section_deep",
-    )
-
-
-def section_weights(deep, grad_coarse, grad_mix, cot_blocks, coarse_blocks, fine_blocks, count):
-    windows, fine, channels = deep.shape
-    width = cot_blocks[0].shape[1]
+        [up, lateral, point, bias, taps, grad_deep],
+        [((windows * fine, channels), LOW), ((3, channels), jnp.float32)]
+        + halves(windows, (fine, width), LOW),
+        scalars=where,
+        scratch=[
+            pltpu.VMEM((windows * short, width), LOW),
+            pltpu.VMEM((windows * long, width), LOW),
+            pltpu.SemaphoreType.DMA((2 * windows,)),
+        ],
+        far=list(coarse_blocks) + list(fine_blocks),
+    )
+
+
+def section_weights(deep, grad_coarse, grad_mix, cot_blocks, coarse_blocks, fine_blocks, sums, count):
+    windows = len(cot_blocks)
+    channels, width = deep.shape[1], cot_blocks[0].shape[1]
+    fine, own = deep.shape[0] // windows, grad_coarse.shape[0] // windows
     share = channels // count
 
-    def kernel(deep_ref, coarse_ref, mix_ref, *refs):
+    def kernel(*refs):
         cot_refs, refs = refs[:windows], refs[windows:]
         row_refs, refs = refs[:windows], refs[windows:]
-        fine_refs, (out_ref,) = refs[:windows], refs[windows:]
-        pairs = ((deep_ref, cot_refs), (coarse_ref, row_refs), (mix_ref, fine_refs))
-        for which, (left_ref, right_refs) in enumerate(pairs):
-            total = dot_leading(left_ref[0], right_refs[0][...])
-            for m in range(1, windows):
-                total = total + dot_leading(left_ref[m], right_refs[m][...])
-            low = total.astype(LOW)
+        fine_refs, refs = refs[:windows], refs[windows:]
+        deep_ref, coarse_ref, mix_ref, sums_ref, out_ref = refs[:5]
+        cot_all, row_all, fine_all, sems = refs[5:]
+        groups = ((cot_refs, cot_all, fine), (row_refs, row_all, own), (fine_refs, fine_all, fine))
+        copies = [
+            start_copies(
+                [
+                    (blocks[m].at[:size, :], whole.at[m * size : (m + 1) * size, :])
+                    for m in range(windows)
+                ],
+                sems,
+                n * windows,
+            )
+            for n, (blocks, whole, size) in enumerate(groups)
+        ]
+        row = lax.broadcasted_iota(jnp.int32, (channels, 128), 0)
+        column = lax.broadcasted_iota(jnp.int32, (channels, 128), 1)
+        for t in range(count):
+            chosen = ((row == column + t * share) & (column < share)).astype(jnp.float32)
+            out_ref[t, 3 * share :, :128] = dot_rows(
+                sums_ref[...].astype(LOW), chosen.astype(LOW)
+            ).astype(LOW)
+            out_ref[t, 3 * share :, 128:] = jnp.zeros((16, width - 128), LOW)
+        lefts = (deep_ref, coarse_ref, mix_ref)
+        for which, (left_ref, (_, whole, _)) in enumerate(zip(lefts, groups, strict=True)):
+            wait_copies(copies[which])
+            low = dot_leading(left_ref[...], whole[...]).astype(LOW)
             for t in range(count):
                 out_ref[t, which * share : (which + 1) * share, :] = low[t * share : (t + 1) * share]
 
     return run_kernel(
         kernel,
-        [deep, grad_coarse, grad_mix] + list(cot_blocks) + list(coarse_blocks) + list(fine_blocks),
-        [((count, 3 * share, width), LOW)],
-        flops=5 * windows * fine * width * channels,
-        name="section_weights",
+        [deep, grad_coarse, grad_mix, sums],
+        [((count, 3 * share + 16, width), LOW)],
+        scratch=[
+            pltpu.VMEM((windows * fine, width), LOW),
+            pltpu.VMEM((windows * own, width), LOW),
+            pltpu.VMEM((windows * fine, width), LOW),
+            pltpu.SemaphoreType.DMA((3 * windows,)),
+        ],
+        far=list(cot_blocks) + list(coarse_blocks) + list(fine_blocks),
     )[0]
 
 
@@ -801,34 +847,35 @@
 
 
 def send_sum(cells, mask, dtype):
-    return dp_flip(cells.astype(dtype), mask).astype(jnp.float32)
-
-
-def core_pairs(even, odd):
-    return even.astype(jnp.float32) + dp_flip(odd, 1).astype(jnp.float32)
+    return dp_flip(cells.astype(dtype), mask)
+
+
+def core_pairs(blocks):
+    chips = len(blocks) // 2
+    return [
+        mine.astype(jnp.float32) + dp_flip(theirs, 1).astype(jnp.float32)
+        for mine, theirs in zip(blocks[:chips], blocks[chips:], strict=True)
+    ]
 
 
 def corner_sums(pairs, dtype):
-    half = half_rows(pairs, 1)
-    return send_sum(pairs[3, :half], 2, dtype), send_sum(pairs[3, half:], 4, dtype)
+    half = half_rows(pairs[3])
+    return send_sum(pairs[3][:half], 2, dtype), send_sum(pairs[3][half:], 4, dtype)
 
 
 def chip_sums(pairs, corners, dtype):
-    half = half_rows(pairs, 1)
-    near = jnp.concatenate([pairs[1, :half], pairs[1, half:] + corners[1]], axis=0)
-    far = jnp.concatenate([pairs[2, :half] + corners[0], pairs[2, half:]], axis=0)
-    return pairs[0] + send_sum(near, 2, dtype) + send_sum(far, 4, dtype)
+    half = half_rows(pairs[3])
+    corners = [corner.astype(jnp.float32) for corner in corners]
+    near = jnp.concatenate([pairs[1][:half], pairs[1][half:] + corners[1]], axis=0)
+    far = jnp.concatenate([pairs[2][:half] + corners[0], pairs[2][half:]], axis=0)
+    near, far = send_sum(near, 2, dtype), send_sum(far, 4, dtype)
+    return pairs[0] + near.astype(jnp.float32) + far.astype(jnp.float32)
 
 
 def direct_sums(pairs, dtype):
-    return pairs[0] + sum(send_sum(pairs[chip], 2 * chip, dtype) for chip in (1, 2, 3))
-
-
-def scatter_halves(even, odd, small=False):
-    pairs, dtype = core_pairs(even, odd), even.dtype
-    if small:
-        return direct_sums(pairs, dtype)
-    return chip_sums(pairs, corner_sums(pairs, dtype), dtype)
+    return pairs[0] + sum(
+        send_sum(pairs[chip], 2 * chip, dtype).astype(jnp.float32) for chip in (1, 2, 3)
+    )
 
 
 def gather_dp(shard):
@@ -974,6 +1021,7 @@
         rel_turned,
         attn_blocks,
         local_heads,
+        own,
     )
     resid_one, unit_two, scale_two, normed_two = second_norm(
         attn_parts[0],
@@ -1033,31 +1081,34 @@
     ffn_out = scatter_dp(
         feed_forward_weights(
             where, normed_two_all, grad_ffn_all, hidden_low, grad_hidden_pre, 1
-        )[0][0]
+        )[0]
     ).astype(jnp.float32)
 
-    head_parts, (grad_attn_all, grad_heads, grad_normed_part, bias_sums, rel_grad) = (
-        attention_backward(
-            where, spread_blocks(grad_attn), saved, rel_turned, basis_turned, local_heads
-        )
-    )
+    head_parts, (grad_attn_all, grad_heads, bias_sums, rel_grad, own_sums) = attention_backward(
+        where,
+        spread_blocks(grad_attn),
+        saved,
+        rel_turned,
+        basis_turned,
+        gain_vals[:1],
+        sums_two,
+        local_heads,
+        own,
+    )
+    head_received = collect_blocks(head_parts[1:])
     grad_resid_in = first_norm_back(
-        where,
-        head_parts[0],
-        collect_blocks(head_parts[1:]),
-        saved[2],
-        saved[3],
-        gain_vals[:1],
-        grad_resid_one,
-    )
-    weights, _, small, _ = attention_weights(
-        where, saved, grad_attn_all, grad_heads, grad_normed_part, gain_vals[:1], sums_two,
-        bias_sums, rel_grad, 1,
-    )
-    attn_out = scatter_dp(weights[0]).astype(jnp.float32)
-    norm_cols = jnp.swapaxes(small[0, :6].reshape(6, windows, channels), 0, 1)
-    head_cols = small[0, 8 : 10 + BASIS, :keys].reshape(2 + BASIS, local_heads, KEYD)
-    head_cols = jnp.transpose(head_cols, (2, 0, 1))
+        where, head_parts[0], head_received, saved[2], saved[3], gain_vals[:1], grad_resid_one
+    )
+    weights = attention_weights(
+        where, saved, grad_attn_all, grad_heads, own_sums, head_received, bias_sums, rel_grad, 1
+    )[0]
+    attn_out = scatter_dp(weights).astype(jnp.float32)
+    norm_sums = own_sums[:6]
+    for block in head_received:
+        norm_sums = norm_sums + block[own : own + 6].astype(jnp.float32)
+    norm_cols = jnp.swapaxes(norm_sums.reshape(6, windows, channels), 0, 1)
+    head_cols = jnp.concatenate([bias_sums, rel_grad], axis=0)
+    head_cols = jnp.transpose(head_cols.reshape(2 + BASIS, local_heads, KEYD), (2, 0, 1))
     heads_cols = jnp.concatenate(
         [
             head_cols[:, 2:].reshape(windows, -1),
@@ -1069,13 +1120,12 @@
     small_out = scatter_dp(jnp.concatenate([norm_cols.reshape(windows, -1), heads_cols], axis=1))
     small_out = small_out[0]
     n_norm = 6 * channels
-    group_cols = jnp.concatenate([small_out[:n_norm].reshape(6, channels), grad_section_small.T])
-    group_cols = jnp.swapaxes(group_cols.reshape(10, count, -1), 0, 1).reshape(count, -1)
-    group_cols = to_own(group_cols)
-    norm_out = group_cols[0]
+    section_sums = grad_section_small.T
     for k in range(1, count):
-        norm_out = norm_out + from_ahead(group_cols[k], count - k)
-    norm_out = norm_out.reshape(10, -1)
+        section_sums = section_sums + from_ahead(grad_section_small.T, k)
+    norm_out = jnp.concatenate([small_out[:n_norm].reshape(6, channels), section_sums])
+    share = channels // count
+    norm_out = lax.dynamic_slice_in_dim(norm_out, lax.axis_index("tensor") * share, share, 1)
     heads_out = small_out[n_norm:]
     return (
         section_out[None],
@@ -1145,22 +1195,34 @@
             content_bias.T.reshape(-1),
             position_bias.T.reshape(-1),
         ]
-    )[None]
+    )
+    entries = packed.shape[0]
+    packed = jnp.pad(packed[None], ((0, 0), (0, width - entries)))
+    ends = [cotangent[0, :1], cotangent[0, -1:], encoder[0, :1], encoder[0, -1:]]
+    packed = jnp.concatenate([packed] + ends + [jnp.zeros((3, width), LOW)], axis=0)
+    raw = spread_blocks(jnp.concatenate([activations[0], packed], axis=0))
     attn_shard = jnp.concatenate([query_weight, key_weight, value_weight, output_weight.T], axis=1)
+    attn_rows = attn_shard.shape[0]
     attn_chips = chips_of(attn_shard)
-    line = spread_blocks(packed)
-    section_shard = jnp.concatenate([pointwise_weight, upsample_weight.T, lateral_weight.T], axis=0)
+    w_ffn = gather_dp(jnp.concatenate([expand_weight, contract_weight.T], axis=1))
+    raw, attn_chips, cot, section_shard = join(
+        raw, attn_chips, cotangent[0], [pointwise_weight, upsample_weight.T, lateral_weight.T]
+    )
+    section_shard = jnp.concatenate(section_shard, axis=0)
     w_section = lax.all_gather(section_shard, "tensor", axis=0, tiled=True)
-    line, rows = join(line, activations[0])
-    raw = spread_blocks(rows)
-    small_chips = jnp.concatenate(chips_of(jnp.concatenate(line, axis=0)), axis=0)
-    small_blocks = [small_chips, dp_flip(small_chips, 1)]
+    blank = jnp.zeros((14, width), LOW)
+    cot = [cot, raw[-1][own + 2 : own + 3], raw[1][own + 1 : own + 2], blank]
+    cot = jnp.concatenate(cot, axis=0)
+    enc = [encoder[0], raw[-1][own + 4 : own + 5], raw[1][own + 3 : own + 4], blank]
+    enc = jnp.concatenate(enc, axis=0)
+    line = jnp.concatenate([block[own : own + 1, :entries] for block in raw], axis=0)
+    small_rows = gather_dp(line)
     attn_blocks = both_cores(*attn_chips)
-    attn_blocks, small_blocks, raw, cot = join(attn_blocks, small_blocks, raw, cotangent[0])
+    small_rows, attn_blocks, cot = join(small_rows, attn_blocks, cot)
     cot_chips = chips_of(cot)
     basis_turned = jnp.pad(basis_table(length, BASIS).astype(LOW)[::-1], ((0, 1), (0, 0)))
     rows, (depth_taps, bias_section, rel_turned, content_flat, position_flat) = unpack_small(
-        where, small_blocks, basis_turned, width, local_heads, count
+        where, small_rows, basis_turned, width, local_heads, count
     )
     gain_one, gain_two, shift_one, shift_two, species_row = rows
     attn_parts, saved = attention_forward(
@@ -1170,134 +1232,154 @@
         rel_turned,
         attn_blocks,
         local_heads,
+        own,
     )
     attn_parts, cot_chips = join(attn_parts, cot_chips)
 
     attn_received = collect_blocks(attn_parts[1:])
     cot_blocks = both_cores(*cot_chips)
-    grad_deep, head, tail, w_point, w_up, w_lateral = section_grad_deep(
-        cot_blocks, w_section, count
-    )
-    before, following = edges(head, tail)
-    attn_received, before, following, expand, contract = join(
-        attn_received, before, following, expand_weight, contract_weight
-    )
+    grad_deep, grad_mix, grad_coarse, bias_grad, *halves_two, w_point, w_up, w_lateral = (
+        section_gradient(where, cot_blocks, w_section, depth_taps, count)
+    )
+    attn_received, halves_two = join(attn_received, halves_two)
 
     resid_one, unit_two, scale_two, normed_two = second_norm(
-        attn_parts[0], attn_received, [raw[0], species_row], gain_two, shift_two
-    )
-    normed_two, before, following, expand, contract = join(
-        normed_two, before, following, expand, contract
-    )
-    w_ffn = gather_dp(jnp.concatenate([expand, contract.T], axis=1))
+        attn_parts[0], attn_received, [activations[0], species_row], gain_two, shift_two
+    )
+    normed_two, halves_two = join(normed_two, halves_two)
     normed_blocks = spread_blocks(normed_two)
-    grad_mix, grad_coarse, even, odd, bias_grad = section_grad_mix(
-        grad_deep, before, following, depth_taps, w_up
-    )
-    grad_resid_two = direct_sums(core_pairs(even, odd), LOW)
-    normed_blocks, grad_resid_two, enc = join(normed_blocks, grad_resid_two, encoder[0])
+    grad_resid_two = direct_sums(core_pairs(halves_two), LOW)
+    normed_blocks, grad_resid_two, enc = join(normed_blocks, grad_resid_two, enc)
 
     grad_ffn = spread_blocks(grad_resid_two.astype(LOW))
     contract_part, normed_two_all, hidden_low, slope = feed_forward_up(where, normed_blocks, w_ffn)
     enc_chips = chips_of(enc)
-    grad_ffn, contract_part, enc_chips = join(grad_ffn, contract_part, enc_chips)
+    grad_ffn, contract_part, enc_chips, late_mix = join(
+        grad_ffn, contract_part, enc_chips, grad_mix
+    )
 
     contract_sum = scatter_tensor(contract_part)
+    encoder_part = section_grad_encoder(where, late_mix, w_lateral, lax.axis_size("dp"))
     enc_blocks = both_cores(*enc_chips)
     ffn_parts, (grad_ffn_all, grad_hidden_pre) = feed_forward_back(grad_ffn, slope, w_ffn)
     ffn_received = collect_blocks(ffn_parts[1:])
-    ffn_grads = feed_forward_weights(
-        where, normed_two_all, grad_ffn_all, hidden_low, grad_hidden_pre, 1
-    )[0][0]
-    enc_pairs = core_pairs(*section_grad_encoder(grad_mix, w_lateral))
-    coarse_chips = chips_of((resid_one + contract_sum.astype(jnp.float32)).astype(LOW))
-    ffn_received, ffn_grads, enc_pairs, enc_blocks, coarse_chips = join(
-        ffn_received, ffn_grads, enc_pairs, enc_blocks, coarse_chips
-    )
+    ffn_halves = feed_forward_weights(
+        where, normed_two_all, grad_ffn_all, hidden_low, grad_hidden_pre, len(attn_blocks)
+    )
+    ffn_received, ffn_halves, enc_blocks, encoder_part = join(
+        ffn_received, ffn_halves, enc_blocks, encoder_part
+    )
+    encoder_grad = scatter_dp(encoder_part).astype(jnp.float32)
 
     grad_resid_one, grad_attn, sums_two = second_norm_back(
         ffn_parts[0], ffn_received, unit_two, scale_two, gain_two, grad_resid_two
     )
-    grad_attn, ffn_grads, coarse_chips = join(grad_attn, ffn_grads, coarse_chips)
+    coarse = (resid_one + contract_sum.astype(jnp.float32)).astype(LOW)
+    grad_attn = [grad_attn, coarse[:1], coarse[-1:], jnp.zeros((6, width), LOW)]
+    grad_attn, ffn_halves = join(jnp.concatenate(grad_attn, axis=0), ffn_halves)
     grad_attn_blocks = spread_blocks(grad_attn)
-    ffn_out = scatter_dp(ffn_grads).astype(jnp.float32)
-    encoder_grad = chip_sums(enc_pairs, corner_sums(enc_pairs, LOW), LOW)
+    ffn_pairs = core_pairs(ffn_halves)
+    grad_attn_blocks, ffn_pairs = join(grad_attn_blocks, ffn_pairs)
+
+    coarse = [coarse, grad_attn_blocks[-1][own + 1 : own + 2], grad_attn_blocks[1][own : own + 1]]
+    coarse_chips = chips_of(jnp.concatenate(coarse + [blank], axis=0))
+    ffn_corners = corner_sums(ffn_pairs, LOW)
+    head_parts, (grad_attn_all, grad_heads, bias_sums, rel_grad, own_sums) = attention_backward(
+        where,
+        grad_attn_blocks,
+        saved,
+        rel_turned,
+        basis_turned,
+        gain_one,
+        sums_two,
+        local_heads,
+        own,
+    )
+    head_parts, ffn_corners = join(head_parts, ffn_corners)
+    head_received = collect_blocks(head_parts[1:])
+    ffn_out = chip_sums(ffn_pairs, ffn_corners, LOW)
     coarse_blocks = both_cores(*coarse_chips)
-    section_mix, head, tail = section_mixture(
-        coarse_blocks, enc_blocks, w_up, w_lateral, bias_section
-    )
-    before, following = edges(head, tail)
-    grad_attn_blocks, encoder_grad, before, following = join(
-        grad_attn_blocks, encoder_grad, before, following
-    )
-
-    head_parts, (grad_attn_all, grad_heads, grad_normed_part, bias_sums, rel_grad) = (
-        attention_backward(
-            where, grad_attn_blocks, saved, rel_turned, basis_turned, local_heads
-        )
-    )
-    head_parts, before, following = join(head_parts, before, following)
-    head_received = collect_blocks(head_parts[1:])
-    deep_rows, out_even, out_odd, taps_grad = section_deep(
-        section_mix, before, following, depth_taps, w_point, grad_deep
-    )
+    deep_rows, taps_grad, *out_halves = section_forward(
+        where,
+        coarse_blocks,
+        enc_blocks,
+        w_up,
+        w_lateral,
+        w_point,
+        bias_section,
+        depth_taps,
+        grad_deep,
+        count,
+    )
+    section_sums = jnp.pad(jnp.concatenate([taps_grad, bias_grad], axis=0), ((0, 12), (0, 0)))
     cols_part = section_weights(
-        deep_rows, grad_coarse, grad_mix, cot_blocks, coarse_blocks, enc_blocks, count
-    )
-    even, odd, small_even, small_odd = attention_weights(
+        deep_rows,
+        grad_coarse,
+        grad_mix,
+        cot_blocks,
+        coarse_blocks,
+        enc_blocks,
+        section_sums,
+        count,
+    )
+    section_cols = scatter_tensor(cols_part)[0].astype(jnp.float32)
+    out_pairs = core_pairs(out_halves)
+    head_received, out_pairs, ffn_out = join(head_received, out_pairs, ffn_out)
+
+    grad_resid_in = first_norm_back(
+        where, head_parts[0], head_received, saved[2], saved[3], gain_one, grad_resid_one
+    )
+    attn_halves = attention_weights(
         where,
         saved,
         grad_attn_all,
         grad_heads,
-        grad_normed_part,
-        gain_one,
-        sums_two,
+        own_sums,
+        head_received,
         bias_sums,
         rel_grad,
         len(attn_blocks),
     )
-    head_received, ffn_out, out_even, out_odd, even, odd, small_even, small_odd, cols_part = join(
-        head_received, ffn_out, out_even, out_odd, even, odd, small_even, small_odd, cols_part
-    )
-
-    section_cols = scatter_tensor(cols_part)[0].astype(jnp.float32)
-    grad_resid_in = first_norm_back(
-        where, head_parts[0], head_received, saved[2], saved[3], gain_one, grad_resid_one
-    )
-    section_out = scatter_halves(out_even, out_odd).astype(LOW)
-    attn_out = scatter_halves(even, odd)
-    small_out = scatter_halves(small_even, small_odd, small=True)
-
-    n_norm = 4 + SPECIES
-    group = share * count
-    group_cols = jnp.concatenate([small_out[:n_norm, :group], taps_grad, bias_grad], axis=0)
-    norm_out = group_cols
-    for k in range(1, count):
-        norm_out = norm_out + from_ahead(group_cols, k)
-    norm_out = lax.dynamic_slice_in_dim(norm_out, lax.axis_index("tensor") * share, share, 1)
+    attn_pairs = core_pairs(attn_halves)
+    out_corners = corner_sums(out_pairs, LOW)
+    attn_pairs, out_corners, grad_resid_in, encoder_grad = join(
+        attn_pairs, out_corners, grad_resid_in, encoder_grad
+    )
+    attn_out = direct_sums(attn_pairs, LOW)
+    section_out = chip_sums(out_pairs, out_corners, LOW).astype(LOW)
+
+    small_out, attn_out = attn_out[attn_rows:], attn_out[:attn_rows]
+    norm_out = lax.dynamic_slice_in_dim(
+        small_out[: 4 + SPECIES], lax.axis_index("tensor") * share, share, 1
+    )
     part = KEYD // lax.axis_size("dp")
-    heads_out = small_out[8 : 10 + BASIS, :keys].reshape(2 + BASIS, local_heads, KEYD)[:, :, :part]
-    heads_out = jnp.transpose(heads_out, (2, 0, 1))
+
+    def heads_of(rows):
+        return rows.reshape(rows.shape[0], local_heads, KEYD)[:, :, :part]
+
+    bias_out = jnp.transpose(heads_of(small_out[8:10, :keys]), (2, 0, 1))
+    rel_out = [small_out[:, 256 : 256 + keys], small_out[:, 256 + keys : 256 + 2 * keys]]
+    rel_out = jnp.transpose(heads_of(jnp.concatenate(rel_out, axis=0)), (2, 0, 1))
     return (
         section_out[None],
         grad_resid_in,
         encoder_grad[None],
         norm_out[0:2],
         norm_out[2:4],
-        norm_out[4:n_norm],
+        norm_out[4:],
         attn_out[:, :keys],
         attn_out[:, keys : 2 * keys],
         attn_out[:, 2 * keys : 2 * keys + values],
         attn_out[:, 2 * keys + values :].T,
         ffn_out[:, :hidden_count],
         ffn_out[:, hidden_count:].T,
-        heads_out[:, 2:],
-        heads_out[:, 0],
-        heads_out[:, 1],
+        rel_out,
+        bias_out[:, 0],
+        bias_out[:, 1],
         section_cols[share : 2 * share].T,
-        section_cols[2 * share :].T,
-        norm_out[n_norm : n_norm + 3],
-        norm_out[n_norm + 3],
+        section_cols[2 * share : 3 * share].T,
+        section_cols[3 * share : 3 * share + 3, :share],
+        section_cols[3 * share + 3, :share],
         section_cols[:share],
     )
 

time: 364 us -> 341 us (0.937)
  waiting for transfers between devices: 133 us -> 113 us
  starting transfers between devices: 97.8 us -> 83 us
  blocking collectives: 0 us -> 9.24 us
  Pallas kernels: 83 us -> 74.3 us
  local copies, waits for them, and re-layouts: 14.6 us -> 20.7 us
  other arithmetic: 20.2 us -> 24 us
    reduce_scatter x2, waiting for transfers between devices: 22.2 us -> 0.01 us  [scatter_tensor(): return lax.psum_scatter(whole, 'tensor', scatter_dimension=0, tiled=True)]
    ppermute x27 -> x21, waiting for transfers between devices: 52.2 us -> 67.5 us  [from_ahead(): lax.ppermute(rows, 'tensor', [((i + step) % count, i) for i in range(coun...]
    all_gather x1, waiting for transfers between devices: 12.4 us -> 0.01 us  [gather_dp(): return lax.all_gather(shard, 'dp', axis=0, tiled=True)]
    ppermute x55 -> x58, starting transfers between devices: 46.3 us -> 35.9 us  [dp_flip(): return lax.ppermute(cells, 'dp', [(i, i ^ mask) for i in range(count)])]
    ppermute x4 -> x0, starting transfers between devices: 9.84 us -> none  [the longest x2 7.04 us: edges(): lax.ppermute(tail, 'tensor', [(i, i + 1) for i in range(ends)])]
    all_gather x0 -> x1, blocking collectives: none -> 9.24 us  [gather_dp(): return lax.all_gather(shard, 'dp', axis=0, tiled=True)]
    pallas_call x16 -> x14, Pallas kernels: 83 us -> 74.3 us  [run_kernel(): pl.pallas_call(kernel, in_specs=specs, out_specs=[whole] * len(outs) + [o...]
    ppermute x27 -> x21, starting transfers between devices: 41.5 us -> 46.9 us  [from_ahead(): lax.ppermute(rows, 'tensor', [((i + step) % count, i) for i in range(coun...]
  transfers between devices with their start and end apart: 91 -> 84, of which waited for: 39 -> 26; matrix products, arithmetic and copies ran while one was open for 7% -> 8% of each run, Pallas kernels for 21% -> 22%
where the time goes in v4:
time: 341 us; the launch traced here: 340 us
  waiting for transfers between devices  113 us (33%)
  starting transfers between devices  83 us (24%)
  Pallas kernels  74.3 us (22%)
  other arithmetic  24 us (7%)
  local copies, waits for them, and re-layouts  20.7 us (6%)
  between operations  15.7 us (5%)
  blocking collectives  9.24 us (3%)
    pallas_call x14, Pallas kernels, run_kernel(): pl.pallas_call(kernel, in_specs=specs, out_specs=[whole] * len(outs) + [o...  74.3 us
    ppermute x21, waiting for transfers between devices, from_ahead(): lax.ppermute(rows, 'tensor', [((i + step) % count, i) for i in range(coun...  67.5 us
    ppermute x21, starting transfers between devices, from_ahead(): lax.ppermute(rows, 'tensor', [((i + step) % count, i) for i in range(coun...  46.9 us
    ppermute x58, waiting for transfers between devices, dp_flip(): return lax.ppermute(cells, 'dp', [(i, i ^ mask) for i in range(count)])  45.7 us
    ppermute x58, starting transfers between devices, dp_flip(): return lax.ppermute(cells, 'dp', [(i, i ^ mask) for i in range(count)])  35.9 us
    all_gather x1, blocking collectives, gather_dp(): return lax.all_gather(shard, 'dp', axis=0, tiled=True)  9.24 us
  transfers between devices with their start and end apart: 84, of which 26 were waited for; matrix products, arithmetic and copies ran while one was open for 8% of the time, Pallas kernels for 22%

profile of v4, /device:TPU:0, one launch (start us, length us, event | category | flops | bytes accessed | tf_op | source)
XLA Modules:
  0.0 340.1 jit_solution(16980561755458564672)
XLA Ops:
  15.4 5.1 %collective-permute-start = (bf16[72,1536]{1,0:T(8,128)(2,1)S(1)}, bf16[72,1536]{1,0:T(8,128)(2,1)S(1)}, u32[]{:S(2)}, u32[]{:S(2)}) collective-permute-start(bf16[72,1536]{1,0:T(8,128)(2,1)S(1)} %concatenate.57.refs_0_), channel_id=1, source_target_pairs={{1,0},{2,1},{3,2},{0,3},{5,4},{6,5},{7,6},{4,7},{9,8},{10,9},{11,1... | collective-permute-start | bytes 663560 | tf_op jit(solution)/shard_map/ppermute | solution.py:816
  26.2 14.2 %collective-permute-done.1.refs_2_ = bf16[72,1536]{1,0:T(8,128)(2,1)S(1)} collective-permute-done((bf16[72,1536]{1,0:T(8,128)(2,1)S(1)}, bf16[72,1536]{1,0:T(8,128)(2,1)S(1)}, u32[]{:S(2)}, u32[]{:S(2)}) %collective-permute-start.1) | collective-permute-done | bytes 221216 | tf_op jit(solution)/shard_map/ppermute | solution.py:816
  45.8 9.2 %all-gather = bf16[8,4,1024]{2,1,0:T(4,128)(2,1)S(1)} all-gather(bf16[1,4,1024]{2,1,0:T(4,128)(2,1)S(1)} %maximum_bitcast_fusion), channel_id=1, replica_groups=mesh['dp'=8,'tensor'=4] {'dp'}, dimensions={0}, use_global_device_ids=true | all-gather | bytes 73728 | tf_op jit(solution)/shard_map/all_gather | solution.py:882
  60.7 7.7 %attention_forward.1 = (f32[64,1536]{1,0:T(8,128)}, bf16[64,1536]{1,0:T(8,128)(2,1)S(1)}, bf16[64,1536]{1,0:T(8,128)(2,1)S(1)}, bf16[64,1536]{1,0:T(8,128)(2,1)}...) custom-call(s32[3]{0:T(128)S(1)} %pad_add_fusion.where_ref, ...), custom_call_target="tpu_custom_call" | custom-call | tf_op jit(solution)/shard_map/attention_forward/pallas_call | solution.py:75
  68.4 9.1 %collective-permute-done.11.refs_4_ = bf16[144,1536]{1,0:T(8,128)(2,1)} collective-permute-done((bf16[144,1536]{1,0:T(8,128)(2,1)S(1)}, bf16[144,1536]{1,0:T(8,128)(2,1)}, u32[]{:S(2)}, u32[]{:S(2)}) %collective-permute-start.11) | collective-permute-done | bytes 442400 | tf_op jit(solution)/shard_map/ppermute | solution.py:834
  84.3 8.0 %section_gradient.1 = (bf16[1024,192]{1,0:T(8,128)(2,1)}, bf16[1024,192]{1,0:T(8,128)(2,1)}, bf16[512,192]{1,0:T(8,128)(2,1)}, f32[1,192]{1,0:T(1,128)S(1)}, bf1...) custom-call(s32[3]{0:T(128)S(1)} %pad_add_fusion.where_ref, ...), custom_call_target="tpu_custom_call" | custom-call | tf_op jit(solution)/shard_map/section_gradient/pallas_call | solution.py:75
  103.2 5.2 %collective-permute-start.20 = (bf16[64,1536]{1,0:T(8,128)(2,1)S(1)}, bf16[64,1536]{1,0:T(8,128)(2,1)S(1)}, u32[]{:S(2)}, u32[]{:S(2)}) collective-permute-start(bf16[64,1536]{1,0:T(8,128)(2,1)S(1)} %get-tuple-element.309.refs_0_), channel_id=1, source_target_pairs={{1,0},{2,1},{3,2},{0,3},{5,4},{6,5},{7,6},{4,7},{9,8},{10,9},{11,1... | collective-permute-start | bytes 589832 | tf_op jit(solution)/shard_map/ppermute | solution.py:816
  109.3 5.7 %collective-permute-start.22 = (bf16[64,1536]{1,0:T(8,128)(2,1)S(1)}, bf16[64,1536]{1,0:T(8,128)(2,1)S(1)}, u32[]{:S(2)}, u32[]{:S(2)}) collective-permute-start(bf16[64,1536]{1,0:T(8,128)(2,1)S(1)} %get-tuple-element.309.refs_0_), channel_id=1, source_target_pairs={{3,0},{0,1},{1,2},{2,3},{7,4},{4,5},{5,6},{6,7},{11,8},{8,9},{9,10... | collective-permute-start | bytes 589832 | tf_op jit(solution)/shard_map/ppermute | solution.py:816
  116.0 10.0 %collective-permute-done.21.refs_2_ = bf16[64,1536]{1,0:T(8,128)(2,1)S(1)} collective-permute-done((bf16[64,1536]{1,0:T(8,128)(2,1)S(1)}, bf16[64,1536]{1,0:T(8,128)(2,1)S(1)}, u32[]{:S(2)}, u32[]{:S(2)}) %collective-permute-start.21) | collective-permute-done | bytes 196640 | tf_op jit(solution)/shard_map/ppermute | solution.py:816
  130.8 5.1 %collective-permute-done.30.refs_1_ = bf16[64,1536]{1,0:T(8,128)(2,1)S(1)} collective-permute-done((bf16[64,1536]{1,0:T(8,128)(2,1)S(1)}, bf16[64,1536]{1,0:T(8,128)(2,1)S(1)}, u32[]{:S(2)}, u32[]{:S(2)}) %collective-permute-start.30) | collective-permute-done | bytes 196640 | tf_op jit(solution)/shard_map/ppermute | solution.py:816
  135.9 9.5 %collective-permute-start.32 = (bf16[64,1536]{1,0:T(8,128)(2,1)S(1)}, bf16[64,1536]{1,0:T(8,128)(2,1)S(1)}, u32[]{:S(2)}, u32[]{:S(2)}) collective-permute-start(bf16[64,1536]{1,0:T(8,128)(2,1)S(1)} %convert_element_type.229.refs_0_), channel_id=1, source_target_pairs={{3,0},{0,1},{1,2},{2,3},{7,4},{4,5},{5,6},{6,7},{11,8},{8,9},{9,10... | collective-permute-start | bytes 589832 | tf_op jit(solution)/shard_map/ppermute | solution.py:816
  145.4 5.1 %feed_forward_up.1 = (bf16[256,1536]{1,0:T(8,128)(2,1)}, bf16[256,1536]{1,0:T(8,128)(2,1)}, bf16[256,768]{1,0:T(8,128)(2,1)}, f32[256,768]{1,0:T(8,128)}) custom-call(s32[3]{0:T(128)S(1)} %pad_add_fusion.where_ref, bf16[64,1536]{1,0:T(8,128)(2,1)S(1)} %get-tuple-element.309.refs_0_, bf16[64,1536]{1,0:T(8,128)(2,1)S(1)} %collective-permute-done.20.refs_1_, ...), custom_call_target="tpu_custom_call" | custom-call | tf_op jit(solution)/shard_map/feed_forward_up/pallas_call | solution.py:75
  151.3 5.3 %feed_forward_back.1 = (f32[64,1536]{1,0:T(8,128)}, bf16[64,1536]{1,0:T(8,128)(2,1)S(1)}, bf16[64,1536]{1,0:T(8,128)(2,1)S(1)}, bf16[64,1536]{1,0:T(8,128)(2,1)S...) custom-call(bf16[64,1536]{1,0:T(8,128)(2,1)S(1)} %convert_element_type.229.refs_0_, ...), custom_call_target="tpu_custom_call" | custom-call | tf_op jit(solution)/shard_map/feed_forward_back/pallas_call | solution.py:75
  158.1 11.6 %collective-permute-done.36.refs_0_ = bf16[64,1536]{1,0:T(8,128)(2,1)S(1)} collective-permute-done((bf16[64,1536]{1,0:T(8,128)(2,1)S(1)}, bf16[64,1536]{1,0:T(8,128)(2,1)S(1)}, u32[]{:S(2)}, u32[]{:S(2)}) %collective-permute-start.36) | collective-permute-done | bytes 196640 | tf_op jit(solution)/shard_map/ppermute | solution.py:816
  169.7 6.0 %collective-permute-start.37 = (bf16[64,1536]{1,0:T(8,128)(2,1)S(1)}, bf16[64,1536]{1,0:T(8,128)(2,1)S(1)}, u32[]{:S(2)}, u32[]{:S(2)}) collective-permute-start(bf16[64,1536]{1,0:T(8,128)(2,1)S(1)} %get-tuple-element.323), channel_id=1, source_target_pairs={{2,0},{3,1},{0,2},{1,3},{6,4},{7,5},{4,6},{5,7},{10,8},{11,9},{8,1... | collective-permute-start | bytes 589832 | tf_op jit(solution)/shard_map/ppermute | solution.py:816
  175.7 7.2 %collective-permute-done.37.refs_1_ = bf16[64,1536]{1,0:T(8,128)(2,1)S(1)} collective-permute-done((bf16[64,1536]{1,0:T(8,128)(2,1)S(1)}, bf16[64,1536]{1,0:T(8,128)(2,1)S(1)}, u32[]{:S(2)}, u32[]{:S(2)}) %collective-permute-start.37) | collective-permute-done | bytes 196640 | tf_op jit(solution)/shard_map/ppermute | solution.py:816
  186.9 5.0 %feed_forward_weights.1 = (bf16[192,1536]{1,0:T(8,128)(2,1)}, bf16[192,1536]{1,0:T(8,128)(2,1)}, bf16[192,1536]{1,0:T(8,128)(2,1)}, bf16[192,1536]{1,0:T(8,128)(...) custom-call(s32[3]{0:T(128)S(1)} %pad_add_fusion.where_ref, ...), custom_call_target="tpu_custom_call" | custom-call | tf_op jit(solution)/shard_map/feed_forward_weights/pallas_call | solution.py:75
  204.5 14.9 %collective-permute-done.44.refs_2_ = bf16[72,1536]{1,0:T(8,128)(2,1)S(1)} collective-permute-done((bf16[72,1536]{1,0:T(8,128)(2,1)S(1)}, bf16[72,1536]{1,0:T(8,128)(2,1)S(1)}, u32[]{:S(2)}, u32[]{:S(2)}) %collective-permute-start.44) | collective-permute-done | bytes 221216 | tf_op jit(solution)/shard_map/ppermute | solution.py:816
  223.9 8.4 %attention_backward.1 = (f32[64,1536]{1,0:T(8,128)}, bf16[80,1536]{1,0:T(8,128)(2,1)}, bf16[80,1536]{1,0:T(8,128)(2,1)}, bf16[80,1536]{1,0:T(8,128)(2,1)}, bf16[...) custom-call(s32[3]{0:T(128)S(1)} %pad_add_fusion.where_ref, ...), custom_call_target="tpu_custom_call" | custom-call | tf_op jit(solution)/shard_map/attention_backward/pallas_call | solution.py:75
  240.6 5.7 %collective-permute-done.60.refs_6_.refs_14_ = bf16[80,1536]{1,0:T(8,128)(2,1)S(1)} collective-permute-done((bf16[80,1536]{1,0:T(8,128)(2,1)S(1)}, bf16[80,1536]{1,0:T(8,128)(2,1)S(1)}, u32[]{:S(2)}, u32[]{:S(2)}) %collective-permute-start.60) | collective-permute-done | bytes 245792 | tf_op jit(solution)/shard_map/ppermute | solution.py:834
  251.3 11.1 %section_forward.1 = (bf16[1024,192]{1,0:T(8,128)(2,1)}, f32[3,192]{1,0:T(4,128)S(1)}, bf16[128,1536]{1,0:T(8,128)(2,1)}, bf16[128,1536]{1,0:T(8,128)(2,1)}, bf1...) custom-call(s32[3]{0:T(128)S(1)} %pad_add_fusion.where_ref, ...), custom_call_target="tpu_custom_call" | custom-call | tf_op jit(solution)/shard_map/section_forward/pallas_call | solution.py:75
  262.5 6.9 %section_weights.1 = bf16[4,160,1536]{2,1,0:T(8,128)(2,1)} custom-call(bf16[144,1536]{1,0:T(8,128)(2,1)} %copy-done.8, bf16[144,1536]{1,0:T(8,128)(2,1)} %copy-done.16, bf16[144,1536]{1,0:T(8,128)(2,1)} %collective-permute-done.10.refs_2_, bf16[144,1536]{1,0:T(8,128)(2,1)} %copy-done.17, bf16[144,1536]{1,0:T(8,128)(2,1)} %collective-permute-done.11.refs_4_, ...), custom_call_target="tpu_custom_call" | custom-call | tf_op jit(solution)/shard_map/section_weights/pallas_call | solution.py:75
  303.4 5.6 %collective-permute-done.75 = bf16[128,1536]{1,0:T(8,128)(2,1)} collective-permute-done((bf16[128,1536]{1,0:T(8,128)(2,1)}, bf16[128,1536]{1,0:T(8,128)(2,1)}, u32[]{:S(2)}, u32[]{:S(2)}) %collective-permute-start.75) | collective-permute-done | bytes 393248 | tf_op jit(solution)/shard_map/ppermute | solution.py:834
  312.2 8.1 %collective-permute-done.78 = bf16[208,1024]{1,0:T(8,128)(2,1)S(1)} collective-permute-done((bf16[208,1024]{1,0:T(8,128)(2,1)S(1)}, bf16[208,1024]{1,0:T(8,128)(2,1)S(1)}, u32[]{:S(2)}, u32[]{:S(2)}) %collective-permute-start.78) | collective-permute-done | bytes 426016 | tf_op jit(solution)/shard_map/ppermute | solution.py:834
  (393 shorter events, 134.7 us)
Async XLA Ops:
  7.2 77.0 %all-gather.4.cloned.1.call-start = ((), (), s32[]{:S(2)}) async-start(), calls=%async_computation.3 | async-start | bytes 2211840 | tf_op jit(solution)/shard_map/all_gather | solution.py:1212
  42.8 102.6 %all-gather.6.cloned.1.call-start = ((), (), s32[]{:S(2)}) async-start(), calls=%async_computation.4 | async-start | bytes 5308416 | tf_op jit(solution)/shard_map/all_gather | solution.py:882
  43.8 150.6 %reduce-scatter.4.cloned.1.call-start = ((), (), s32[]{:S(2)}) async-start(), calls=%async_computation.5 | async-start | bytes 983040 | tf_op jit(solution)/shard_map/reduce_scatter | solution.py:890
  55.8 21.7 %collective-permute-start.11 = (bf16[144,1536]{1,0:T(8,128)(2,1)S(1)}, bf16[144,1536]{1,0:T(8,128)(2,1)}, u32[]{:S(2)}, u32[]{:S(2)}) collective-permute-start(bf16[144,1536]{1,0:T(8,128)(2,1)S(1)} %get-tuple-element.269.refs_0_), channel_id=1, source_target_pairs={{0,16},{4,20},{8,24},{12,28},{16,0},{20,4},{24,8},{28,12},{1,17},{... | collective-permute-start | bytes 1327112 | tf_op jit(solution)/shard_map/ppermute | solution.py:834
  57.3 20.2 %collective-permute-start.12 = (bf16[144,1536]{1,0:T(8,128)(2,1)S(1)}, bf16[144,1536]{1,0:T(8,128)(2,1)}, u32[]{:S(2)}, u32[]{:S(2)}) collective-permute-start(bf16[144,1536]{1,0:T(8,128)(2,1)S(1)} %get-tuple-element.269.refs_0_), channel_id=1, source_target_pairs={{0,24},{4,28},{8,16},{12,20},{16,8},{20,12},{24,0},{28,4},{1,25},{... | collective-permute-start | bytes 1327112 | tf_op jit(solution)/shard_map/ppermute | solution.py:834
  126.0 24.5 %collective-permute-start.33 = (bf16[144,1536]{1,0:T(8,128)(2,1)S(1)}, bf16[144,1536]{1,0:T(8,128)(2,1)}, u32[]{:S(2)}, u32[]{:S(2)}) collective-permute-start(bf16[144,1536]{1,0:T(8,128)(2,1)S(1)} %get-tuple-element.389.refs_8_.refs_16_), channel_id=1, source_target_pairs={{0,8},{4,12},{8,0},{12,4},{16,24},{20,28},{24,16},{28,20},{1,9},{5... | collective-permute-start | bytes 1327112 | tf_op jit(solution)/shard_map/ppermute | solution.py:834
  127.5 23.0 %collective-permute-start.34 = (bf16[144,1536]{1,0:T(8,128)(2,1)S(1)}, bf16[144,1536]{1,0:T(8,128)(2,1)}, u32[]{:S(2)}, u32[]{:S(2)}) collective-permute-start(bf16[144,1536]{1,0:T(8,128)(2,1)S(1)} %get-tuple-element.389.refs_8_.refs_16_), channel_id=1, source_target_pairs={{0,16},{4,20},{8,24},{12,28},{16,0},{20,4},{24,8},{28,12},{1,17},{... | collective-permute-start | bytes 1327112 | tf_op jit(solution)/shard_map/ppermute | solution.py:834
  128.1 22.5 %collective-permute-start.35 = (bf16[144,1536]{1,0:T(8,128)(2,1)S(1)}, bf16[144,1536]{1,0:T(8,128)(2,1)}, u32[]{:S(2)}, u32[]{:S(2)}) collective-permute-start(bf16[144,1536]{1,0:T(8,128)(2,1)S(1)} %get-tuple-element.389.refs_8_.refs_16_), channel_id=1, source_target_pairs={{0,24},{4,28},{8,16},{12,20},{16,8},{20,12},{24,0},{28,4},{1,25},{... | collective-permute-start | bytes 1327112 | tf_op jit(solution)/shard_map/ppermute | solution.py:834
  129.6 20.9 %collective-permute-start.31 = (bf16[64,1536]{1,0:T(8,128)(2,1)S(1)}, bf16[64,1536]{1,0:T(8,128)(2,1)S(1)}, u32[]{:S(2)}, u32[]{:S(2)}) collective-permute-start(bf16[64,1536]{1,0:T(8,128)(2,1)S(1)} %convert_element_type.229.refs_0_), channel_id=1, source_target_pairs={{2,0},{3,1},{0,2},{1,3},{6,4},{7,5},{4,6},{5,7},{10,8},{11,9},{8,1... | collective-permute-start | bytes 589832 | tf_op jit(solution)/shard_map/ppermute | solution.py:816
  150.6 139.0 %reduce-scatter.6.cloned.1.call-start = ((), (), s32[]{:S(2)}) async-start(), calls=%async_computation.6 | async-start | bytes 3538944 | tf_op jit(solution)/shard_map/reduce_scatter | solution.py:886
  157.1 34.9 %collective-permute-start.39 = (bf16[144,1536]{1,0:T(8,128)(2,1)S(1)}, bf16[144,1536]{1,0:T(8,128)(2,1)}, u32[]{:S(2)}, u32[]{:S(2)}) collective-permute-start(bf16[144,1536]{1,0:T(8,128)(2,1)S(1)} %copy-done.10), channel_id=1, source_target_pairs={{0,4},{4,0},{8,12},{12,8},{16,20},{20,16},{24,28},{28,24},{1,5},{5... | collective-permute-start | bytes 1327112 | tf_op jit(solution)/shard_map/ppermute | solution.py:834
  157.1 34.9 %collective-permute-start.40 = (bf16[144,1536]{1,0:T(8,128)(2,1)}, bf16[144,1536]{1,0:T(8,128)(2,1)}, u32[]{:S(2)}, u32[]{:S(2)}) collective-permute-start(bf16[144,1536]{1,0:T(8,128)(2,1)} %collective-permute-done.33.refs_10_.refs_18_), channel_id=1, source_target_pairs={{0,4},{4,0},{8,12},{12,8},{16,20},{20,16},{24,28},{28,24},{1,5},{5... | collective-permute-start | bytes 1327112 | tf_op jit(solution)/shard_map/ppermute | solution.py:834
  157.6 34.4 %collective-permute-start.41 = (bf16[144,1536]{1,0:T(8,128)(2,1)}, bf16[144,1536]{1,0:T(8,128)(2,1)}, u32[]{:S(2)}, u32[]{:S(2)}) collective-permute-start(bf16[144,1536]{1,0:T(8,128)(2,1)} %collective-permute-done.34.refs_12_.refs_20_), channel_id=1, source_target_pairs={{0,4},{4,0},{8,12},{12,8},{16,20},{20,16},{24,28},{28,24},{1,5},{5... | collective-permute-start | bytes 1327112 | tf_op jit(solution)/shard_map/ppermute | solution.py:834
  157.6 34.4 %collective-permute-start.42 = (bf16[144,1536]{1,0:T(8,128)(2,1)}, bf16[144,1536]{1,0:T(8,128)(2,1)}, u32[]{:S(2)}, u32[]{:S(2)}) collective-permute-start(bf16[144,1536]{1,0:T(8,128)(2,1)} %collective-permute-done.35.refs_14_.refs_22_), channel_id=1, source_target_pairs={{0,4},{4,0},{8,12},{12,8},{16,20},{20,16},{24,28},{28,24},{1,5},{5... | collective-permute-start | bytes 1327112 | tf_op jit(solution)/shard_map/ppermute | solution.py:834
  196.2 134.1 %reduce-scatter.8.cloned.1.call-start = ((), (), s32[]{:S(2)}) async-start(), calls=%async_computation.7 | async-start | bytes 2457600 | tf_op jit(solution)/shard_map/reduce_scatter | solution.py:890
  197.3 22.1 %collective-permute-start.44 = (bf16[72,1536]{1,0:T(8,128)(2,1)S(1)}, bf16[72,1536]{1,0:T(8,128)(2,1)S(1)}, u32[]{:S(2)}, u32[]{:S(2)}) collective-permute-start(bf16[72,1536]{1,0:T(8,128)(2,1)S(1)} %maximum_maximum_fusion.refs_0_), channel_id=1, source_target_pairs={{2,0},{3,1},{0,2},{1,3},{6,4},{7,5},{4,6},{5,7},{10,8},{11,9},{8,1... | collective-permute-start | bytes 663560 | tf_op jit(solution)/shard_map/ppermute | solution.py:816
  237.2 32.2 %collective-permute-start.67 = (bf16[192,1536]{1,0:T(8,128)(2,1)}, bf16[192,1536]{1,0:T(8,128)(2,1)S(1)}, u32[]{:S(2)}, u32[]{:S(2)}) collective-permute-start(bf16[192,1536]{1,0:T(8,128)(2,1)} %pad_maximum_fusion.4), channel_id=1, source_target_pairs={{0,16},{4,20},{8,24},{12,28},{16,0},{20,4},{24,8},{28,12},{1,17},{... | collective-permute-start | bytes 1769480 | tf_op jit(solution)/shard_map/ppermute | solution.py:834
  238.4 31.1 %collective-permute-start.66 = (bf16[192,1536]{1,0:T(8,128)(2,1)}, bf16[192,1536]{1,0:T(8,128)(2,1)}, u32[]{:S(2)}, u32[]{:S(2)}) collective-permute-start(bf16[192,1536]{1,0:T(8,128)(2,1)} %pad_maximum_fusion.3), channel_id=1, source_target_pairs={{0,8},{4,12},{8,0},{12,4},{16,24},{20,28},{24,16},{28,20},{1,9},{5... | collective-permute-start | bytes 1769480 | tf_op jit(solution)/shard_map/ppermute | solution.py:834
  246.3 28.8 %collective-permute-start.52 = (bf16[80,1536]{1,0:T(8,128)(2,1)}, bf16[80,1536]{1,0:T(8,128)(2,1)S(1)}, u32[]{:S(2)}, u32[]{:S(2)}) collective-permute-start(bf16[80,1536]{1,0:T(8,128)(2,1)} %get-tuple-element.386), channel_id=1, source_target_pairs={{3,0},{0,1},{1,2},{2,3},{7,4},{4,5},{5,6},{6,7},{11,8},{8,9},{9,10... | collective-permute-start | bytes 737288 | tf_op jit(solution)/shard_map/ppermute | solution.py:816
  247.2 28.0 %collective-permute-start.53 = (bf16[80,1536]{1,0:T(8,128)(2,1)}, bf16[80,1536]{1,0:T(8,128)(2,1)S(1)}, u32[]{:S(2)}, u32[]{:S(2)}) collective-permute-start(bf16[80,1536]{1,0:T(8,128)(2,1)} %get-tuple-element.387), channel_id=1, source_target_pairs={{2,0},{3,1},{0,2},{1,3},{6,4},{7,5},{4,6},{5,7},{10,8},{11,9},{8,1... | collective-permute-start | bytes 737288 | tf_op jit(solution)/shard_map/ppermute | solution.py:816
  248.5 26.7 %collective-permute-start.54 = (bf16[80,1536]{1,0:T(8,128)(2,1)}, bf16[80,1536]{1,0:T(8,128)(2,1)S(1)}, u32[]{:S(2)}, u32[]{:S(2)}) collective-permute-start(bf16[80,1536]{1,0:T(8,128)(2,1)} %get-tuple-element.388), channel_id=1, source_target_pairs={{1,0},{2,1},{3,2},{0,3},{5,4},{6,5},{7,6},{4,7},{9,8},{10,9},{11,1... | collective-permute-start | bytes 737288 | tf_op jit(solution)/shard_map/ppermute | solution.py:816
  299.9 20.4 %collective-permute-start.78 = (bf16[208,1024]{1,0:T(8,128)(2,1)S(1)}, bf16[208,1024]{1,0:T(8,128)(2,1)S(1)}, u32[]{:S(2)}, u32[]{:S(2)}) collective-permute-start(bf16[208,1024]{1,0:T(8,128)(2,1)S(1)} %copy-done.32), channel_id=1, source_target_pairs={{0,24},{4,28},{8,16},{12,20},{16,8},{20,12},{24,0},{28,4},{1,25},{... | collective-permute-start | bytes 1277960 | tf_op jit(solution)/shard_map/ppermute | solution.py:834
  302.0 22.4 %collective-permute-start.77 = (bf16[208,1024]{1,0:T(8,128)(2,1)S(1)}, bf16[208,1024]{1,0:T(8,128)(2,1)S(1)}, u32[]{:S(2)}, u32[]{:S(2)}) collective-permute-start(bf16[208,1024]{1,0:T(8,128)(2,1)S(1)} %copy-done.30), channel_id=1, source_target_pairs={{0,16},{4,20},{8,24},{12,28},{16,0},{20,4},{24,8},{28,12},{1,17},{... | collective-permute-start | bytes 1277960 | tf_op jit(solution)/shard_map/ppermute | solution.py:834
  302.5 23.9 %collective-permute-start.76 = (bf16[208,1024]{1,0:T(8,128)(2,1)S(1)}, bf16[208,1024]{1,0:T(8,128)(2,1)S(1)}, u32[]{:S(2)}, u32[]{:S(2)}) collective-permute-start(bf16[208,1024]{1,0:T(8,128)(2,1)S(1)} %copy-done.29), channel_id=1, source_target_pairs={{0,8},{4,12},{8,0},{12,4},{16,24},{20,28},{24,16},{28,20},{1,9},{5... | collective-permute-start | bytes 1277960 | tf_op jit(solution)/shard_map/ppermute | solution.py:834
  (126 other events, 1223.0 us)
Sparse Core Ops, SparseCore 0:
  42.9 38.9 all-gather.3
  84.4 41.4 all-gather.5
  150.7 24.5 reduce-scatter.3
  196.3 63.5 reduce-scatter.5
  269.5 38.7 reduce-scatter.7

commit v5 on v4

--- a/solution.py
+++ b/solution.py
@@ -63,7 +63,7 @@
     return jnp.dot(left_side, right_side, preferred_element_type=jnp.float32)
 
 
-def run_kernel(kernel, ins, outs, scalars=None, scratch=(), far=(), far_outs=()):
+def run_kernel(kernel, ins, outs, scalars=None, scratch=(), far=(), far_outs=(), room=52):
     whole = pl.BlockSpec(memory_space=pltpu.VMEM)
     outside = pl.BlockSpec(memory_space=pl.ANY)
     specs = [outside] * len(far) + [whole] * len(ins)
@@ -78,7 +78,7 @@
         out_specs=[whole] * len(outs) + [outside] * len(far_outs),
         out_shape=shapes,
         scratch_shapes=scratch,
-        compiler_params=pltpu.CompilerParams(vmem_limit_bytes=53 * 1024 * 1024),
+        compiler_params=pltpu.CompilerParams(vmem_limit_bytes=room * 1024 * 1024),
         name=kernel.__qualname__.split(".")[0],
     )(*args)
 
@@ -351,6 +351,92 @@
     )
 
 
+def pack_rows(rows, channel_rows, weights, biases, cotangent, encoder):
+    own, width = rows.shape
+    fine = cotangent.shape[0]
+    part, heads, basis = weights.shape
+    share = channel_rows[0].shape[1]
+    n_rows = sum(block.shape[0] for block in channel_rows)
+    first = n_rows * share
+
+    def kernel(cot_ref, enc_ref, rows_ref, *refs):
+        channel_refs, refs = refs[: len(channel_rows)], refs[len(channel_rows) :]
+        weights_ref, content_ref, position_ref, out_ref, ends_ref, sems = refs
+        copies = start_copies(
+            [
+                (cot_ref.at[:16, :], ends_ref.at[0:16, :]),
+                (cot_ref.at[fine - 16 :, :], ends_ref.at[16:32, :]),
+                (enc_ref.at[:16, :], ends_ref.at[32:48, :]),
+                (enc_ref.at[fine - 16 :, :], ends_ref.at[48:64, :]),
+            ],
+            sems,
+        )
+        out_ref[:own, :] = rows_ref[...]
+
+        def place_of(size, start):
+            column = lax.broadcasted_iota(jnp.int32, (size, width), 1) - start
+            return column, lax.broadcasted_iota(jnp.int32, (size, width), 0)
+
+        def widen(values, chosen, mine):
+            found = dot_rows(values.astype(LOW), chosen.astype(jnp.float32).astype(LOW))
+            return jnp.sum(jnp.where(mine, found, 0.0), axis=0, keepdims=True)
+
+        def in_order(values, start):
+            height, size = values.shape
+            column, index = place_of(size, start)
+            chosen = (column >= 0) & (column % size == index)
+            column, index = place_of(height, start)
+            return widen(values, chosen, (column >= 0) & (column // size == index))
+
+        channel = jnp.concatenate([ref[...].astype(jnp.float32) for ref in channel_refs], axis=0)
+        row = in_order(channel, 0)
+        values = jnp.concatenate(
+            [weights_ref[k].astype(jnp.float32) for k in range(part)], axis=0
+        )
+        column, index = place_of(basis, first)
+        chosen = (column >= 0) & (column // (heads * part) == index)
+        column, index = place_of(part * heads, first)
+        mine = (column % part == index // heads) & (column // part % heads == index % heads)
+        mine = mine & (column >= 0) & (column < part * heads * basis)
+        row = row + widen(values, chosen, mine)
+        start = first + part * heads * basis
+        for ref in (content_ref, position_ref):
+            row = row + in_order(ref[...].astype(jnp.float32), start)
+            start += part * heads
+        wait_copies(copies)
+        ends = ends_ref[...].astype(jnp.float32)
+        tail = [row, ends[:1], ends[31:32], ends[32:33], ends[63:], jnp.zeros((3, width), jnp.float32)]
+        out_ref[own:, :] = jnp.concatenate(tail, axis=0).astype(LOW)
+
+    return run_kernel(
+        kernel,
+        [rows] + list(channel_rows) + [weights] + list(biases),
+        [((own + 8, width), LOW)],
+        scratch=[pltpu.VMEM((64, width), LOW), pltpu.SemaphoreType.DMA((4,))],
+        far=[cotangent, encoder],
+        room=62,
+    )[0]
+
+
+def pick_rows(blocks, own, entries):
+    width = blocks[0].shape[1]
+
+    def kernel(*refs):
+        block_refs, (line_ref, cot_ref, enc_ref) = refs[: len(blocks)], refs[len(blocks) :]
+        tails = [ref[own:, :].astype(jnp.float32) for ref in block_refs]
+        blank = jnp.zeros((14, width), jnp.float32)
+        line_ref[...] = jnp.concatenate([tail[:1, :entries] for tail in tails], axis=0).astype(LOW)
+        cot_ref[...] = jnp.concatenate([tails[-1][2:3], tails[1][1:2], blank], axis=0).astype(LOW)
+        enc_ref[...] = jnp.concatenate([tails[-1][4:5], tails[1][3:4], blank], axis=0).astype(LOW)
+
+    return run_kernel(
+        kernel,
+        blocks,
+        [((len(blocks), entries), LOW), ((16, width), LOW), ((16, width), LOW)],
+        room=62,
+    )
+
+
 def unpack_small(where, found, basis_turned, width, local_heads, count):
     total = found.shape[0]
     n_blocks = total // count
@@ -1184,38 +1270,29 @@
     share = section_bias.shape[0]
     where = jnp.stack([lax.axis_index("dp"), lax.axis_index("tensor"), species[0]])
 
-    packed = jnp.concatenate(
-        [
-            norm_gain.reshape(-1),
-            norm_shift.reshape(-1),
-            species_table.reshape(-1),
-            depthwise_weight.reshape(-1),
-            section_bias,
-            jnp.transpose(position_weight, (1, 2, 0)).reshape(-1),
-            content_bias.T.reshape(-1),
-            position_bias.T.reshape(-1),
-        ]
-    )
-    entries = packed.shape[0]
-    packed = jnp.pad(packed[None], ((0, 0), (0, width - entries)))
-    ends = [cotangent[0, :1], cotangent[0, -1:], encoder[0, :1], encoder[0, -1:]]
-    packed = jnp.concatenate([packed] + ends + [jnp.zeros((3, width), LOW)], axis=0)
-    raw = spread_blocks(jnp.concatenate([activations[0], packed], axis=0))
+    small = [norm_gain, norm_shift, species_table, depthwise_weight, section_bias[None]]
+    entries = sum(block.size for block in small + [position_weight, content_bias, position_bias])
+    raw = spread_blocks(
+        pack_rows(
+            activations[0],
+            small,
+            jnp.swapaxes(position_weight, 1, 2),
+            [content_bias.T, position_bias.T],
+            cotangent[0],
+            encoder[0],
+        )
+    )
     attn_shard = jnp.concatenate([query_weight, key_weight, value_weight, output_weight.T], axis=1)
     attn_rows = attn_shard.shape[0]
     attn_chips = chips_of(attn_shard)
-    w_ffn = gather_dp(jnp.concatenate([expand_weight, contract_weight.T], axis=1))
     raw, attn_chips, cot, section_shard = join(
         raw, attn_chips, cotangent[0], [pointwise_weight, upsample_weight.T, lateral_weight.T]
     )
     section_shard = jnp.concatenate(section_shard, axis=0)
     w_section = lax.all_gather(section_shard, "tensor", axis=0, tiled=True)
+    line, cot_ends, enc_ends = pick_rows(raw, own, entries)
+    cot = jnp.concatenate([cot, cot_ends], axis=0)
     blank = jnp.zeros((14, width), LOW)
-    cot = [cot, raw[-1][own + 2 : own + 3], raw[1][own + 1 : own + 2], blank]
-    cot = jnp.concatenate(cot, axis=0)
-    enc = [encoder[0], raw[-1][own + 4 : own + 5], raw[1][own + 3 : own + 4], blank]
-    enc = jnp.concatenate(enc, axis=0)
-    line = jnp.concatenate([block[own : own + 1, :entries] for block in raw], axis=0)
     small_rows = gather_dp(line)
     attn_blocks = both_cores(*attn_chips)
     small_rows, attn_blocks, cot = join(small_rows, attn_blocks, cot)
@@ -1234,7 +1311,11 @@
         local_heads,
         own,
     )
-    attn_parts, cot_chips = join(attn_parts, cot_chips)
+    attn_parts, cot_chips, ffn_shard, enc = join(
+        attn_parts, cot_chips, [expand_weight, contract_weight.T], encoder[0]
+    )
+    w_ffn = gather_dp(jnp.concatenate(ffn_shard, axis=1))
+    enc = jnp.concatenate([enc, enc_ends], axis=0)
 
     attn_received = collect_blocks(attn_parts[1:])
     cot_blocks = both_cores(*cot_chips)
@@ -1259,31 +1340,30 @@
     )
 
     contract_sum = scatter_tensor(contract_part)
-    encoder_part = section_grad_encoder(where, late_mix, w_lateral, lax.axis_size("dp"))
     enc_blocks = both_cores(*enc_chips)
     ffn_parts, (grad_ffn_all, grad_hidden_pre) = feed_forward_back(grad_ffn, slope, w_ffn)
     ffn_received = collect_blocks(ffn_parts[1:])
-    ffn_halves = feed_forward_weights(
-        where, normed_two_all, grad_ffn_all, hidden_low, grad_hidden_pre, len(attn_blocks)
-    )
-    ffn_received, ffn_halves, enc_blocks, encoder_part = join(
-        ffn_received, ffn_halves, enc_blocks, encoder_part
-    )
-    encoder_grad = scatter_dp(encoder_part).astype(jnp.float32)
+    ffn_received, grad_hidden_pre, enc_blocks = join(ffn_received, grad_hidden_pre, enc_blocks)
 
     grad_resid_one, grad_attn, sums_two = second_norm_back(
         ffn_parts[0], ffn_received, unit_two, scale_two, gain_two, grad_resid_two
     )
     coarse = (resid_one + contract_sum.astype(jnp.float32)).astype(LOW)
     grad_attn = [grad_attn, coarse[:1], coarse[-1:], jnp.zeros((6, width), LOW)]
-    grad_attn, ffn_halves = join(jnp.concatenate(grad_attn, axis=0), ffn_halves)
+    grad_attn, grad_hidden_pre, late_mix = join(
+        jnp.concatenate(grad_attn, axis=0), grad_hidden_pre, late_mix
+    )
     grad_attn_blocks = spread_blocks(grad_attn)
-    ffn_pairs = core_pairs(ffn_halves)
-    grad_attn_blocks, ffn_pairs = join(grad_attn_blocks, ffn_pairs)
+    encoder_part = section_grad_encoder(where, late_mix, w_lateral, lax.axis_size("dp"))
+    ffn_halves = feed_forward_weights(
+        where, normed_two_all, grad_ffn_all, hidden_low, grad_hidden_pre, lax.axis_size("dp")
+    )
+    grad_attn_blocks, ffn_halves, encoder_part = join(grad_attn_blocks, ffn_halves, encoder_part)
+    encoder_grad = scatter_dp(encoder_part).astype(jnp.float32)
 
     coarse = [coarse, grad_attn_blocks[-1][own + 1 : own + 2], grad_attn_blocks[1][own : own + 1]]
     coarse_chips = chips_of(jnp.concatenate(coarse + [blank], axis=0))
-    ffn_corners = corner_sums(ffn_pairs, LOW)
+    ffn_pairs = core_pairs(ffn_halves)
     head_parts, (grad_attn_all, grad_heads, bias_sums, rel_grad, own_sums) = attention_backward(
         where,
         grad_attn_blocks,
@@ -1295,7 +1375,8 @@
         local_heads,
         own,
     )
-    head_parts, ffn_corners = join(head_parts, ffn_corners)
+    head_parts, coarse_chips, ffn_pairs = join(head_parts, coarse_chips, ffn_pairs)
+    ffn_corners = corner_sums(ffn_pairs, LOW)
     head_received = collect_blocks(head_parts[1:])
     ffn_out = chip_sums(ffn_pairs, ffn_corners, LOW)
     coarse_blocks = both_cores(*coarse_chips)
@@ -1341,12 +1422,11 @@
         len(attn_blocks),
     )
     attn_pairs = core_pairs(attn_halves)
-    out_corners = corner_sums(out_pairs, LOW)
-    attn_pairs, out_corners, grad_resid_in, encoder_grad = join(
-        attn_pairs, out_corners, grad_resid_in, encoder_grad
+    section_out = direct_sums(out_pairs, LOW).astype(LOW)
+    attn_pairs, section_out, grad_resid_in, encoder_grad = join(
+        attn_pairs, section_out, grad_resid_in, encoder_grad
     )
     attn_out = direct_sums(attn_pairs, LOW)
-    section_out = chip_sums(out_pairs, out_corners, LOW).astype(LOW)
 
     small_out, attn_out = attn_out[attn_rows:], attn_out[:attn_rows]
     norm_out = lax.dynamic_slice_in_dim(

time: 341 us -> 334 us (0.979)
  other arithmetic: 24 us -> 19.4 us
  waiting for transfers between devices: 113 us -> 109 us
    reshape x7 -> x0, local copies, waits for them, and re-layouts: 4.66 us -> none  [the longest x1 0.84 us: body_direct(): norm_gain.reshape(-1)]
    unnamed x133 -> x141, local copies, waits for them, and re-layouts: 4.91 us -> 8.22 us
    ppermute x58 -> x57, waiting for transfers between devices: 45.7 us -> 42.5 us  [dp_flip(): return lax.ppermute(cells, 'dp', [(i, i ^ mask) for i in range(count)])]
    pallas_call x14 -> x16, Pallas kernels: 74.3 us -> 76.6 us  [run_kernel(): pl.pallas_call(kernel, in_specs=specs, out_specs=[whole] * len(outs) + [o...]
    ppermute x58 -> x57, starting transfers between devices: 35.9 us -> 37.3 us  [dp_flip(): return lax.ppermute(cells, 'dp', [(i, i ^ mask) for i in range(count)])]
  transfers between devices with their start and end apart: 84 -> 83, of which waited for: 26 -> 20; matrix products, arithmetic and copies ran while one was open for 8% -> 7% of each run, Pallas kernels for 22% -> 22%
where the time goes in v5:
time: 334 us; the launch traced here: 333 us
  waiting for transfers between devices  109 us (33%)
  starting transfers between devices  84.7 us (25%)
  Pallas kernels  76.6 us (23%)
  other arithmetic  19.4 us (6%)
  local copies, waits for them, and re-layouts  17.9 us (5%)
  between operations  15.6 us (5%)
  blocking collectives  9.35 us (3%)
    pallas_call x16, Pallas kernels, run_kernel(): pl.pallas_call(kernel, in_specs=specs, out_specs=[whole] * len(outs) + [o...  76.6 us
    ppermute x21, waiting for transfers between devices, from_ahead(): lax.ppermute(rows, 'tensor', [((i + step) % count, i) for i in range(coun...  66.6 us
    ppermute x21, starting transfers between devices, from_ahead(): lax.ppermute(rows, 'tensor', [((i + step) % count, i) for i in range(coun...  47.2 us
    ppermute x57, waiting for transfers between devices, dp_flip(): return lax.ppermute(cells, 'dp', [(i, i ^ mask) for i in range(count)])  42.5 us
    ppermute x57, starting transfers between devices, dp_flip(): return lax.ppermute(cells, 'dp', [(i, i ^ mask) for i in range(count)])  37.3 us
    all_gather x1, blocking collectives, gather_dp(): return lax.all_gather(shard, 'dp', axis=0, tiled=True)  9.35 us
    unnamed x141, local copies, waits for them, and re-layouts  8.22 us
  transfers between devices with their start and end apart: 83, of which 20 were waited for; matrix products, arithmetic and copies ran while one was open for 7% of the time, Pallas kernels for 22%

profile of v5, /device:TPU:0, one launch (start us, length us, event | category | flops | bytes accessed | tf_op | source)
XLA Modules:
  0.0 332.8 jit_solution(6932465642869572522)
XLA Ops:
  10.1 5.1 %collective-permute-start = (bf16[72,1536]{1,0:T(8,128)(2,1)}, bf16[72,1536]{1,0:T(8,128)(2,1)S(1)}, u32[]{:S(2)}, u32[]{:S(2)}) collective-permute-start(bf16[72,1536]{1,0:T(8,128)(2,1)} %pack_rows.1.refs_0_), channel_id=1, source_target_pairs={{1,0},{2,1},{3,2},{0,3},{5,4},{6,5},{7,6},{4,7},{9,8},{10,9},{11,1... | collective-permute-start | bytes 663560 | tf_op jit(solution)/shard_map/ppermute | solution.py:902
  21.4 13.4 %collective-permute-done.1.refs_2_ = bf16[72,1536]{1,0:T(8,128)(2,1)S(1)} collective-permute-done((bf16[72,1536]{1,0:T(8,128)(2,1)}, bf16[72,1536]{1,0:T(8,128)(2,1)S(1)}, u32[]{:S(2)}, u32[]{:S(2)}) %collective-permute-start.1) | collective-permute-done | bytes 221216 | tf_op jit(solution)/shard_map/ppermute | solution.py:902
  40.3 9.4 %all-gather = bf16[8,4,1024]{2,1,0:T(4,128)(2,1)S(1)} all-gather(bf16[1,4,1024]{2,1,0:T(4,128)(2,1)} %bitcast.56), channel_id=1, replica_groups=mesh['dp'=8,'tensor'=4] {'dp'}, dimensions={0}, use_global_device_ids=true | all-gather | bytes 73728 | tf_op jit(solution)/shard_map/all_gather | solution.py:968
  56.1 7.3 %attention_forward.1 = (f32[64,1536]{1,0:T(8,128)}, bf16[64,1536]{1,0:T(8,128)(2,1)S(1)}, bf16[64,1536]{1,0:T(8,128)(2,1)S(1)}, bf16[64,1536]{1,0:T(8,128)(2,1)S...) custom-call(s32[3]{0:T(128)S(1)} %pad_add_fusion.where_ref, ...), custom_call_target="tpu_custom_call" | custom-call | tf_op jit(solution)/shard_map/attention_forward/pallas_call | solution.py:75
  66.6 6.4 %collective-permute-done.11.refs_4_ = bf16[144,1536]{1,0:T(8,128)(2,1)} collective-permute-done((bf16[144,1536]{1,0:T(8,128)(2,1)S(1)}, bf16[144,1536]{1,0:T(8,128)(2,1)}, u32[]{:S(2)}, u32[]{:S(2)}) %collective-permute-start.11) | collective-permute-done | bytes 442400 | tf_op jit(solution)/shard_map/ppermute | solution.py:920
  81.7 7.7 %section_gradient.1 = (bf16[1024,192]{1,0:T(8,128)(2,1)}, bf16[1024,192]{1,0:T(8,128)(2,1)}, bf16[512,192]{1,0:T(8,128)(2,1)S(1)}, f32[1,192]{1,0:T(1,128)S(1)},...) custom-call(s32[3]{0:T(128)S(1)} %pad_add_fusion.where_ref, ...), custom_call_target="tpu_custom_call" | custom-call | tf_op jit(solution)/shard_map/section_gradient/pallas_call | solution.py:75
  99.8 6.1 %collective-permute-start.20 = (bf16[64,1536]{1,0:T(8,128)(2,1)S(1)}, bf16[64,1536]{1,0:T(8,128)(2,1)S(1)}, u32[]{:S(2)}, u32[]{:S(2)}) collective-permute-start(bf16[64,1536]{1,0:T(8,128)(2,1)S(1)} %get-tuple-element.317.refs_0_), channel_id=1, source_target_pairs={{1,0},{2,1},{3,2},{0,3},{5,4},{6,5},{7,6},{4,7},{9,8},{10,9},{11,1... | collective-permute-start | bytes 589832 | tf_op jit(solution)/shard_map/ppermute | solution.py:902
  106.0 6.2 %collective-permute-start.22 = (bf16[64,1536]{1,0:T(8,128)(2,1)S(1)}, bf16[64,1536]{1,0:T(8,128)(2,1)S(1)}, u32[]{:S(2)}, u32[]{:S(2)}) collective-permute-start(bf16[64,1536]{1,0:T(8,128)(2,1)S(1)} %get-tuple-element.317.refs_0_), channel_id=1, source_target_pairs={{3,0},{0,1},{1,2},{2,3},{7,4},{4,5},{5,6},{6,7},{11,8},{8,9},{9,10... | collective-permute-start | bytes 589832 | tf_op jit(solution)/shard_map/ppermute | solution.py:902
  112.7 10.0 %collective-permute-done.21.refs_2_ = bf16[64,1536]{1,0:T(8,128)(2,1)S(1)} collective-permute-done((bf16[64,1536]{1,0:T(8,128)(2,1)S(1)}, bf16[64,1536]{1,0:T(8,128)(2,1)S(1)}, u32[]{:S(2)}, u32[]{:S(2)}) %collective-permute-start.21) | collective-permute-done | bytes 196640 | tf_op jit(solution)/shard_map/ppermute | solution.py:902
  128.3 4.4 %collective-permute-done.30.refs_1_ = bf16[64,1536]{1,0:T(8,128)(2,1)S(1)} collective-permute-done((bf16[64,1536]{1,0:T(8,128)(2,1)S(1)}, bf16[64,1536]{1,0:T(8,128)(2,1)S(1)}, u32[]{:S(2)}, u32[]{:S(2)}) %collective-permute-start.30) | collective-permute-done | bytes 196640 | tf_op jit(solution)/shard_map/ppermute | solution.py:902
  132.8 10.0 %collective-permute-start.32 = (bf16[64,1536]{1,0:T(8,128)(2,1)S(1)}, bf16[64,1536]{1,0:T(8,128)(2,1)S(1)}, u32[]{:S(2)}, u32[]{:S(2)}) collective-permute-start(bf16[64,1536]{1,0:T(8,128)(2,1)S(1)} %convert_element_type.229.refs_0_), channel_id=1, source_target_pairs={{3,0},{0,1},{1,2},{2,3},{7,4},{4,5},{5,6},{6,7},{11,8},{8,9},{9,10... | collective-permute-start | bytes 589832 | tf_op jit(solution)/shard_map/ppermute | solution.py:902
  142.8 5.4 %feed_forward_up.1 = (bf16[256,1536]{1,0:T(8,128)(2,1)}, bf16[256,1536]{1,0:T(8,128)(2,1)}, bf16[256,768]{1,0:T(8,128)(2,1)S(1)}, f32[256,768]{1,0:T(8,128)}) custom-call(s32[3]{0:T(128)S(1)} %pad_add_fusion.where_ref, bf16[64,1536]{1,0:T(8,128)(2,1)S(1)} %get-tuple-element.317.refs_0_, bf16[64,1536]{1,0:T(8,128)(2,1)S(1)} %collective-permute-done.20.refs_1_, ...), custom_call_target="tpu_custom_call" | custom-call | tf_op jit(solution)/shard_map/feed_forward_up/pallas_call | solution.py:75
  153.9 12.3 %collective-permute-done.36.refs_0_ = bf16[64,1536]{1,0:T(8,128)(2,1)S(1)} collective-permute-done((bf16[64,1536]{1,0:T(8,128)(2,1)S(1)}, bf16[64,1536]{1,0:T(8,128)(2,1)S(1)}, u32[]{:S(2)}, u32[]{:S(2)}) %collective-permute-start.36) | collective-permute-done | bytes 196640 | tf_op jit(solution)/shard_map/ppermute | solution.py:902
  170.1 8.9 %collective-permute-done.37.refs_1_ = bf16[64,1536]{1,0:T(8,128)(2,1)S(1)} collective-permute-done((bf16[64,1536]{1,0:T(8,128)(2,1)S(1)}, bf16[64,1536]{1,0:T(8,128)(2,1)S(1)}, u32[]{:S(2)}, u32[]{:S(2)}) %collective-permute-start.37) | collective-permute-done | bytes 196640 | tf_op jit(solution)/shard_map/ppermute | solution.py:902
  179.7 5.1 %collective-permute-done.38.refs_2_ = bf16[64,1536]{1,0:T(8,128)(2,1)S(1)} collective-permute-done((bf16[64,1536]{1,0:T(8,128)(2,1)S(1)}, bf16[64,1536]{1,0:T(8,128)(2,1)S(1)}, u32[]{:S(2)}, u32[]{:S(2)}) %collective-permute-start.38) | collective-permute-done | bytes 196640 | tf_op jit(solution)/shard_map/ppermute | solution.py:902
  195.1 4.6 %feed_forward_weights.1 = (bf16[192,1536]{1,0:T(8,128)(2,1)S(1)}, bf16[192,1536]{1,0:T(8,128)(2,1)S(1)}, bf16[192,1536]{1,0:T(8,128)(2,1)}, bf16[192,1536]{1,0:T...) custom-call(s32[3]{0:T(128)S(1)} %pad_add_fusion.where_ref, ...), custom_call_target="tpu_custom_call" | custom-call | tf_op jit(solution)/shard_map/feed_forward_weights/pallas_call | solution.py:75
  199.7 7.0 %collective-permute-done.44.refs_2_ = bf16[72,1536]{1,0:T(8,128)(2,1)} collective-permute-done((bf16[72,1536]{1,0:T(8,128)(2,1)S(1)}, bf16[72,1536]{1,0:T(8,128)(2,1)}, u32[]{:S(2)}, u32[]{:S(2)}) %collective-permute-start.44) | collective-permute-done | bytes 221216 | tf_op jit(solution)/shard_map/ppermute | solution.py:902
  212.8 8.7 %attention_backward.1 = (f32[64,1536]{1,0:T(8,128)}, bf16[80,1536]{1,0:T(8,128)(2,1)}, bf16[80,1536]{1,0:T(8,128)(2,1)}, bf16[80,1536]{1,0:T(8,128)(2,1)}, bf16[...) custom-call(s32[3]{0:T(128)S(1)} %pad_add_fusion.where_ref, ...), custom_call_target="tpu_custom_call" | custom-call | tf_op jit(solution)/shard_map/attention_backward/pallas_call | solution.py:75
  232.1 12.1 %section_forward.1 = (bf16[1024,192]{1,0:T(8,128)(2,1)}, f32[3,192]{1,0:T(4,128)S(1)}, bf16[128,1536]{1,0:T(8,128)(2,1)}, bf16[128,1536]{1,0:T(8,128)(2,1)}, bf1...) custom-call(s32[3]{0:T(128)S(1)} %pad_add_fusion.where_ref, ...), custom_call_target="tpu_custom_call" | custom-call | tf_op jit(solution)/shard_map/section_forward/pallas_call | solution.py:75
  244.3 7.7 %section_weights.1 = bf16[4,160,1536]{2,1,0:T(8,128)(2,1)} custom-call(bf16[144,1536]{1,0:T(8,128)(2,1)} %copy-done.28, bf16[144,1536]{1,0:T(8,128)(2,1)} %copy-done.33, bf16[144,1536]{1,0:T(8,128)(2,1)} %copy-done.32, bf16[144,1536]{1,0:T(8,128)(2,1)} %copy-done.34, bf16[144,1536]{1,0:T(8,128)(2,1)} %collective-permute-done.11.refs_4_, ...), custom_call_target="tpu_custom_call" | custom-call | tf_op jit(solution)/shard_map/section_weights/pallas_call | solution.py:75
  263.4 9.1 %collective-permute-done.67 = bf16[192,1536]{1,0:T(8,128)(2,1)S(1)} collective-permute-done((bf16[192,1536]{1,0:T(8,128)(2,1)S(1)}, bf16[192,1536]{1,0:T(8,128)(2,1)S(1)}, u32[]{:S(2)}, u32[]{:S(2)}) %collective-permute-start.67) | collective-permute-done | bytes 589856 | tf_op jit(solution)/shard_map/ppermute | solution.py:920
  288.3 6.5 %collective-permute-done.73 = bf16[128,1536]{1,0:T(8,128)(2,1)S(1)} collective-permute-done((bf16[128,1536]{1,0:T(8,128)(2,1)}, bf16[128,1536]{1,0:T(8,128)(2,1)S(1)}, u32[]{:S(2)}, u32[]{:S(2)}) %collective-permute-start.73) | collective-permute-done | bytes 393248 | tf_op jit(solution)/shard_map/ppermute | solution.py:920
  307.1 6.8 %collective-permute-done.77 = bf16[208,1024]{1,0:T(8,128)(2,1)S(1)} collective-permute-done((bf16[208,1024]{1,0:T(8,128)(2,1)S(1)}, bf16[208,1024]{1,0:T(8,128)(2,1)S(1)}, u32[]{:S(2)}, u32[]{:S(2)}) %collective-permute-start.77) | collective-permute-done | bytes 426016 | tf_op jit(solution)/shard_map/ppermute | solution.py:920
  313.9 8.5 %collective-permute-done.76 = bf16[208,1024]{1,0:T(8,128)(2,1)S(1)} collective-permute-done((bf16[208,1024]{1,0:T(8,128)(2,1)S(1)}, bf16[208,1024]{1,0:T(8,128)(2,1)S(1)}, u32[]{:S(2)}, u32[]{:S(2)}) %collective-permute-start.76) | collective-permute-done | bytes 426016 | tf_op jit(solution)/shard_map/ppermute | solution.py:920
  (375 shorter events, 128.5 us)
Async XLA Ops:
  7.3 74.4 %all-gather.4.cloned.1.call-start = ((), (), s32[]{:S(2)}) async-start(), calls=%async_computation.3 | async-start | bytes 2211840 | tf_op jit(solution)/shard_map/all_gather | solution.py:1292
  15.3 19.5 %collective-permute-start.3 = (bf16[192,1024]{1,0:T(8,128)(2,1)S(1)}, bf16[192,1024]{1,0:T(8,128)(2,1)}, u32[]{:S(2)}, u32[]{:S(2)}) collective-permute-start(bf16[192,1024]{1,0:T(8,128)(2,1)S(1)} %pad_maximum_fusion.6.refs_10_), channel_id=1, source_target_pairs={{0,8},{4,12},{8,0},{12,4},{16,24},{20,28},{24,16},{28,20},{1,9},{5... | collective-permute-start | bytes 1179656 | tf_op jit(solution)/shard_map/ppermute | solution.py:920
  16.8 18.8 %collective-permute-start.4 = (bf16[192,1024]{1,0:T(8,128)(2,1)S(1)}, bf16[192,1024]{1,0:T(8,128)(2,1)}, u32[]{:S(2)}, u32[]{:S(2)}) collective-permute-start(bf16[192,1024]{1,0:T(8,128)(2,1)S(1)} %pad_maximum_fusion.6.refs_10_), channel_id=1, source_target_pairs={{0,16},{4,20},{8,24},{12,28},{16,0},{20,4},{24,8},{28,12},{1,17},{... | collective-permute-start | bytes 1179656 | tf_op jit(solution)/shard_map/ppermute | solution.py:920
  36.5 106.3 %all-gather.6.cloned.1.call-start = ((), (), s32[]{:S(2)}) async-start(), calls=%async_computation.4 | async-start | bytes 5308416 | tf_op jit(solution)/shard_map/all_gather | solution.py:968
  51.3 21.7 %collective-permute-start.11 = (bf16[144,1536]{1,0:T(8,128)(2,1)S(1)}, bf16[144,1536]{1,0:T(8,128)(2,1)}, u32[]{:S(2)}, u32[]{:S(2)}) collective-permute-start(bf16[144,1536]{1,0:T(8,128)(2,1)S(1)} %pad_maximum_fusion.3.refs_0_), channel_id=1, source_target_pairs={{0,16},{4,20},{8,24},{12,28},{16,0},{20,4},{24,8},{28,12},{1,17},{... | collective-permute-start | bytes 1327112 | tf_op jit(solution)/shard_map/ppermute | solution.py:920
  52.6 20.4 %collective-permute-start.12 = (bf16[144,1536]{1,0:T(8,128)(2,1)S(1)}, bf16[144,1536]{1,0:T(8,128)(2,1)}, u32[]{:S(2)}, u32[]{:S(2)}) collective-permute-start(bf16[144,1536]{1,0:T(8,128)(2,1)S(1)} %pad_maximum_fusion.3.refs_0_), channel_id=1, source_target_pairs={{0,24},{4,28},{8,16},{12,20},{16,8},{20,12},{24,0},{28,4},{1,25},{... | collective-permute-start | bytes 1327112 | tf_op jit(solution)/shard_map/ppermute | solution.py:920
  73.9 113.6 %reduce-scatter.4.cloned.1.call-start = ((), (), s32[]{:S(2)}) async-start(), calls=%async_computation.5 | async-start | bytes 983040 | tf_op jit(solution)/shard_map/reduce_scatter | solution.py:976
  122.7 25.4 %collective-permute-start.33 = (bf16[144,1536]{1,0:T(8,128)(2,1)}, bf16[144,1536]{1,0:T(8,128)(2,1)}, u32[]{:S(2)}, u32[]{:S(2)}) collective-permute-start(bf16[144,1536]{1,0:T(8,128)(2,1)} %pad_maximum_fusion.5.refs_8_.refs_16_), channel_id=1, source_target_pairs={{0,8},{4,12},{8,0},{12,4},{16,24},{20,28},{24,16},{28,20},{1,9},{5... | collective-permute-start | bytes 1327112 | tf_op jit(solution)/shard_map/ppermute | solution.py:920
  124.0 24.1 %collective-permute-start.34 = (bf16[144,1536]{1,0:T(8,128)(2,1)}, bf16[144,1536]{1,0:T(8,128)(2,1)}, u32[]{:S(2)}, u32[]{:S(2)}) collective-permute-start(bf16[144,1536]{1,0:T(8,128)(2,1)} %pad_maximum_fusion.5.refs_8_.refs_16_), channel_id=1, source_target_pairs={{0,16},{4,20},{8,24},{12,28},{16,0},{20,4},{24,8},{28,12},{1,17},{... | collective-permute-start | bytes 1327112 | tf_op jit(solution)/shard_map/ppermute | solution.py:920
  124.7 23.4 %collective-permute-start.35 = (bf16[144,1536]{1,0:T(8,128)(2,1)}, bf16[144,1536]{1,0:T(8,128)(2,1)}, u32[]{:S(2)}, u32[]{:S(2)}) collective-permute-start(bf16[144,1536]{1,0:T(8,128)(2,1)} %pad_maximum_fusion.5.refs_8_.refs_16_), channel_id=1, source_target_pairs={{0,24},{4,28},{8,16},{12,20},{16,8},{20,12},{24,0},{28,4},{1,25},{... | collective-permute-start | bytes 1327112 | tf_op jit(solution)/shard_map/ppermute | solution.py:920
  126.3 21.8 %collective-permute-start.31 = (bf16[64,1536]{1,0:T(8,128)(2,1)S(1)}, bf16[64,1536]{1,0:T(8,128)(2,1)S(1)}, u32[]{:S(2)}, u32[]{:S(2)}) collective-permute-start(bf16[64,1536]{1,0:T(8,128)(2,1)S(1)} %convert_element_type.229.refs_0_), channel_id=1, source_target_pairs={{2,0},{3,1},{0,2},{1,3},{6,4},{7,5},{4,6},{5,7},{10,8},{11,9},{8,1... | collective-permute-start | bytes 589832 | tf_op jit(solution)/shard_map/ppermute | solution.py:902
  148.2 150.1 %reduce-scatter.6.cloned.1.call-start = ((), (), s32[]{:S(2)}) async-start(), calls=%async_computation.6 | async-start | bytes 3538944 | tf_op jit(solution)/shard_map/reduce_scatter | solution.py:972
  152.9 31.9 %collective-permute-start.39 = (bf16[144,1536]{1,0:T(8,128)(2,1)}, bf16[144,1536]{1,0:T(8,128)(2,1)S(1)}, u32[]{:S(2)}, u32[]{:S(2)}) collective-permute-start(bf16[144,1536]{1,0:T(8,128)(2,1)} %pad_maximum_fusion.5.refs_8_.refs_16_), channel_id=1, source_target_pairs={{0,4},{4,0},{8,12},{12,8},{16,20},{20,16},{24,28},{28,24},{1,5},{5... | collective-permute-start | bytes 1327112 | tf_op jit(solution)/shard_map/ppermute | solution.py:920
  152.9 31.9 %collective-permute-start.40 = (bf16[144,1536]{1,0:T(8,128)(2,1)}, bf16[144,1536]{1,0:T(8,128)(2,1)S(1)}, u32[]{:S(2)}, u32[]{:S(2)}) collective-permute-start(bf16[144,1536]{1,0:T(8,128)(2,1)} %collective-permute-done.33.refs_10_.refs_18_), channel_id=1, source_target_pairs={{0,4},{4,0},{8,12},{12,8},{16,20},{20,16},{24,28},{28,24},{1,5},{5... | collective-permute-start | bytes 1327112 | tf_op jit(solution)/shard_map/ppermute | solution.py:920
  153.4 31.4 %collective-permute-start.41 = (bf16[144,1536]{1,0:T(8,128)(2,1)}, bf16[144,1536]{1,0:T(8,128)(2,1)S(1)}, u32[]{:S(2)}, u32[]{:S(2)}) collective-permute-start(bf16[144,1536]{1,0:T(8,128)(2,1)} %collective-permute-done.34.refs_12_.refs_20_), channel_id=1, source_target_pairs={{0,4},{4,0},{8,12},{12,8},{16,20},{20,16},{24,28},{28,24},{1,5},{5... | collective-permute-start | bytes 1327112 | tf_op jit(solution)/shard_map/ppermute | solution.py:920
  153.4 31.4 %collective-permute-start.42 = (bf16[144,1536]{1,0:T(8,128)(2,1)}, bf16[144,1536]{1,0:T(8,128)(2,1)S(1)}, u32[]{:S(2)}, u32[]{:S(2)}) collective-permute-start(bf16[144,1536]{1,0:T(8,128)(2,1)} %collective-permute-done.35.refs_14_.refs_22_), channel_id=1, source_target_pairs={{0,4},{4,0},{8,12},{12,8},{16,20},{20,16},{24,28},{28,24},{1,5},{5... | collective-permute-start | bytes 1327112 | tf_op jit(solution)/shard_map/ppermute | solution.py:920
  206.8 97.0 %reduce-scatter.8.cloned.1.call-start = ((), (), s32[]{:S(2)}) async-start(), calls=%async_computation.7 | async-start | bytes 2457600 | tf_op jit(solution)/shard_map/reduce_scatter | solution.py:976
  227.3 24.8 %collective-permute-start.66 = (bf16[96,1536]{1,0:T(8,128)(2,1)}, bf16[96,1536]{1,0:T(8,128)(2,1)}, u32[]{:S(2)}, u32[]{:S(2)}) collective-permute-start(bf16[96,1536]{1,0:T(8,128)(2,1)} %get-tuple-element.468), channel_id=1, source_target_pairs={{0,8},{4,12},{8,0},{12,4},{16,24},{20,28},{24,16},{28,20},{1,9},{5... | collective-permute-start | bytes 884744 | tf_op jit(solution)/shard_map/ppermute | solution.py:920
  228.3 46.7 %collective-permute-start.53 = (bf16[80,1536]{1,0:T(8,128)(2,1)}, bf16[80,1536]{1,0:T(8,128)(2,1)S(1)}, u32[]{:S(2)}, u32[]{:S(2)}) collective-permute-start(bf16[80,1536]{1,0:T(8,128)(2,1)} %get-tuple-element.393), channel_id=1, source_target_pairs={{3,0},{0,1},{1,2},{2,3},{7,4},{4,5},{5,6},{6,7},{11,8},{8,9},{9,10... | collective-permute-start | bytes 737288 | tf_op jit(solution)/shard_map/ppermute | solution.py:902
  228.6 46.4 %collective-permute-start.54 = (bf16[80,1536]{1,0:T(8,128)(2,1)}, bf16[80,1536]{1,0:T(8,128)(2,1)S(1)}, u32[]{:S(2)}, u32[]{:S(2)}) collective-permute-start(bf16[80,1536]{1,0:T(8,128)(2,1)} %get-tuple-element.394), channel_id=1, source_target_pairs={{2,0},{3,1},{0,2},{1,3},{6,4},{7,5},{4,6},{5,7},{10,8},{11,9},{8,1... | collective-permute-start | bytes 737288 | tf_op jit(solution)/shard_map/ppermute | solution.py:902
  230.7 23.0 %collective-permute-start.64 = (bf16[96,1536]{1,0:T(8,128)(2,1)}, bf16[96,1536]{1,0:T(8,128)(2,1)}, u32[]{:S(2)}, u32[]{:S(2)}) collective-permute-start(bf16[96,1536]{1,0:T(8,128)(2,1)} %get-tuple-element.467), channel_id=1, source_target_pairs={{0,16},{4,20},{8,24},{12,28},{16,0},{20,4},{24,8},{28,12},{1,17},{... | collective-permute-start | bytes 884744 | tf_op jit(solution)/shard_map/ppermute | solution.py:920
  276.5 18.2 %collective-permute-start.73 = (bf16[128,1536]{1,0:T(8,128)(2,1)}, bf16[128,1536]{1,0:T(8,128)(2,1)S(1)}, u32[]{:S(2)}, u32[]{:S(2)}) collective-permute-start(bf16[128,1536]{1,0:T(8,128)(2,1)} %convert_add_fusion.10), channel_id=1, source_target_pairs={{0,16},{4,20},{8,24},{12,28},{16,0},{20,4},{24,8},{28,12},{1,17},{... | collective-permute-start | bytes 1179656 | tf_op jit(solution)/shard_map/ppermute | solution.py:920
  301.7 20.7 %collective-permute-start.76 = (bf16[208,1024]{1,0:T(8,128)(2,1)S(1)}, bf16[208,1024]{1,0:T(8,128)(2,1)S(1)}, u32[]{:S(2)}, u32[]{:S(2)}) collective-permute-start(bf16[208,1024]{1,0:T(8,128)(2,1)S(1)} %convert_add_fusion.6), channel_id=1, source_target_pairs={{0,16},{4,20},{8,24},{12,28},{16,0},{20,4},{24,8},{28,12},{1,17},{... | collective-permute-start | bytes 1277960 | tf_op jit(solution)/shard_map/ppermute | solution.py:920
  302.8 19.6 %collective-permute-start.75 = (bf16[208,1024]{1,0:T(8,128)(2,1)S(1)}, bf16[208,1024]{1,0:T(8,128)(2,1)S(1)}, u32[]{:S(2)}, u32[]{:S(2)}) collective-permute-start(bf16[208,1024]{1,0:T(8,128)(2,1)S(1)} %convert_add_fusion.7), channel_id=1, source_target_pairs={{0,8},{4,12},{8,0},{12,4},{16,24},{20,28},{24,16},{28,20},{1,9},{5... | collective-permute-start | bytes 1277960 | tf_op jit(solution)/shard_map/ppermute | solution.py:920
  (129 other events, 1202.3 us)
Sparse Core Ops, SparseCore 0:
  36.6 40.0 all-gather.3
  79.2 42.4 all-gather.5
  148.3 24.7 reduce-scatter.3
  206.9 51.9 reduce-scatter.5
  261.2 41.4 reduce-scatter.7

commit v6 on v5

--- a/solution.py
+++ b/solution.py
@@ -1376,9 +1376,8 @@
         own,
     )
     head_parts, coarse_chips, ffn_pairs = join(head_parts, coarse_chips, ffn_pairs)
-    ffn_corners = corner_sums(ffn_pairs, LOW)
     head_received = collect_blocks(head_parts[1:])
-    ffn_out = chip_sums(ffn_pairs, ffn_corners, LOW)
+    ffn_out = direct_sums(ffn_pairs, LOW)
     coarse_blocks = both_cores(*coarse_chips)
     deep_rows, taps_grad, *out_halves = section_forward(
         where,

time: 334 us -> 334 us (level)
    reduce_scatter x2, waiting for transfers between devices: 0.02 us -> 18.6 us  [scatter_tensor(): return lax.psum_scatter(whole, 'tensor', scatter_dimension=0, tiled=True)]
    ppermute x57 -> x56, waiting for transfers between devices: 42.5 us -> 24.5 us  [dp_flip(): return lax.ppermute(cells, 'dp', [(i, i ^ mask) for i in range(count)])]
    ppermute x57 -> x56, starting transfers between devices: 37.3 us -> 36 us  [dp_flip(): return lax.ppermute(cells, 'dp', [(i, i ^ mask) for i in range(count)])]
    unnamed x141 -> x139, local copies, waits for them, and re-layouts: 8.22 us -> 8.72 us
  transfers between devices with their start and end apart: 83 -> 82, of which waited for: 20 -> 19; matrix products, arithmetic and copies ran while one was open for 7% -> 7% of each run, Pallas kernels for 22% -> 22%
where the time goes in v6:
time: 334 us; the launch traced here: 332 us
  waiting for transfers between devices  111 us (33%)
  starting transfers between devices  82.1 us (25%)
  Pallas kernels  76.6 us (23%)
  other arithmetic  20.7 us (6%)
  local copies, waits for them, and re-layouts  17.5 us (5%)
  between operations  15.5 us (5%)
  blocking collectives  9.35 us (3%)
    pallas_call x16, Pallas kernels, run_kernel(): pl.pallas_call(kernel, in_specs=specs, out_specs=[whole] * len(outs) + [o...  76.6 us
    ppermute x21, waiting for transfers between devices, from_ahead(): lax.ppermute(rows, 'tensor', [((i + step) % count, i) for i in range(coun...  67.5 us
    ppermute x21, starting transfers between devices, from_ahead(): lax.ppermute(rows, 'tensor', [((i + step) % count, i) for i in range(coun...  45.7 us
    ppermute x56, starting transfers between devices, dp_flip(): return lax.ppermute(cells, 'dp', [(i, i ^ mask) for i in range(count)])  36 us
    ppermute x56, waiting for transfers between devices, dp_flip(): return lax.ppermute(cells, 'dp', [(i, i ^ mask) for i in range(count)])  24.5 us
    reduce_scatter x2, waiting for transfers between devices, scatter_tensor(): return lax.psum_scatter(whole, 'tensor', scatter_dimension=0, tiled=True)  18.6 us
    all_gather x1, blocking collectives, gather_dp(): return lax.all_gather(shard, 'dp', axis=0, tiled=True)  9.35 us
    unnamed x139, local copies, waits for them, and re-layouts  8.72 us
  transfers between devices with their start and end apart: 82, of which 19 were waited for; matrix products, arithmetic and copies ran while one was open for 7% of the time, Pallas kernels for 22%

profile of v6, /device:TPU:0, one launch (start us, length us, event | category | flops | bytes accessed | tf_op | source)
XLA Modules:
  0.0 332.5 jit_solution(9126599219197274770)
XLA Ops:
  10.1 5.1 %collective-permute-start = (bf16[72,1536]{1,0:T(8,128)(2,1)}, bf16[72,1536]{1,0:T(8,128)(2,1)S(1)}, u32[]{:S(2)}, u32[]{:S(2)}) collective-permute-start(bf16[72,1536]{1,0:T(8,128)(2,1)} %pack_rows.1.refs_0_), channel_id=1, source_target_pairs={{1,0},{2,1},{3,2},{0,3},{5,4},{6,5},{7,6},{4,7},{9,8},{10,9},{11,1... | collective-permute-start | bytes 663560 | tf_op jit(solution)/shard_map/ppermute | solution.py:902
  21.4 13.4 %collective-permute-done.1.refs_2_ = bf16[72,1536]{1,0:T(8,128)(2,1)S(1)} collective-permute-done((bf16[72,1536]{1,0:T(8,128)(2,1)}, bf16[72,1536]{1,0:T(8,128)(2,1)S(1)}, u32[]{:S(2)}, u32[]{:S(2)}) %collective-permute-start.1) | collective-permute-done | bytes 221216 | tf_op jit(solution)/shard_map/ppermute | solution.py:902
  40.3 9.4 %all-gather = bf16[8,4,1024]{2,1,0:T(4,128)(2,1)S(1)} all-gather(bf16[1,4,1024]{2,1,0:T(4,128)(2,1)} %bitcast.56), channel_id=1, replica_groups=mesh['dp'=8,'tensor'=4] {'dp'}, dimensions={0}, use_global_device_ids=true | all-gather | bytes 73728 | tf_op jit(solution)/shard_map/all_gather | solution.py:968
  56.1 7.3 %attention_forward.1 = (f32[64,1536]{1,0:T(8,128)}, bf16[64,1536]{1,0:T(8,128)(2,1)S(1)}, bf16[64,1536]{1,0:T(8,128)(2,1)S(1)}, bf16[64,1536]{1,0:T(8,128)(2,1)S...) custom-call(s32[3]{0:T(128)S(1)} %pad_add_fusion.where_ref, ...), custom_call_target="tpu_custom_call" | custom-call | tf_op jit(solution)/shard_map/attention_forward/pallas_call | solution.py:75
  66.6 6.4 %collective-permute-done.11.refs_4_ = bf16[144,1536]{1,0:T(8,128)(2,1)} collective-permute-done((bf16[144,1536]{1,0:T(8,128)(2,1)S(1)}, bf16[144,1536]{1,0:T(8,128)(2,1)}, u32[]{:S(2)}, u32[]{:S(2)}) %collective-permute-start.11) | collective-permute-done | bytes 442400 | tf_op jit(solution)/shard_map/ppermute | solution.py:920
  81.7 7.7 %section_gradient.1 = (bf16[1024,192]{1,0:T(8,128)(2,1)}, bf16[1024,192]{1,0:T(8,128)(2,1)}, bf16[512,192]{1,0:T(8,128)(2,1)S(1)}, f32[1,192]{1,0:T(1,128)S(1)},...) custom-call(s32[3]{0:T(128)S(1)} %pad_add_fusion.where_ref, ...), custom_call_target="tpu_custom_call" | custom-call | tf_op jit(solution)/shard_map/section_gradient/pallas_call | solution.py:75
  99.8 6.1 %collective-permute-start.20 = (bf16[64,1536]{1,0:T(8,128)(2,1)S(1)}, bf16[64,1536]{1,0:T(8,128)(2,1)S(1)}, u32[]{:S(2)}, u32[]{:S(2)}) collective-permute-start(bf16[64,1536]{1,0:T(8,128)(2,1)S(1)} %get-tuple-element.317.refs_0_), channel_id=1, source_target_pairs={{1,0},{2,1},{3,2},{0,3},{5,4},{6,5},{7,6},{4,7},{9,8},{10,9},{11,1... | collective-permute-start | bytes 589832 | tf_op jit(solution)/shard_map/ppermute | solution.py:902
  106.0 5.3 %collective-permute-start.22 = (bf16[64,1536]{1,0:T(8,128)(2,1)S(1)}, bf16[64,1536]{1,0:T(8,128)(2,1)S(1)}, u32[]{:S(2)}, u32[]{:S(2)}) collective-permute-start(bf16[64,1536]{1,0:T(8,128)(2,1)S(1)} %get-tuple-element.317.refs_0_), channel_id=1, source_target_pairs={{3,0},{0,1},{1,2},{2,3},{7,4},{4,5},{5,6},{6,7},{11,8},{8,9},{9,10... | collective-permute-start | bytes 589832 | tf_op jit(solution)/shard_map/ppermute | solution.py:902
  111.7 11.0 %collective-permute-done.21.refs_2_ = bf16[64,1536]{1,0:T(8,128)(2,1)S(1)} collective-permute-done((bf16[64,1536]{1,0:T(8,128)(2,1)S(1)}, bf16[64,1536]{1,0:T(8,128)(2,1)S(1)}, u32[]{:S(2)}, u32[]{:S(2)}) %collective-permute-start.21) | collective-permute-done | bytes 196640 | tf_op jit(solution)/shard_map/ppermute | solution.py:902
  128.3 4.4 %collective-permute-done.30.refs_1_ = bf16[64,1536]{1,0:T(8,128)(2,1)S(1)} collective-permute-done((bf16[64,1536]{1,0:T(8,128)(2,1)S(1)}, bf16[64,1536]{1,0:T(8,128)(2,1)S(1)}, u32[]{:S(2)}, u32[]{:S(2)}) %collective-permute-start.30) | collective-permute-done | bytes 196640 | tf_op jit(solution)/shard_map/ppermute | solution.py:902
  132.7 10.0 %collective-permute-start.32 = (bf16[64,1536]{1,0:T(8,128)(2,1)S(1)}, bf16[64,1536]{1,0:T(8,128)(2,1)S(1)}, u32[]{:S(2)}, u32[]{:S(2)}) collective-permute-start(bf16[64,1536]{1,0:T(8,128)(2,1)S(1)} %convert_element_type.231.refs_0_), channel_id=1, source_target_pairs={{3,0},{0,1},{1,2},{2,3},{7,4},{4,5},{5,6},{6,7},{11,8},{8,9},{9,10... | collective-permute-start | bytes 589832 | tf_op jit(solution)/shard_map/ppermute | solution.py:902
  142.7 5.4 %feed_forward_up.1 = (bf16[256,1536]{1,0:T(8,128)(2,1)}, bf16[256,1536]{1,0:T(8,128)(2,1)}, bf16[256,768]{1,0:T(8,128)(2,1)S(1)}, f32[256,768]{1,0:T(8,128)}) custom-call(s32[3]{0:T(128)S(1)} %pad_add_fusion.where_ref, bf16[64,1536]{1,0:T(8,128)(2,1)S(1)} %get-tuple-element.317.refs_0_, bf16[64,1536]{1,0:T(8,128)(2,1)S(1)} %collective-permute-done.20.refs_1_, ...), custom_call_target="tpu_custom_call" | custom-call | tf_op jit(solution)/shard_map/feed_forward_up/pallas_call | solution.py:75
  148.2 4.3 %feed_forward_back.1 = (f32[64,1536]{1,0:T(8,128)S(1)}, bf16[64,1536]{1,0:T(8,128)(2,1)S(1)}, bf16[64,1536]{1,0:T(8,128)(2,1)S(1)}, bf16[64,1536]{1,0:T(8,128)(2...) custom-call(bf16[64,1536]{1,0:T(8,128)(2,1)S(1)} %convert_element_type.231.refs_0_, ...), custom_call_target="tpu_custom_call" | custom-call | tf_op jit(solution)/shard_map/feed_forward_back/pallas_call | solution.py:75
  153.9 12.4 %collective-permute-done.36.refs_0_ = bf16[64,1536]{1,0:T(8,128)(2,1)S(1)} collective-permute-done((bf16[64,1536]{1,0:T(8,128)(2,1)S(1)}, bf16[64,1536]{1,0:T(8,128)(2,1)S(1)}, u32[]{:S(2)}, u32[]{:S(2)}) %collective-permute-start.36) | collective-permute-done | bytes 196640 | tf_op jit(solution)/shard_map/ppermute | solution.py:902
  170.1 8.9 %collective-permute-done.37.refs_1_ = bf16[64,1536]{1,0:T(8,128)(2,1)S(1)} collective-permute-done((bf16[64,1536]{1,0:T(8,128)(2,1)S(1)}, bf16[64,1536]{1,0:T(8,128)(2,1)S(1)}, u32[]{:S(2)}, u32[]{:S(2)}) %collective-permute-start.37) | collective-permute-done | bytes 196640 | tf_op jit(solution)/shard_map/ppermute | solution.py:902
  179.7 5.1 %collective-permute-done.38.refs_2_ = bf16[64,1536]{1,0:T(8,128)(2,1)S(1)} collective-permute-done((bf16[64,1536]{1,0:T(8,128)(2,1)S(1)}, bf16[64,1536]{1,0:T(8,128)(2,1)S(1)}, u32[]{:S(2)}, u32[]{:S(2)}) %collective-permute-start.38) | collective-permute-done | bytes 196640 | tf_op jit(solution)/shard_map/ppermute | solution.py:902
  195.1 4.6 %feed_forward_weights.1 = (bf16[192,1536]{1,0:T(8,128)(2,1)S(1)}, bf16[192,1536]{1,0:T(8,128)(2,1)S(1)}, bf16[192,1536]{1,0:T(8,128)(2,1)}, bf16[192,1536]{1,0:T...) custom-call(s32[3]{0:T(128)S(1)} %pad_add_fusion.where_ref, ...), custom_call_target="tpu_custom_call" | custom-call | tf_op jit(solution)/shard_map/feed_forward_weights/pallas_call | solution.py:75
  199.7 7.0 %collective-permute-done.44.refs_2_ = bf16[72,1536]{1,0:T(8,128)(2,1)} collective-permute-done((bf16[72,1536]{1,0:T(8,128)(2,1)S(1)}, bf16[72,1536]{1,0:T(8,128)(2,1)}, u32[]{:S(2)}, u32[]{:S(2)}) %collective-permute-start.44) | collective-permute-done | bytes 221216 | tf_op jit(solution)/shard_map/ppermute | solution.py:902
  212.9 8.7 %attention_backward.1 = (f32[64,1536]{1,0:T(8,128)}, bf16[80,1536]{1,0:T(8,128)(2,1)}, bf16[80,1536]{1,0:T(8,128)(2,1)}, bf16[80,1536]{1,0:T(8,128)(2,1)}, bf16[...) custom-call(s32[3]{0:T(128)S(1)} %pad_add_fusion.where_ref, ...), custom_call_target="tpu_custom_call" | custom-call | tf_op jit(solution)/shard_map/attention_backward/pallas_call | solution.py:75
  233.5 12.1 %section_forward.1 = (bf16[1024,192]{1,0:T(8,128)(2,1)}, f32[3,192]{1,0:T(4,128)S(1)}, bf16[128,1536]{1,0:T(8,128)(2,1)}, bf16[128,1536]{1,0:T(8,128)(2,1)}, bf1...) custom-call(s32[3]{0:T(128)S(1)} %pad_add_fusion.where_ref, ...), custom_call_target="tpu_custom_call" | custom-call | tf_op jit(solution)/shard_map/section_forward/pallas_call | solution.py:75
  245.7 7.7 %section_weights.1 = bf16[4,160,1536]{2,1,0:T(8,128)(2,1)} custom-call(bf16[144,1536]{1,0:T(8,128)(2,1)} %copy-done.28, bf16[144,1536]{1,0:T(8,128)(2,1)} %copy-done.31, bf16[144,1536]{1,0:T(8,128)(2,1)} %copy-done.30, bf16[144,1536]{1,0:T(8,128)(2,1)} %copy-done.32, bf16[144,1536]{1,0:T(8,128)(2,1)} %collective-permute-done.11.refs_4_, ...), custom_call_target="tpu_custom_call" | custom-call | tf_op jit(solution)/shard_map/section_weights/pallas_call | solution.py:75
  256.9 6.8 %collective-permute-done.65 = bf16[192,1536]{1,0:T(8,128)(2,1)} collective-permute-done((bf16[192,1536]{1,0:T(8,128)(2,1)}, bf16[192,1536]{1,0:T(8,128)(2,1)}, u32[]{:S(2)}, u32[]{:S(2)}) %collective-permute-start.65) | collective-permute-done | bytes 589856 | tf_op jit(solution)/shard_map/ppermute | solution.py:920
  283.2 8.1 %collective-permute-done.72 = bf16[128,1536]{1,0:T(8,128)(2,1)S(1)} collective-permute-done((bf16[128,1536]{1,0:T(8,128)(2,1)}, bf16[128,1536]{1,0:T(8,128)(2,1)S(1)}, u32[]{:S(2)}, u32[]{:S(2)}) %collective-permute-start.72) | collective-permute-done | bytes 393248 | tf_op jit(solution)/shard_map/ppermute | solution.py:920
  300.2 18.6 %reduce-scatter.8.cloned.1.call-done = bf16[1,160,1536]{2,1,0:T(8,128)(2,1)} async-done(((bf16[4,160,1536]{2,1,0:T(8,128)(2,1)}), bf16[1,160,1536]{2,1,0:T(8,128)(2,1)}) %reduce-scatter.8.cloned.1.call-update) | async-done | bytes 491536 | tf_op jit(solution)/shard_map/reduce_scatter | solution.py:976
  (364 shorter events, 121.3 us)
Async XLA Ops:
  7.3 74.4 %all-gather.4.cloned.1.call-start = ((), (), s32[]{:S(2)}) async-start(), calls=%async_computation.3 | async-start | bytes 2211840 | tf_op jit(solution)/shard_map/all_gather | solution.py:1292
  15.3 19.5 %collective-permute-start.3 = (bf16[192,1024]{1,0:T(8,128)(2,1)S(1)}, bf16[192,1024]{1,0:T(8,128)(2,1)}, u32[]{:S(2)}, u32[]{:S(2)}) collective-permute-start(bf16[192,1024]{1,0:T(8,128)(2,1)S(1)} %pad_maximum_fusion.4.refs_10_), channel_id=1, source_target_pairs={{0,8},{4,12},{8,0},{12,4},{16,24},{20,28},{24,16},{28,20},{1,9},{5... | collective-permute-start | bytes 1179656 | tf_op jit(solution)/shard_map/ppermute | solution.py:920
  36.5 106.2 %all-gather.6.cloned.1.call-start = ((), (), s32[]{:S(2)}) async-start(), calls=%async_computation.4 | async-start | bytes 5308416 | tf_op jit(solution)/shard_map/all_gather | solution.py:968
  51.3 21.7 %collective-permute-start.11 = (bf16[144,1536]{1,0:T(8,128)(2,1)S(1)}, bf16[144,1536]{1,0:T(8,128)(2,1)}, u32[]{:S(2)}, u32[]{:S(2)}) collective-permute-start(bf16[144,1536]{1,0:T(8,128)(2,1)S(1)} %pad_maximum_fusion.1.refs_0_), channel_id=1, source_target_pairs={{0,16},{4,20},{8,24},{12,28},{16,0},{20,4},{24,8},{28,12},{1,17},{... | collective-permute-start | bytes 1327112 | tf_op jit(solution)/shard_map/ppermute | solution.py:920
  52.6 20.4 %collective-permute-start.12 = (bf16[144,1536]{1,0:T(8,128)(2,1)S(1)}, bf16[144,1536]{1,0:T(8,128)(2,1)}, u32[]{:S(2)}, u32[]{:S(2)}) collective-permute-start(bf16[144,1536]{1,0:T(8,128)(2,1)S(1)} %pad_maximum_fusion.1.refs_0_), channel_id=1, source_target_pairs={{0,24},{4,28},{8,16},{12,20},{16,8},{20,12},{24,0},{28,4},{1,25},{... | collective-permute-start | bytes 1327112 | tf_op jit(solution)/shard_map/ppermute | solution.py:920
  73.9 113.6 %reduce-scatter.4.cloned.1.call-start = ((), (), s32[]{:S(2)}) async-start(), calls=%async_computation.5 | async-start | bytes 983040 | tf_op jit(solution)/shard_map/reduce_scatter | solution.py:976
  122.7 25.4 %collective-permute-start.33 = (bf16[144,1536]{1,0:T(8,128)(2,1)}, bf16[144,1536]{1,0:T(8,128)(2,1)}, u32[]{:S(2)}, u32[]{:S(2)}) collective-permute-start(bf16[144,1536]{1,0:T(8,128)(2,1)} %pad_maximum_fusion.3.refs_8_.refs_16_), channel_id=1, source_target_pairs={{0,8},{4,12},{8,0},{12,4},{16,24},{20,28},{24,16},{28,20},{1,9},{5... | collective-permute-start | bytes 1327112 | tf_op jit(solution)/shard_map/ppermute | solution.py:920
  124.0 24.2 %collective-permute-start.34 = (bf16[144,1536]{1,0:T(8,128)(2,1)}, bf16[144,1536]{1,0:T(8,128)(2,1)}, u32[]{:S(2)}, u32[]{:S(2)}) collective-permute-start(bf16[144,1536]{1,0:T(8,128)(2,1)} %pad_maximum_fusion.3.refs_8_.refs_16_), channel_id=1, source_target_pairs={{0,16},{4,20},{8,24},{12,28},{16,0},{20,4},{24,8},{28,12},{1,17},{... | collective-permute-start | bytes 1327112 | tf_op jit(solution)/shard_map/ppermute | solution.py:920
  124.7 23.4 %collective-permute-start.35 = (bf16[144,1536]{1,0:T(8,128)(2,1)}, bf16[144,1536]{1,0:T(8,128)(2,1)}, u32[]{:S(2)}, u32[]{:S(2)}) collective-permute-start(bf16[144,1536]{1,0:T(8,128)(2,1)} %pad_maximum_fusion.3.refs_8_.refs_16_), channel_id=1, source_target_pairs={{0,24},{4,28},{8,16},{12,20},{16,8},{20,12},{24,0},{28,4},{1,25},{... | collective-permute-start | bytes 1327112 | tf_op jit(solution)/shard_map/ppermute | solution.py:920
  126.3 21.9 %collective-permute-start.31 = (bf16[64,1536]{1,0:T(8,128)(2,1)S(1)}, bf16[64,1536]{1,0:T(8,128)(2,1)S(1)}, u32[]{:S(2)}, u32[]{:S(2)}) collective-permute-start(bf16[64,1536]{1,0:T(8,128)(2,1)S(1)} %convert_element_type.231.refs_0_), channel_id=1, source_target_pairs={{2,0},{3,1},{0,2},{1,3},{6,4},{7,5},{4,6},{5,7},{10,8},{11,9},{8,1... | collective-permute-start | bytes 589832 | tf_op jit(solution)/shard_map/ppermute | solution.py:902
  148.2 146.5 %reduce-scatter.6.cloned.1.call-start = ((), (), s32[]{:S(2)}) async-start(), calls=%async_computation.6 | async-start | bytes 3538944 | tf_op jit(solution)/shard_map/reduce_scatter | solution.py:972
  152.9 31.9 %collective-permute-start.39 = (bf16[144,1536]{1,0:T(8,128)(2,1)}, bf16[144,1536]{1,0:T(8,128)(2,1)S(1)}, u32[]{:S(2)}, u32[]{:S(2)}) collective-permute-start(bf16[144,1536]{1,0:T(8,128)(2,1)} %pad_maximum_fusion.3.refs_8_.refs_16_), channel_id=1, source_target_pairs={{0,4},{4,0},{8,12},{12,8},{16,20},{20,16},{24,28},{28,24},{1,5},{5... | collective-permute-start | bytes 1327112 | tf_op jit(solution)/shard_map/ppermute | solution.py:920
  152.9 31.9 %collective-permute-start.40 = (bf16[144,1536]{1,0:T(8,128)(2,1)}, bf16[144,1536]{1,0:T(8,128)(2,1)S(1)}, u32[]{:S(2)}, u32[]{:S(2)}) collective-permute-start(bf16[144,1536]{1,0:T(8,128)(2,1)} %collective-permute-done.33.refs_10_.refs_18_), channel_id=1, source_target_pairs={{0,4},{4,0},{8,12},{12,8},{16,20},{20,16},{24,28},{28,24},{1,5},{5... | collective-permute-start | bytes 1327112 | tf_op jit(solution)/shard_map/ppermute | solution.py:920
  153.4 31.4 %collective-permute-start.41 = (bf16[144,1536]{1,0:T(8,128)(2,1)}, bf16[144,1536]{1,0:T(8,128)(2,1)S(1)}, u32[]{:S(2)}, u32[]{:S(2)}) collective-permute-start(bf16[144,1536]{1,0:T(8,128)(2,1)} %collective-permute-done.34.refs_12_.refs_20_), channel_id=1, source_target_pairs={{0,4},{4,0},{8,12},{12,8},{16,20},{20,16},{24,28},{28,24},{1,5},{5... | collective-permute-start | bytes 1327112 | tf_op jit(solution)/shard_map/ppermute | solution.py:920
  153.4 31.4 %collective-permute-start.42 = (bf16[144,1536]{1,0:T(8,128)(2,1)}, bf16[144,1536]{1,0:T(8,128)(2,1)S(1)}, u32[]{:S(2)}, u32[]{:S(2)}) collective-permute-start(bf16[144,1536]{1,0:T(8,128)(2,1)} %collective-permute-done.35.refs_14_.refs_22_), channel_id=1, source_target_pairs={{0,4},{4,0},{8,12},{12,8},{16,20},{20,16},{24,28},{28,24},{1,5},{5... | collective-permute-start | bytes 1327112 | tf_op jit(solution)/shard_map/ppermute | solution.py:920
  206.8 112.0 %reduce-scatter.8.cloned.1.call-start = ((), (), s32[]{:S(2)}) async-start(), calls=%async_computation.7 | async-start | bytes 2457600 | tf_op jit(solution)/shard_map/reduce_scatter | solution.py:976
  226.2 27.2 %collective-permute-start.64 = (bf16[192,1536]{1,0:T(8,128)(2,1)S(1)}, bf16[192,1536]{1,0:T(8,128)(2,1)}, u32[]{:S(2)}, u32[]{:S(2)}) collective-permute-start(bf16[192,1536]{1,0:T(8,128)(2,1)S(1)} %convert_add_fusion.2), channel_id=1, source_target_pairs={{0,8},{4,12},{8,0},{12,4},{16,24},{20,28},{24,16},{28,20},{1,9},{5... | collective-permute-start | bytes 1769480 | tf_op jit(solution)/shard_map/ppermute | solution.py:920
  227.3 36.4 %collective-permute-start.65 = (bf16[192,1536]{1,0:T(8,128)(2,1)}, bf16[192,1536]{1,0:T(8,128)(2,1)}, u32[]{:S(2)}, u32[]{:S(2)}) collective-permute-start(bf16[192,1536]{1,0:T(8,128)(2,1)} %convert_add_fusion.1), channel_id=1, source_target_pairs={{0,16},{4,20},{8,24},{12,28},{16,0},{20,4},{24,8},{28,12},{1,17},{... | collective-permute-start | bytes 1769480 | tf_op jit(solution)/shard_map/ppermute | solution.py:920
  228.7 35.0 %collective-permute-start.66 = (bf16[192,1536]{1,0:T(8,128)(2,1)}, bf16[192,1536]{1,0:T(8,128)(2,1)}, u32[]{:S(2)}, u32[]{:S(2)}) collective-permute-start(bf16[192,1536]{1,0:T(8,128)(2,1)} %convert_add_fusion), channel_id=1, source_target_pairs={{0,24},{4,28},{8,16},{12,20},{16,8},{20,12},{24,0},{28,4},{1,25},{... | collective-permute-start | bytes 1769480 | tf_op jit(solution)/shard_map/ppermute | solution.py:920
  231.2 39.7 %collective-permute-start.53 = (bf16[80,1536]{1,0:T(8,128)(2,1)}, bf16[80,1536]{1,0:T(8,128)(2,1)S(1)}, u32[]{:S(2)}, u32[]{:S(2)}) collective-permute-start(bf16[80,1536]{1,0:T(8,128)(2,1)} %get-tuple-element.393), channel_id=1, source_target_pairs={{3,0},{0,1},{1,2},{2,3},{7,4},{4,5},{5,6},{6,7},{11,8},{8,9},{9,10... | collective-permute-start | bytes 737288 | tf_op jit(solution)/shard_map/ppermute | solution.py:902
  231.6 39.4 %collective-permute-start.54 = (bf16[80,1536]{1,0:T(8,128)(2,1)}, bf16[80,1536]{1,0:T(8,128)(2,1)S(1)}, u32[]{:S(2)}, u32[]{:S(2)}) collective-permute-start(bf16[80,1536]{1,0:T(8,128)(2,1)} %get-tuple-element.394), channel_id=1, source_target_pairs={{2,0},{3,1},{0,2},{1,3},{6,4},{7,5},{4,6},{5,7},{10,8},{11,9},{8,1... | collective-permute-start | bytes 737288 | tf_op jit(solution)/shard_map/ppermute | solution.py:902
  296.7 25.4 %collective-permute-start.74 = (bf16[208,1024]{1,0:T(8,128)(2,1)S(1)}, bf16[208,1024]{1,0:T(8,128)(2,1)S(1)}, u32[]{:S(2)}, u32[]{:S(2)}) collective-permute-start(bf16[208,1024]{1,0:T(8,128)(2,1)S(1)} %convert_add_fusion.6), channel_id=1, source_target_pairs={{0,8},{4,12},{8,0},{12,4},{16,24},{20,28},{24,16},{28,20},{1,9},{5... | collective-permute-start | bytes 1277960 | tf_op jit(solution)/shard_map/ppermute | solution.py:920
  298.3 23.7 %collective-permute-start.75 = (bf16[208,1024]{1,0:T(8,128)(2,1)S(1)}, bf16[208,1024]{1,0:T(8,128)(2,1)S(1)}, u32[]{:S(2)}, u32[]{:S(2)}) collective-permute-start(bf16[208,1024]{1,0:T(8,128)(2,1)S(1)} %convert_add_fusion.5), channel_id=1, source_target_pairs={{0,16},{4,20},{8,24},{12,28},{16,0},{20,4},{24,8},{28,12},{1,17},{... | collective-permute-start | bytes 1277960 | tf_op jit(solution)/shard_map/ppermute | solution.py:920
  298.8 23.3 %collective-permute-start.76 = (bf16[208,1024]{1,0:T(8,128)(2,1)S(1)}, bf16[208,1024]{1,0:T(8,128)(2,1)S(1)}, u32[]{:S(2)}, u32[]{:S(2)}) collective-permute-start(bf16[208,1024]{1,0:T(8,128)(2,1)S(1)} %convert_add_fusion.4), channel_id=1, source_target_pairs={{0,24},{4,28},{8,16},{12,20},{16,8},{20,12},{24,0},{28,4},{1,25},{... | collective-permute-start | bytes 1277960 | tf_op jit(solution)/shard_map/ppermute | solution.py:920
  (127 other events, 1158.5 us)
Sparse Core Ops, SparseCore 0:
  36.6 40.0 all-gather.3
  79.2 42.7 all-gather.5
  148.3 24.7 reduce-scatter.3
  206.9 65.9 reduce-scatter.5
  275.2 43.5 reduce-scatter.7
